TPU v7x, 32 devices: a whole 2x2x4 slice. The times are simulated.
32 devices in a mesh: seq: 4 (over y, x), chan: 8 (over z, core).
Axes of the slice: x: 2, y: 2, z: 4, core: 2. Of those that a mesh axis runs over, the one named last changes fastest.
Arguments:
- inputs: bfloat16 [4096, 1024], P('chan', 'seq'), may hold values from -0.1875 to 0.1875
- grad_out: bfloat16 [4096, 1024], P('chan', 'seq'), may hold values from -6 to 6
- filt: bfloat16 [4096, 1024], P('chan', 'seq'), may hold values from -0.1875 to 0.1875
- rates: float32 [4096], P('chan'), may hold values from 0.5 to 50
- mix_weight: bfloat16 [4096, 64], P('chan'), may hold values from -0.09375 to 0.09375
Outputs:
- grad_in: bfloat16 [4096, 1024], P('chan', 'seq')
- grad_filt: float32 [4096, 1024], P('chan', 'seq')
- grad_hidden: float32 [64, 1024], P(None, 'seq')
All inputs are finite; a program needn't handle non-finite values.
Results may differ from a plain program's by a relative error of at most 0.0085.
Values may be sent and summed in bfloat16 or wider, within the bound.
No kernel may reach another device: no remote copies, remote signals or barrier semaphores. Data moves between devices by JAX's collectives and lax.ppermute only.
A program may use at most 64 MiB of HBM per device.

v0:
```python
import jax
import jax.numpy as jnp
from jax import lax
from jax.sharding import PartitionSpec as P

TWO_PI = 6.283185307179586


def plain_dot(left, right):
    return jnp.dot(left, right, preferred_element_type=jnp.float32)


def transform(left, right):
    return jnp.dot(left, right, precision=lax.Precision.HIGH, preferred_element_type=jnp.float32)


def trig_table(row_index, col_index, period):
    phase = jnp.mod(row_index[:, None] * col_index[None, :], period).astype(jnp.float32) * (
        TWO_PI / period
    )
    return (jnp.cos(phase), jnp.sin(phase))


def split_pair(table):
    high_part = table.astype(jnp.bfloat16)
    low_part = (table - high_part.astype(jnp.float32)).astype(jnp.bfloat16)
    return (high_part, low_part)


def spectrum_half(values, high_part, low_part, rows):
    width = values.shape[1]
    joined = plain_dot(values, high_part[:width]) + plain_dot(values, low_part[:width])
    return (joined[:, :rows], joined[:, rows:])


def project_hidden(weight, values):
    high_part = values.astype(jnp.bfloat16)
    rest = values - high_part.astype(jnp.float32)
    middle = rest.astype(jnp.bfloat16)
    lowest = (rest - middle.astype(jnp.float32)).astype(jnp.bfloat16)
    return plain_dot(weight, high_part) + plain_dot(weight, middle) + plain_dot(weight, lowest)


def body(inputs, grad_out, filt, rates, mix_weight):
    channels, block_len = inputs.shape
    cycle_size = lax.axis_size("seq")
    seq_total = cycle_size * block_len
    period = 2 * block_len
    offset = lax.axis_index("seq") * block_len
    freqs = jnp.arange(period, dtype=jnp.int32)
    fwd_cos, fwd_sin = trig_table(freqs, freqs, period)
    table_high, table_low = split_pair(jnp.concatenate([fwd_cos, -fwd_sin], axis=1))
    back_cos, back_sin = trig_table(
        freqs, block_len - jnp.arange(block_len, dtype=jnp.int32), period
    )
    filt_all = lax.all_gather(filt, "seq", axis=1, tiled=True)
    filt_pad = jnp.concatenate(
        [
            jnp.zeros((channels, period), jnp.bfloat16),
            filt_all,
            jnp.zeros((channels, block_len), jnp.bfloat16),
        ],
        axis=1,
    )
    zero_spec = jnp.zeros((channels, period), jnp.float32)
    lag_cos, lag_sin = trig_table(freqs, jnp.mod(freqs - block_len, period), period)
    own_re, own_im = spectrum_half(inputs, table_high, table_low, period)
    initial = (zero_spec, zero_spec, jnp.zeros((channels, seq_total + 3 * block_len), jnp.float32))
    arrived = lax.all_gather(grad_out, "seq", axis=1, tiled=True)
    length = arrived.shape[1]
    sub_len = min(length, block_len)
    count = length // sub_len
    stacked = arrived.reshape(channels, count, sub_len).transpose(1, 0, 2)

    def step(sub_index, state):
        values = lax.dynamic_index_in_dim(stacked, sub_index, 0, keepdims=False)
        lead = sub_index * sub_len - offset
        live_flag = (lead > -block_len).astype(jnp.float32)
        spec_re, spec_im = spectrum_half(values, table_high, table_low, period)
        window = lax.dynamic_slice_in_dim(filt_pad, lead + block_len, period, 1)
        filt_re, filt_im = spectrum_half(window, table_high, table_low, period)
        acc_re = state[0] + live_flag * (spec_re * filt_re + spec_im * filt_im)
        acc_im = state[1] + live_flag * (spec_re * filt_im - spec_im * filt_re)
        prod_re = own_re * spec_re + own_im * spec_im
        prod_im = own_re * spec_im - own_im * spec_re
        lagged = (transform(prod_re, lag_cos) - transform(prod_im, lag_sin)) / period
        current = lax.dynamic_slice_in_dim(state[2], lead + block_len, period, 1)
        updated = lax.dynamic_update_slice_in_dim(
            state[2], current + live_flag * lagged, lead + block_len, 1
        )
        return (acc_re, acc_im, updated)

    final = lax.fori_loop(0, count, step, initial)
    grad_in = ((transform(final[0], back_cos) - transform(final[1], back_sin)) / period).astype(
        jnp.bfloat16
    )
    grad_filt = lax.psum_scatter(
        final[2][:, period : period + seq_total], "seq", scatter_dimension=1, tiled=True
    )
    lags = (offset + jnp.arange(block_len, dtype=jnp.int32)).astype(jnp.float32)
    decay = jnp.exp(-rates[:, None] * lags[None, :] / seq_total)
    partial_hidden = project_hidden(mix_weight.T, grad_filt * decay)
    grad_hidden = lax.psum(partial_hidden, "chan")
    return (grad_in, grad_filt, grad_hidden)


def solution(mesh):
    return jax.shard_map(
        body,
        mesh=mesh,
        in_specs=(P("chan", "seq"), P("chan", "seq"), P("chan", "seq"), P("chan"), P("chan", None)),
        out_specs=(P("chan", "seq"), P("chan", "seq"), P(None, "seq")),
        check_vma=False,
    )
```

profile of v0, /device:TPU:0, one launch (start us, length us, event | category | flops | bytes accessed | tf_op | source)
XLA Modules:
  0.0 276.9 jit_solution(11144478301624440529)
XLA Ops:
  8.0 1.8 copy.10
  9.8 4.1 %sine_negate_fusion = (f32[512,512]{1,0:T(8,128)S(1)}, f32[512,512]{1,0:T(8,128)S(1)}) fusion(), kind=kLoop, calls=%fused_computation.71 | loop fusion | flops 3932160 | bytes 2097152 | tf_op jit(solution)/shard_map/neg | solution.py:52
  14.0 1.1 fusion.50
  15.4 1.5 fusion.64
  17.6 1.3 copy.12
  19.0 1.3 copy.13
  20.3 18.8 %all-gather.5.cloned.1.call-done = bf16[512,1024]{1,0:T(8,128)(2,1)} async-done(((bf16[512,256]{1,0:T(8,128)(2,1)}), bf16[512,1024]{1,0:T(8,128)(2,1)}) %all-gather.5.cloned.1.call-update) | async-done | bytes 1048592 | tf_op jit(solution)/shard_map/all_gather | solution.py:56
  39.1 2.7 maximum_maximum_fusion
  41.8 26.3 %all-gather.3.cloned.1.call-done = bf16[512,1024]{0,1:T(8,128)(2,1)} async-done(((bf16[512,256]{0,1:T(8,128)(2,1)}), bf16[512,1024]{0,1:T(8,128)(2,1)}) %all-gather.3.cloned.1.call-update) | async-done | bytes 1048592 | tf_op jit(solution)/shard_map/all_gather | solution.py:69
  68.1 2.0 broadcast_in_dim.9
  70.2 101.6 %while.22 = (s32[]{:T(128)}, f32[512,512]{1,0:T(8,128)}, f32[512,512]{1,0:T(8,128)}, f32[512,1792]{1,0:T(8,128)}, s32[]{:T(128)}, /*index=5*/bf16[4,512,256]{1,2...) while((s32[]{:T(128)}, f32[512,512]{1,0:T(8,128)}, ...), condition=%wide.region_1.2_spmd.clone.clone.clone, body=%wide.region_0.1_spmd.clone.clone.clone.sunk | while | flops 3235119104 | bytes 67637696 | solution.py:93
  70.2 2.1 fusion.133
  72.3 1.9 convolution_add_fusion.6
  74.2 1.5 fusion.134
  75.7 1.8 convolution_add_fusion.7
  77.5 3.9 %select_add_fusion.3 = (f32[512,512]{1,0:T(8,128)}, f32[512,512]{1,0:T(8,128)}) fusion(f32[512,512]{1,0:T(8,128)} %get-tuple-element.575, f32[512,1024]{1,0:T(8,128)S(1)} %convolution_add_fusion.6, f32[512,1024]{1,0:T(8,128)} %convolution_add_fusion.7, f32[]{:T(128)S(6)} %convert_element_type.151, pred[]{:T(512)S(6)} %compare.12, ...), kind=kLoop, calls=%fused_computation.14.clone.1 | loop fusion | flops 3145728 | bytes 8388613 | tf_op jit(solution)/shard_map/while/body/eval_jaxpr/add | solution.py:83
  81.5 5.8 %fusion.135 = f32[512,512]{1,0:T(8,128)} fusion(f32[512,512]{1,0:T(8,128)S(1)} %copy-done.7, f32[512,512]{1,0:T(8,128)S(1)} %copy-done.6, f32[512,1024]{1,0:T(8,128)S(1)} %copy-done.1, s32[512]{0:T(512)S(1)} %get-tuple-element.603), kind=kOutput, calls=%fused_computation.17.clone.1 | convolution fusion | flops 809762816 | bytes 5244928 | tf_op jit(solution)/shard_map/while/body/eval_jaxpr/dot_general | solution.py:14
  87.2 7.9 %fusion.136 = f32[512,1792]{1,0:T(8,128)} fusion(f32[512,1792]{1,0:T(8,128)} %get-tuple-element.576, s32[]{:T(128)S(6)} %select_n.112, f32[512,512]{1,0:T(8,128)} %fusion.135, f32[512,512]{1,0:T(8,128)} %get-tuple-element.602, f32[512,512]{1,0:T(8,128)} %get-tuple-element.601, f32[512,1024]{1,0:T(8,128)S(1)} %copy-done.2, ...), kind=kOutput, calls=%fused_computation.10.clone.1 | convolution fusion | flops 810549248 | bytes 7342088 | tf_op jit(solution)/shard_map/while/body/eval_jaxpr/dot_general | solution.py:14
  95.1 2.1 fusion.133
  97.2 1.9 convolution_add_fusion.6
  99.1 1.5 fusion.134
  100.6 1.8 convolution_add_fusion.7
  102.5 4.5 %select_add_fusion.3 = (f32[512,512]{1,0:T(8,128)}, f32[512,512]{1,0:T(8,128)}) fusion(f32[512,512]{1,0:T(8,128)} %get-tuple-element.575, f32[512,1024]{1,0:T(8,128)S(1)} %convolution_add_fusion.6, f32[512,1024]{1,0:T(8,128)} %convolution_add_fusion.7, f32[]{:T(128)S(6)} %convert_element_type.151, pred[]{:T(512)S(6)} %compare.12, ...), kind=kLoop, calls=%fused_computation.14.clone.1 | loop fusion | flops 3145728 | bytes 8388613 | tf_op jit(solution)/shard_map/while/body/eval_jaxpr/add | solution.py:83
  107.0 5.8 %fusion.135 = f32[512,512]{1,0:T(8,128)} fusion(f32[512,512]{1,0:T(8,128)S(1)} %copy-done.7, f32[512,512]{1,0:T(8,128)S(1)} %copy-done.6, f32[512,1024]{1,0:T(8,128)S(1)} %copy-done.1, s32[512]{0:T(512)S(1)} %get-tuple-element.603), kind=kOutput, calls=%fused_computation.17.clone.1 | convolution fusion | flops 809762816 | bytes 5244928 | tf_op jit(solution)/shard_map/while/body/eval_jaxpr/dot_general | solution.py:14
  112.8 7.8 %fusion.136 = f32[512,1792]{1,0:T(8,128)} fusion(f32[512,1792]{1,0:T(8,128)} %get-tuple-element.576, s32[]{:T(128)S(6)} %select_n.112, f32[512,512]{1,0:T(8,128)} %fusion.135, f32[512,512]{1,0:T(8,128)} %get-tuple-element.602, f32[512,512]{1,0:T(8,128)} %get-tuple-element.601, f32[512,1024]{1,0:T(8,128)S(1)} %copy-done.2, ...), kind=kOutput, calls=%fused_computation.10.clone.1 | convolution fusion | flops 810549248 | bytes 7342088 | tf_op jit(solution)/shard_map/while/body/eval_jaxpr/dot_general | solution.py:14
  120.6 2.1 fusion.133
  122.8 1.9 convolution_add_fusion.6
  124.7 1.5 fusion.134
  126.2 1.8 convolution_add_fusion.7
  128.0 4.5 %select_add_fusion.3 = (f32[512,512]{1,0:T(8,128)}, f32[512,512]{1,0:T(8,128)}) fusion(f32[512,512]{1,0:T(8,128)} %get-tuple-element.575, f32[512,1024]{1,0:T(8,128)S(1)} %convolution_add_fusion.6, f32[512,1024]{1,0:T(8,128)} %convolution_add_fusion.7, f32[]{:T(128)S(6)} %convert_element_type.151, pred[]{:T(512)S(6)} %compare.12, ...), kind=kLoop, calls=%fused_computation.14.clone.1 | loop fusion | flops 3145728 | bytes 8388613 | tf_op jit(solution)/shard_map/while/body/eval_jaxpr/add | solution.py:83
  132.6 5.8 %fusion.135 = f32[512,512]{1,0:T(8,128)} fusion(f32[512,512]{1,0:T(8,128)S(1)} %copy-done.7, f32[512,512]{1,0:T(8,128)S(1)} %copy-done.6, f32[512,1024]{1,0:T(8,128)S(1)} %copy-done.1, s32[512]{0:T(512)S(1)} %get-tuple-element.603), kind=kOutput, calls=%fused_computation.17.clone.1 | convolution fusion | flops 809762816 | bytes 5244928 | tf_op jit(solution)/shard_map/while/body/eval_jaxpr/dot_general | solution.py:14
  138.3 7.9 %fusion.136 = f32[512,1792]{1,0:T(8,128)} fusion(f32[512,1792]{1,0:T(8,128)} %get-tuple-element.576, s32[]{:T(128)S(6)} %select_n.112, f32[512,512]{1,0:T(8,128)} %fusion.135, f32[512,512]{1,0:T(8,128)} %get-tuple-element.602, f32[512,512]{1,0:T(8,128)} %get-tuple-element.601, f32[512,1024]{1,0:T(8,128)S(1)} %copy-done.2, ...), kind=kOutput, calls=%fused_computation.10.clone.1 | convolution fusion | flops 810549248 | bytes 7342088 | tf_op jit(solution)/shard_map/while/body/eval_jaxpr/dot_general | solution.py:14
  146.2 2.1 fusion.133
  148.3 1.9 convolution_add_fusion.6
  150.2 1.5 fusion.134
  151.7 1.8 convolution_add_fusion.7
  153.6 4.5 %select_add_fusion.3 = (f32[512,512]{1,0:T(8,128)}, f32[512,512]{1,0:T(8,128)}) fusion(f32[512,512]{1,0:T(8,128)} %get-tuple-element.575, f32[512,1024]{1,0:T(8,128)S(1)} %convolution_add_fusion.6, f32[512,1024]{1,0:T(8,128)} %convolution_add_fusion.7, f32[]{:T(128)S(6)} %convert_element_type.151, pred[]{:T(512)S(6)} %compare.12, ...), kind=kLoop, calls=%fused_computation.14.clone.1 | loop fusion | flops 3145728 | bytes 8388613 | tf_op jit(solution)/shard_map/while/body/eval_jaxpr/add | solution.py:83
  158.1 5.8 %fusion.135 = f32[512,512]{1,0:T(8,128)} fusion(f32[512,512]{1,0:T(8,128)S(1)} %copy-done.7, f32[512,512]{1,0:T(8,128)S(1)} %copy-done.6, f32[512,1024]{1,0:T(8,128)S(1)} %copy-done.1, s32[512]{0:T(512)S(1)} %get-tuple-element.603), kind=kOutput, calls=%fused_computation.17.clone.1 | convolution fusion | flops 809762816 | bytes 5244928 | tf_op jit(solution)/shard_map/while/body/eval_jaxpr/dot_general | solution.py:14
  163.9 7.9 %fusion.136 = f32[512,1792]{1,0:T(8,128)} fusion(f32[512,1792]{1,0:T(8,128)} %get-tuple-element.576, s32[]{:T(128)S(6)} %select_n.112, f32[512,512]{1,0:T(8,128)} %fusion.135, f32[512,512]{1,0:T(8,128)} %get-tuple-element.602, f32[512,512]{1,0:T(8,128)} %get-tuple-element.601, f32[512,1024]{1,0:T(8,128)S(1)} %copy-done.2, ...), kind=kOutput, calls=%fused_computation.10.clone.1 | convolution fusion | flops 810549248 | bytes 7342088 | tf_op jit(solution)/shard_map/while/body/eval_jaxpr/dot_general | solution.py:14
  171.8 3.2 %slice.79 = f32[512,1024]{1,0:T(8,128)} slice(f32[512,1792]{1,0:T(8,128)} %get-tuple-element.315), slice={[0:512], [512:1536]} | slice | bytes 4194304 | tf_op jit(solution)/shard_map/slice | solution.py:98
  176.2 2.5 fusion.67
  178.7 31.7 %reduce-scatter.2.cloned.1.call-done = f32[512,256]{1,0:T(8,128)} async-done(((f32[512,1024]{1,0:T(8,128)}), f32[512,256]{1,0:T(8,128)}) %reduce-scatter.2.cloned.1.call-update) | async-done | bytes 524304 | tf_op jit(solution)/shard_map/reduce_scatter | solution.py:97
  210.4 1.3 fusion.74
  211.7 1.4 convolution_add_fusion.3
  213.1 2.0 fusion.53
  215.1 3.8 %fusion.52 = bf16[512,256]{1,0:T(8,128)(2,1)} fusion(f32[512,256]{1,0:T(8,128)S(1)} %fusion.67, f32[512,512]{1,0:T(8,128)S(1)} %copy-done.4, s32[256]{0:T(256)S(1)} %iota_subtract_fusion), kind=kOutput, calls=%fused_computation.64 | convolution fusion | flops 404881408 | bytes 1836032 | tf_op jit(solution)/shard_map/dot_general | solution.py:14
  218.9 50.0 %all-reduce.2.cloned.1.call-done = f32[64,256]{1,0:T(8,128)} async-done(((f32[64,256]{1,0:T(8,128)}), f32[64,256]{1,0:T(8,128)}) %all-reduce.2.cloned.1.call-update) | async-done | bytes 65552 | tf_op jit(solution)/shard_map/psum | solution.py:103
  268.9 1.5 copy.29
  (71 shorter events, 3.1 us)
Async XLA Ops:
  7.2 8.3 %copy-start = (bf16[512,256]{1,0:T(8,128)(2,1)S(1)}, bf16[512,256]{1,0:T(8,128)(2,1)}, u32[]{:S(2)}) copy-start(bf16[512,256]{1,0:T(8,128)(2,1)} %param.7) | copy-start | bytes 786436
  7.2 31.9 %all-gather.5.cloned.1.call-start = ((), (), s32[]{:S(2)}) async-start(), calls=%async_computation.2 | async-start | bytes 1310720 | tf_op jit(solution)/shard_map/all_gather | solution.py:56
  7.9 60.2 %all-gather.3.cloned.1.call-start = ((), (), s32[]{:S(2)}) async-start(), calls=%async_computation.1 | async-start | bytes 1310720 | tf_op jit(solution)/shard_map/all_gather | solution.py:69
  9.8 200.6 %reduce-scatter.2.cloned.1.call-start = ((), (), s32[]{:S(2)}) async-start(), calls=%async_computation.3 | async-start | bytes 2621440 | tf_op jit(solution)/shard_map/reduce_scatter | solution.py:97
  72.3 1.9 copy-start.5
  77.5 3.9 %copy-start.1 = (f32[512,1024]{1,0:T(8,128)S(1)}, f32[512,1024]{1,0:T(8,128)}, u32[]{:S(2)}) copy-start(f32[512,1024]{1,0:T(8,128)} %convolution_add_fusion.7) | copy-start | bytes 6291460 | tf_op jit(solution)/shard_map/while
  77.5 3.9 %copy-start.6 = (f32[512,512]{1,0:T(8,128)S(1)}, f32[512,512]{1,0:T(8,128)}, u32[]{:S(2)}) copy-start(f32[512,512]{1,0:T(8,128)} %get-tuple-element.601) | copy-start | bytes 3145732 | tf_op jit(solution)/shard_map/while
  77.5 3.9 %copy-start.7 = (f32[512,512]{1,0:T(8,128)S(1)}, f32[512,512]{1,0:T(8,128)}, u32[]{:S(2)}) copy-start(f32[512,512]{1,0:T(8,128)} %get-tuple-element.602) | copy-start | bytes 3145732 | tf_op jit(solution)/shard_map/while
  81.5 5.8 %copy-start.2 = (f32[512,1024]{1,0:T(8,128)S(1)}, f32[512,1024]{1,0:T(8,128)}, u32[]{:S(2)}) copy-start(f32[512,1024]{1,0:T(8,128)} %convolution_add_fusion.7) | copy-start | bytes 6291460 | tf_op jit(solution)/shard_map/while
  97.2 1.9 copy-start.5
  102.5 4.5 %copy-start.1 = (f32[512,1024]{1,0:T(8,128)S(1)}, f32[512,1024]{1,0:T(8,128)}, u32[]{:S(2)}) copy-start(f32[512,1024]{1,0:T(8,128)} %convolution_add_fusion.7) | copy-start | bytes 6291460 | tf_op jit(solution)/shard_map/while
  102.5 4.5 %copy-start.6 = (f32[512,512]{1,0:T(8,128)S(1)}, f32[512,512]{1,0:T(8,128)}, u32[]{:S(2)}) copy-start(f32[512,512]{1,0:T(8,128)} %get-tuple-element.601) | copy-start | bytes 3145732 | tf_op jit(solution)/shard_map/while
  102.5 4.5 %copy-start.7 = (f32[512,512]{1,0:T(8,128)S(1)}, f32[512,512]{1,0:T(8,128)}, u32[]{:S(2)}) copy-start(f32[512,512]{1,0:T(8,128)} %get-tuple-element.602) | copy-start | bytes 3145732 | tf_op jit(solution)/shard_map/while
  107.0 5.8 %copy-start.2 = (f32[512,1024]{1,0:T(8,128)S(1)}, f32[512,1024]{1,0:T(8,128)}, u32[]{:S(2)}) copy-start(f32[512,1024]{1,0:T(8,128)} %convolution_add_fusion.7) | copy-start | bytes 6291460 | tf_op jit(solution)/shard_map/while
  122.7 1.9 copy-start.5
  128.0 4.5 %copy-start.1 = (f32[512,1024]{1,0:T(8,128)S(1)}, f32[512,1024]{1,0:T(8,128)}, u32[]{:S(2)}) copy-start(f32[512,1024]{1,0:T(8,128)} %convolution_add_fusion.7) | copy-start | bytes 6291460 | tf_op jit(solution)/shard_map/while
  128.0 4.5 %copy-start.6 = (f32[512,512]{1,0:T(8,128)S(1)}, f32[512,512]{1,0:T(8,128)}, u32[]{:S(2)}) copy-start(f32[512,512]{1,0:T(8,128)} %get-tuple-element.601) | copy-start | bytes 3145732 | tf_op jit(solution)/shard_map/while
  128.0 4.5 %copy-start.7 = (f32[512,512]{1,0:T(8,128)S(1)}, f32[512,512]{1,0:T(8,128)}, u32[]{:S(2)}) copy-start(f32[512,512]{1,0:T(8,128)} %get-tuple-element.602) | copy-start | bytes 3145732 | tf_op jit(solution)/shard_map/while
  132.6 5.8 %copy-start.2 = (f32[512,1024]{1,0:T(8,128)S(1)}, f32[512,1024]{1,0:T(8,128)}, u32[]{:S(2)}) copy-start(f32[512,1024]{1,0:T(8,128)} %convolution_add_fusion.7) | copy-start | bytes 6291460 | tf_op jit(solution)/shard_map/while
  148.3 1.9 copy-start.5
  153.6 4.5 %copy-start.1 = (f32[512,1024]{1,0:T(8,128)S(1)}, f32[512,1024]{1,0:T(8,128)}, u32[]{:S(2)}) copy-start(f32[512,1024]{1,0:T(8,128)} %convolution_add_fusion.7) | copy-start | bytes 6291460 | tf_op jit(solution)/shard_map/while
  153.6 4.5 %copy-start.6 = (f32[512,512]{1,0:T(8,128)S(1)}, f32[512,512]{1,0:T(8,128)}, u32[]{:S(2)}) copy-start(f32[512,512]{1,0:T(8,128)} %get-tuple-element.601) | copy-start | bytes 3145732 | tf_op jit(solution)/shard_map/while
  153.6 4.5 %copy-start.7 = (f32[512,512]{1,0:T(8,128)S(1)}, f32[512,512]{1,0:T(8,128)}, u32[]{:S(2)}) copy-start(f32[512,512]{1,0:T(8,128)} %get-tuple-element.602) | copy-start | bytes 3145732 | tf_op jit(solution)/shard_map/while
  158.1 5.8 %copy-start.2 = (f32[512,1024]{1,0:T(8,128)S(1)}, f32[512,1024]{1,0:T(8,128)}, u32[]{:S(2)}) copy-start(f32[512,1024]{1,0:T(8,128)} %convolution_add_fusion.7) | copy-start | bytes 6291460 | tf_op jit(solution)/shard_map/while
  175.0 0.7 copy-start.8
  175.0 1.2 copy-start.3
  175.0 35.4 %copy-start.9 = (bf16[512,64]{0,1:T(8,128)(2,1)S(1)}, bf16[512,64]{0,1:T(8,128)(2,1)}, u32[]{:S(2)}) copy-start(bf16[512,64]{0,1:T(8,128)(2,1)} %param.11) | copy-start | bytes 196612
  175.0 93.9 %all-reduce.2.cloned.1.call-start = ((), (), s32[]{:S(2)}) async-start(), calls=%async_computation.4 | async-start | bytes 131072 | tf_op jit(solution)/shard_map/psum | solution.py:103
  176.2 38.9 %copy-start.4 = (f32[512,512]{1,0:T(8,128)S(1)}, f32[512,512]{1,0:T(8,128)}, u32[]{:S(2)}) copy-start(f32[512,512]{1,0:T(8,128)} %get-tuple-element.314) | copy-start | bytes 3145732
Sparse Core Ops, SparseCore 0:
  9.8 29.1 all-gather.4
  41.5 26.6 all-gather.2
  175.1 35.2 reduce-scatter.1
  215.2 53.5 all-reduce.1
where the time goes:
time: 278 us; the launch traced here: 277 us
  waiting for transfers between devices  127 us (46%)
  matrix products  96.8 us (35%)
  other arithmetic  25.8 us (9%)
  between operations  13.9 us (5%)
  local copies, waits for them, and re-layouts  12.3 us (4%)
    dot_general x10, matrix products, transform(): jnp.dot(left, right, precision=lax.Precision.HIGH, preferred_element_type...  60.8 us
    psum x1, waiting for transfers between devices, body(): grad_hidden = lax.psum(partial_hidden, 'chan')  50 us
    dot_general x21, matrix products, plain_dot(): return jnp.dot(left, right, preferred_element_type=jnp.float32)  36.1 us
    reduce_scatter x1, waiting for transfers between devices, body(): lax.psum_scatter(final[2][:, period:period + seq_total], 'seq', scatter_d...  31.7 us
    all_gather x1, waiting for transfers between devices, body(): arrived = lax.all_gather(grad_out, 'seq', axis=1, tiled=True)  26.3 us
    all_gather x1, waiting for transfers between devices, body(): filt_all = lax.all_gather(filt, 'seq', axis=1, tiled=True)  18.8 us
    add x4, other arithmetic, step(): acc_im = state[1] + live_flag * (spec_re * filt_im - spec_im * filt_re)  17.5 us
    unnamed x14, local copies, waits for them, and re-layouts  6.87 us
  transfers between devices with their start and end apart: 4, of which 4 were waited for; matrix products, arithmetic and copies ran while one was open for 8% of the time, Pallas kernels for 0%

commit v1 on v0

v1 whole, which is shorter than its diff:
```python
import functools

import jax
import jax.numpy as jnp
import ml_dtypes
import numpy as np
from jax import lax
from jax.experimental import pallas as pl
from jax.experimental.pallas import tpu as pltpu
from jax.sharding import PartitionSpec as P

F32 = jnp.float32
BF16 = jnp.bfloat16


def tables(block):
    k = np.concatenate([np.arange(0, block, 2), np.arange(1, block, 2)]).astype(np.float64)
    phase = np.pi * (k[None, :] + 0.5) * np.arange(block, dtype=np.float64)[:, None] / block
    forward = np.concatenate([np.cos(phase), -np.sin(phase)], axis=1)
    back = forward.T / block
    return forward.astype(ml_dtypes.bfloat16), back.astype(ml_dtypes.bfloat16)


def dot(left, right):
    return jnp.dot(left, right, preferred_element_type=F32)


def xor_permute(value, axis, size, k):
    return lax.ppermute(value, axis, [(j, j ^ k) for j in range(size)])


def correlate(rows, block, spec_g, spec_z, prod):
    half = block // 2
    step = 16

    def chunk(c, carry):
        at = pl.ds(pl.multiple_of(c * step, step), step)
        for part, sign in ((0, 1.0), (1, -1.0)):
            re = pl.ds(part * half, half)
            im = pl.ds(block + part * half, half)
            g = [(spec_g[j, at, re], spec_g[j, at, im]) for j in range(4)]
            z = [(spec_z[j, at, re], spec_z[j, at, im]) for j in range(4)]
            later = None
            for d in (3, 2, 1, 0):
                sum_re = sum_im = None
                for j in range(d, 4):
                    gr, gi = g[j]
                    zr, zi = z[j - d]
                    term_re = gr * zr + gi * zi
                    term_im = gi * zr - gr * zi
                    sum_re = term_re if sum_re is None else sum_re + term_re
                    sum_im = term_im if sum_im is None else sum_im + term_im
                if later is None:
                    out_re, out_im = sum_re, sum_im
                elif sign > 0:
                    out_re, out_im = sum_re + later[1], sum_im - later[0]
                else:
                    out_re, out_im = sum_re - later[1], sum_im + later[0]
                prod[d, at, re] = out_re.astype(BF16)
                prod[d, at, im] = out_im.astype(BF16)
                later = (sum_re, sum_im)
        return carry

    lax.fori_loop(0, rows // step, chunk, 0)


def filter_kernel(rows, block, total, s0, s1, s2, s3, table, back, rates_ref, mix_ref, *refs):
    filt_out, hidden_out, (spec_g, spec_z, prod) = refs[:4], refs[4:8], refs[8:]
    me = lax.axis_index("seq")
    for k, slot in enumerate((s0, s1, s2, s3)):
        spec = dot(slot[...], table[...])
        spec_g[me ^ k] = spec[:rows]
        spec_z[me ^ k] = spec[rows:]
    correlate(rows, block, spec_g, spec_z, prod)
    mine = pl.ds(pl.multiple_of(me * rows, rows), rows)
    rates = jnp.broadcast_to(rates_ref[:, mine], (block, rows)).T
    mix = mix_ref[:, mine]
    for k in range(4):
        values = dot(prod[me ^ k], back[...])
        lags = lax.broadcasted_iota(jnp.int32, (rows, block), 1) + (me ^ k) * block
        windowed = values * jnp.exp(-rates * lags.astype(F32) / total)
        high = windowed.astype(BF16)
        low = (windowed - high.astype(F32)).astype(BF16)
        hidden = dot(mix, high) + dot(mix, low)
        filt_out[k][...] = values.astype(filt_out[k].dtype)
        hidden_out[k][...] = hidden.astype(hidden_out[k].dtype)


def input_kernel(rows, block, s0, s1, s2, s3, f0, f1, f2, f3, w1, w2, w3, table, back, *refs):
    outs, (spec_g, spec_z, prod) = refs[:4], refs[4:]
    me = lax.axis_index("seq")
    for k, (slot, f) in enumerate(((s0, f0), (s1, f1), (s2, f2), (s3, f3))):
        spec_g[me ^ k] = dot(slot[:rows], table[...])
        spec_z[me ^ k] = dot(f[...], table[...])
    correlate(rows, block, spec_g, spec_z, prod)
    for k, out in enumerate(outs):
        out[:rows] = dot(prod[me ^ k], back[...]).astype(BF16)
    for out, w in zip(outs[1:], (w1, w2, w3)):
        out[rows:] = w[...]


def sum_kernel(h0, h1, h2, h3, after, out, sent):
    del after
    total = (h0[...] + h1[...].astype(F32)) + (h2[...].astype(F32) + h3[...].astype(F32))
    out[...] = total
    sent[...] = total.astype(BF16)


def unpack_kernel(rows, w0, v0, r1, r2, r3, filt_out, in_out):
    me = lax.axis_index("seq")
    filt_out[me] = w0[...]
    in_out[me] = v0[...]
    for k, r in enumerate((r1, r2, r3), 1):
        in_out[me ^ k] = r[:rows]
        filt_out[me ^ k] = r[rows:].astype(F32)


def body_four(channel_axis, inputs, grad_out, filt, rates, mix_weight):
    channels, block = inputs.shape
    rows = channels // 4
    total = 4 * block
    hidden = mix_weight.shape[1]
    forward, back = (jnp.asarray(t) for t in tables(block))
    shape = jax.ShapeDtypeStruct
    vmem = pl.BlockSpec(memory_space=pltpu.VMEM)
    params = pltpu.CompilerParams(vmem_limit_bytes=8 * 1024 * 1024)
    small = pltpu.CompilerParams(vmem_limit_bytes=2 * 1024 * 1024)
    cost = pl.CostEstimate(flops=1000, bytes_accessed=1000, transcendentals=0)
    scratch = [
        pltpu.VMEM((4, rows, 2 * block), F32),
        pltpu.VMEM((4, rows, 2 * block), F32),
        pltpu.VMEM((4, rows, 2 * block), BF16),
    ]

    me = lax.axis_index("seq")
    arrays = jnp.stack([value.reshape(4, rows, block) for value in (grad_out, inputs, filt)], 1)
    parts = [lax.dynamic_index_in_dim(arrays, me ^ k, 0, keepdims=False) for k in range(4)]
    slots = [p[:2].reshape(2 * rows, block) for p in parts]
    slots_f = [p[2] for p in parts]
    slots = slots[:1] + [xor_permute(slots[k], "seq", 4, k) for k in (1, 2, 3)]
    slots_f = slots_f[:1] + [xor_permute(slots_f[k], "seq", 4, k) for k in (1, 2, 3)]

    made = pl.pallas_call(
        functools.partial(filter_kernel, rows, block, total),
        out_shape=[shape((rows, block), F32)]
        + [shape((rows, block), BF16)] * 3
        + [shape((hidden, block), F32)]
        + [shape((hidden, block), BF16)] * 3,
        in_specs=[vmem] * 8,
        out_specs=[vmem] * 8,
        scratch_shapes=scratch,
        compiler_params=params,
        cost_estimate=cost,
    )(*slots, forward, back, rates.reshape(1, channels), mix_weight.T)

    got_hidden = [xor_permute(made[4 + k], "seq", 4, k) for k in (1, 2, 3)]

    made_in = pl.pallas_call(
        functools.partial(input_kernel, rows, block),
        out_shape=[shape((rows, block), BF16)] + [shape((2 * rows, block), BF16)] * 3,
        in_specs=[vmem] * 13,
        out_specs=[vmem] * 4,
        scratch_shapes=scratch,
        compiler_params=params,
        cost_estimate=cost,
    )(*slots, *slots_f, *made[1:4], forward, back)
    got = [xor_permute(made_in[k], "seq", 4, k) for k in (1, 2, 3)]

    partial, partial_sent = pl.pallas_call(
        sum_kernel,
        out_shape=[shape((hidden, block), F32), shape((hidden, block), BF16)],
        in_specs=[vmem] * 4 + [pl.BlockSpec(memory_space=pl.ANY)],
        out_specs=[vmem] * 2,
        compiler_params=small,
        cost_estimate=cost,
    )(made[4], *got_hidden, made_in[1])
    pair = partial + xor_permute(partial_sent, "chan", channel_axis, 1).astype(F32)
    pair_sent = pair.astype(BF16)
    grad_hidden = pair
    for k in range(2, channel_axis, 2):
        grad_hidden = grad_hidden + xor_permute(pair_sent, "chan", channel_axis, k).astype(F32)

    grad_filt, grad_in = pl.pallas_call(
        functools.partial(unpack_kernel, rows),
        out_shape=[shape((4, rows, block), F32), shape((4, rows, block), BF16)],
        in_specs=[vmem] * 5,
        out_specs=[vmem] * 2,
        compiler_params=small,
        cost_estimate=cost,
    )(made[0], made_in[0], *got)
    return grad_in.reshape(channels, block), grad_filt.reshape(channels, block), grad_hidden


def body_any(blocks, inputs, grad_out, filt, rates, mix_weight):
    channels, block = inputs.shape
    rows = channels // blocks
    total = blocks * block
    half = block // 2
    me = lax.axis_index("seq")
    forward, back = (jnp.asarray(t) for t in tables(block))
    sign = jnp.where(jnp.arange(block) < half, 1.0, -1.0).astype(F32)

    def spread(value):
        return lax.all_to_all(value.reshape(blocks, rows, block), "seq", 0, 0, tiled=True)

    def spectrum(value):
        spec = dot(value, forward)
        return spec[..., :block], spec[..., block:]

    def correlate_blocks(g, z):
        sums = []
        for d in range(blocks):
            gr, gi, zr, zi = g[0][d:], g[1][d:], z[0][: blocks - d], z[1][: blocks - d]
            sums.append(((gr * zr + gi * zi).sum(0), (gi * zr - gr * zi).sum(0)))
        sums.append((jnp.zeros_like(sums[0][0]),) * 2)
        out = [
            jnp.concatenate([sums[d][0] + sign * sums[d + 1][1], sums[d][1] - sign * sums[d + 1][0]], axis=-1)
            for d in range(blocks)
        ]
        return dot(jnp.stack(out).astype(BF16), back)

    spec_g = spectrum(spread(grad_out))
    grad_filt = correlate_blocks(spec_g, spectrum(spread(inputs)))
    grad_in = correlate_blocks(spec_g, spectrum(spread(filt)))
    grad_in = spread(grad_in.astype(BF16)).reshape(channels, block)
    grad_filt = lax.all_to_all(grad_filt, "seq", 0, 0, tiled=True).reshape(channels, block)
    lags = (me * block + jnp.arange(block, dtype=jnp.int32)).astype(F32)
    windowed = grad_filt * jnp.exp(-rates[:, None] * lags[None, :] / total)
    high = windowed.astype(BF16)
    low = (windowed - high.astype(F32)).astype(BF16)
    grad_hidden = lax.psum(dot(mix_weight.T, high) + dot(mix_weight.T, low), "chan")
    return grad_in, grad_filt, grad_hidden


def solution(mesh):
    blocks, chan = mesh.shape["seq"], mesh.shape["chan"]

    def body(inputs, grad_out, filt, rates, mix_weight):
        if blocks == 4 and chan & (chan - 1) == 0 and inputs.shape[0] % 512 == 0 and inputs.shape[1] % 256 == 0:
            return body_four(chan, inputs, grad_out, filt, rates, mix_weight)
        return body_any(blocks, inputs, grad_out, filt, rates, mix_weight)

    return jax.shard_map(
        body,
        mesh=mesh,
        in_specs=(P("chan", "seq"), P("chan", "seq"), P("chan", "seq"), P("chan"), P("chan", None)),
        out_specs=(P("chan", "seq"), P("chan", "seq"), P(None, "seq")),
        check_vma=False,
    )
```

time: 278 us -> 39.9 us (0.14)
  waiting for transfers between devices: 127 us -> 11.3 us
  matrix products: 96.8 us -> 0 us
  other arithmetic: 25.8 us -> 1.86 us
  starting transfers between devices: 0.38 us -> 21 us
  between operations: 13.9 us -> 0.73 us
  local copies, waits for them, and re-layouts: 12.3 us -> 0.75 us
  Pallas kernels: 0 us -> 4.08 us
    dot_general x31 -> x0, matrix products: 96.8 us -> none  [the longest x10 60.8 us: transform(): jnp.dot(left, right, precision=lax.Precision.HIGH, preferred_element_type...]
    psum x1 -> x0, waiting for transfers between devices: 50 us -> none  [body(): grad_hidden = lax.psum(partial_hidden, 'chan')]
    all_gather x2 -> x0, waiting for transfers between devices: 45.1 us -> none  [the longest x1 26.3 us: body(): arrived = lax.all_gather(grad_out, 'seq', axis=1, tiled=True)]
    reduce_scatter x1 -> x0, waiting for transfers between devices: 31.7 us -> none  [body(): lax.psum_scatter(final[2][:, period:period + seq_total], 'seq', scatter_d...]
    ppermute x0 -> x16, starting transfers between devices: none -> 21 us  [xor_permute(): return lax.ppermute(value, axis, [(j, j ^ k) for j in range(size)])]
    add x4 -> x1, other arithmetic: 17.5 us -> 0.65 us  [body_four(): grad_hidden + xor_permute(pair_sent, 'chan', channel_axis, k).astype(F32)]
    ppermute x0 -> x16, waiting for transfers between devices: none -> 11.3 us  [xor_permute(): return lax.ppermute(value, axis, [(j, j ^ k) for j in range(size)])]
    unnamed x14 -> x8, local copies, waits for them, and re-layouts: 6.87 us -> 0.68 us
  transfers between devices with their start and end apart: 4 -> 16, of which waited for: 4 -> 8; matrix products, arithmetic and copies ran while one was open for 8% -> 2% of each run, Pallas kernels for 0% -> 8%
where the time goes in v1:
time: 39.9 us; the launch traced here: 39.7 us
  starting transfers between devices  21 us (53%)
  waiting for transfers between devices  11.3 us (28%)
  Pallas kernels  4.08 us (10%)
  other arithmetic  1.86 us (5%)
  local copies, waits for them, and re-layouts  0.75 us (2%)
  between operations  0.73 us (2%)
    ppermute x16, starting transfers between devices, xor_permute(): return lax.ppermute(value, axis, [(j, j ^ k) for j in range(size)])  21 us
    ppermute x16, waiting for transfers between devices, xor_permute(): return lax.ppermute(value, axis, [(j, j ^ k) for j in range(size)])  11.3 us
    pallas_call x1, Pallas kernels, body_four(): pl.pallas_call(functools.partial(filter_kernel, rows, block, total), out_...  1.95 us
    another operation x1, other arithmetic, body_four(): jnp.stack([value.reshape(4, rows, block) for value in (grad_out, inputs,...  1.2 us
    pallas_call x1, Pallas kernels, body_four(): pl.pallas_call(functools.partial(input_kernel, rows, block), out_shape=[s...  1.17 us
    pallas_call x1, Pallas kernels, body_four(): pl.pallas_call(functools.partial(unpack_kernel, rows), out_shape=[shape((...  0.94 us
  transfers between devices with their start and end apart: 16, of which 8 were waited for; matrix products, arithmetic and copies ran while one was open for 2% of the time, Pallas kernels for 8%

profile of v1, /device:TPU:0, one launch (start us, length us, event | category | flops | bytes accessed | tf_op | source)
XLA Modules:
  0.0 39.7 jit_solution(17869982233025394593)
XLA Ops:
  0.7 1.2 %pad_maximum_fusion = bf16[4,3,128,256]{3,2,1,0:T(8,128)(2,1)S(1)} fusion(bf16[4,1,128,256]{3,2,1,0:T(8,128)(2,1)} %bitcast.23, bf16[4,1,128,256]{3,2,1,0:T(8,128)(2,1)} %bitcast.24, bf16[4,1,128,256]{3,2,1,0:T(8,128)(2,1)} %bitcast.25), kind=kLoop, calls=%fused_computation | loop fusion | flops 786432 | bytes 1572864 | tf_op jit(solution)/shard_map/stack | solution.py:136
  1.9 0.0 copy-start.2
  1.9 3.0 %collective-permute-start.1 = (bf16[256,256]{1,0:T(8,128)(2,1)S(1)}, bf16[256,256]{1,0:T(8,128)(2,1)S(1)}, u32[]{:S(2)}, u32[]{:S(2)}) collective-permute-start(bf16[256,256]{1,0:T(8,128)(2,1)S(1)} %bitcast.28), channel_id=1, source_target_pairs={{0,16},{8,24},{16,0},{24,8},{1,17},{9,25},{17,1},{25,9},{2,18},{10... | collective-permute-start | bytes 393224 | tf_op jit(solution)/shard_map/ppermute | solution.py:29
  5.0 1.4 %collective-permute-start.2 = (bf16[256,256]{1,0:T(8,128)(2,1)S(1)}, bf16[256,256]{1,0:T(8,128)(2,1)S(1)}, u32[]{:S(2)}, u32[]{:S(2)}) collective-permute-start(bf16[256,256]{1,0:T(8,128)(2,1)S(1)} %bitcast.27), channel_id=1, source_target_pairs={{0,24},{8,16},{16,8},{24,0},{1,25},{9,17},{17,9},{25,1},{2,26},{10... | collective-permute-start | bytes 393224 | tf_op jit(solution)/shard_map/ppermute | solution.py:29
  6.4 0.1 collective-permute-start
  6.5 0.0 copy-start
  6.5 0.0 copy-start.1
  6.5 2.9 %collective-permute-start.5 = (bf16[128,256]{1,0:T(8,128)(2,1)S(1)}, bf16[128,256]{1,0:T(8,128)(2,1)S(1)}, u32[]{:S(2)}, u32[]{:S(2)}) collective-permute-start(bf16[128,256]{1,0:T(8,128)(2,1)S(1)} %get-tuple-element.35), channel_id=1, source_target_pairs={{0,24},{8,16},{16,8},{24,0},{1,25},{9,17},{17,9},{25,1},{2,26},{10... | collective-permute-start | bytes 196616 | tf_op jit(solution)/shard_map/ppermute | solution.py:29
  9.5 0.5 %collective-permute-start.4 = (bf16[128,256]{1,0:T(8,128)(2,1)S(1)}, bf16[128,256]{1,0:T(8,128)(2,1)S(1)}, u32[]{:S(2)}, u32[]{:S(2)}) collective-permute-start(bf16[128,256]{1,0:T(8,128)(2,1)S(1)} %get-tuple-element.36), channel_id=1, source_target_pairs={{0,16},{8,24},{16,0},{24,8},{1,17},{9,25},{17,1},{25,9},{2,18},{10... | collective-permute-start | bytes 196616 | tf_op jit(solution)/shard_map/ppermute | solution.py:29
  10.0 1.9 %collective-permute-done.1.s2 = bf16[256,256]{1,0:T(8,128)(2,1)S(1)} collective-permute-done((bf16[256,256]{1,0:T(8,128)(2,1)S(1)}, bf16[256,256]{1,0:T(8,128)(2,1)S(1)}, u32[]{:S(2)}, u32[]{:S(2)}) %collective-permute-start.1) | collective-permute-done | bytes 131104 | tf_op jit(solution)/shard_map/ppermute | solution.py:29
  11.9 1.6 %collective-permute-start.3 = (bf16[128,256]{1,0:T(8,128)(2,1)S(1)}, bf16[128,256]{1,0:T(8,128)(2,1)S(1)}, u32[]{:S(2)}, u32[]{:S(2)}) collective-permute-start(bf16[128,256]{1,0:T(8,128)(2,1)S(1)} %get-tuple-element.37), channel_id=1, source_target_pairs={{0,8},{8,0},{16,24},{24,16},{1,9},{9,1},{17,25},{25,17},{2,10},{10... | collective-permute-start | bytes 196616 | tf_op jit(solution)/shard_map/ppermute | solution.py:29
  13.4 0.0 collective-permute-done.2.s3
  13.4 0.2 collective-permute-done.s1
  13.7 0.0 copy-start.3
  13.7 0.0 copy-done.2
  13.7 0.0 copy-done
  13.7 0.0 copy-done.1
  13.7 0.7 %copy-done.3 = f32[512]{0:T(512)S(1)} copy-done((f32[512]{0:T(512)S(1)}, f32[512]{0:T(512)}, u32[]{:S(2)}) %copy-start.3) | copy-done | bytes 2072
  14.3 2.0 %shard_map.94 = (f32[128,256]{1,0:T(8,128)S(1)}, bf16[128,256]{1,0:T(8,128)(2,1)S(1)}, bf16[128,256]{1,0:T(8,128)(2,1)S(1)}, bf16[128,256]{1,0:T(8,128)(2,1)S(1)...) custom-call(bf16[256,256]{1,0:T(8,128)(2,1)S(1)} %bitcast.19, ...), custom_call_target="tpu_custom_call" | custom-call | flops 1000 | bytes 1000 | tf_op jit(solution)/shard_map/pallas_call | solution.py:143
  16.3 2.0 %collective-permute-start.9 = (bf16[64,256]{1,0:T(8,128)(2,1)S(1)}, bf16[64,256]{1,0:T(8,128)(2,1)S(1)}, u32[]{:S(2)}, u32[]{:S(2)}) collective-permute-start(bf16[64,256]{1,0:T(8,128)(2,1)S(1)} %get-tuple-element.30), channel_id=1, source_target_pairs={{0,8},{8,0},{16,24},{24,16},{1,9},{9,1},{17,25},{25,17},{2,10},{10... | collective-permute-start | bytes 98312 | tf_op jit(solution)/shard_map/ppermute | solution.py:29
  18.3 1.5 %collective-permute-start.10 = (bf16[64,256]{1,0:T(8,128)(2,1)S(1)}, bf16[64,256]{1,0:T(8,128)(2,1)S(1)}, u32[]{:S(2)}, u32[]{:S(2)}) collective-permute-start(bf16[64,256]{1,0:T(8,128)(2,1)S(1)} %get-tuple-element.31), channel_id=1, source_target_pairs={{0,16},{8,24},{16,0},{24,8},{1,17},{9,25},{17,1},{25,9},{2,18},{10... | collective-permute-start | bytes 98312 | tf_op jit(solution)/shard_map/ppermute | solution.py:29
  19.8 0.0 collective-permute-done.5.f3
  19.8 0.2 collective-permute-start.11
  20.1 0.0 collective-permute-done.4.f2
  20.1 0.0 collective-permute-done.3.f1
  20.1 1.2 %shard_map.95 = (bf16[128,256]{1,0:T(8,128)(2,1)S(1)}, bf16[256,256]{1,0:T(8,128)(2,1)S(1)}, bf16[256,256]{1,0:T(8,128)(2,1)S(1)}, bf16[256,256]{1,0:T(8,128)(2,1)S(1)}) custom-call(bf16[256,256]{1,0:T(8,128)(2,1)S(1)} %bitcast.20, bf16[256,256]{1,0:T(8,128)(2,1)S(1)} %collective-permute-done.s1, bf16[256,256]{1,0:T(8,128)(2,1)S(1)} %collective-permute-done.1.s2, ...), custom_call_target="tpu_custom_call" | custom-call | flops 1000 | bytes 1000 | tf_op jit(solution)/shard_map/pallas_call | solution.py:158
  21.3 0.0 collective-permute-done.9.h1
  21.3 1.0 %collective-permute-done.10.h2 = bf16[64,256]{1,0:T(8,128)(2,1)S(1)} collective-permute-done((bf16[64,256]{1,0:T(8,128)(2,1)S(1)}, bf16[64,256]{1,0:T(8,128)(2,1)S(1)}, u32[]{:S(2)}, u32[]{:S(2)}) %collective-permute-start.10) | collective-permute-done | bytes 32800 | tf_op jit(solution)/shard_map/ppermute | solution.py:29
  22.2 2.4 %collective-permute-done.11.h3 = bf16[64,256]{1,0:T(8,128)(2,1)S(1)} collective-permute-done((bf16[64,256]{1,0:T(8,128)(2,1)S(1)}, bf16[64,256]{1,0:T(8,128)(2,1)S(1)}, u32[]{:S(2)}, u32[]{:S(2)}) %collective-permute-start.11) | collective-permute-done | bytes 32800 | tf_op jit(solution)/shard_map/ppermute | solution.py:29
  24.7 0.1 collective-permute-start.12
  24.8 1.2 %collective-permute-done.12 = bf16[64,256]{1,0:T(8,128)(2,1)S(1)} collective-permute-done((bf16[64,256]{1,0:T(8,128)(2,1)S(1)}, bf16[64,256]{1,0:T(8,128)(2,1)S(1)}, u32[]{:S(2)}, u32[]{:S(2)}) %collective-permute-start.12) | collective-permute-done | bytes 32800 | tf_op jit(solution)/shard_map/ppermute | solution.py:29
  26.0 3.7 %collective-permute-start.15 = (bf16[64,256]{1,0:T(8,128)(2,1)S(1)}, bf16[64,256]{1,0:T(8,128)(2,1)S(1)}, u32[]{:S(2)}, u32[]{:S(2)}) collective-permute-start(bf16[64,256]{1,0:T(8,128)(2,1)S(1)} %fusion), channel_id=1, source_target_pairs={{0,6},{1,7},{2,4},{3,5},{4,2},{5,3},{6,0},{7,1},{8,14},{9,15},{10,... | collective-permute-start | bytes 98312 | tf_op jit(solution)/shard_map/ppermute | solution.py:29
  29.6 0.0 collective-permute-start.14
  29.6 0.8 %collective-permute-start.13 = (bf16[64,256]{1,0:T(8,128)(2,1)S(1)}, bf16[64,256]{1,0:T(8,128)(2,1)S(1)}, u32[]{:S(2)}, u32[]{:S(2)}) collective-permute-start(bf16[64,256]{1,0:T(8,128)(2,1)S(1)} %fusion), channel_id=1, source_target_pairs={{0,2},{1,3},{2,0},{3,1},{4,6},{5,7},{6,4},{7,5},{8,10},{9,11},{10,... | collective-permute-start | bytes 98312 | tf_op jit(solution)/shard_map/ppermute | solution.py:29
  30.4 0.8 %collective-permute-start.6 = (bf16[256,256]{1,0:T(8,128)(2,1)S(1)}, bf16[256,256]{1,0:T(8,128)(2,1)S(1)}, u32[]{:S(2)}, u32[]{:S(2)}) collective-permute-start(bf16[256,256]{1,0:T(8,128)(2,1)S(1)} %get-tuple-element.24.after), channel_id=1, source_target_pairs={{0,8},{8,0},{16,24},{24,16},{1,9},{9,1},{17,25},{25,17},{2,10},{10... | collective-permute-start | bytes 393224 | tf_op jit(solution)/shard_map/ppermute | solution.py:29
  31.2 0.1 collective-permute-start.7
  31.3 0.4 %collective-permute-done.15 = bf16[64,256]{1,0:T(8,128)(2,1)S(1)} collective-permute-done((bf16[64,256]{1,0:T(8,128)(2,1)S(1)}, bf16[64,256]{1,0:T(8,128)(2,1)S(1)}, u32[]{:S(2)}, u32[]{:S(2)}) %collective-permute-start.15) | collective-permute-done | bytes 32800 | tf_op jit(solution)/shard_map/ppermute | solution.py:29
  31.7 2.2 %collective-permute-start.8 = (bf16[256,256]{1,0:T(8,128)(2,1)S(1)}, bf16[256,256]{1,0:T(8,128)(2,1)S(1)}, u32[]{:S(2)}, u32[]{:S(2)}) collective-permute-start(bf16[256,256]{1,0:T(8,128)(2,1)S(1)} %get-tuple-element.26), channel_id=1, source_target_pairs={{0,24},{8,16},{16,8},{24,0},{1,25},{9,17},{17,9},{25,1},{2,26},{10... | collective-permute-start | bytes 393224 | tf_op jit(solution)/shard_map/ppermute | solution.py:29
  33.9 0.5 %collective-permute-done.14 = bf16[64,256]{1,0:T(8,128)(2,1)S(1)} collective-permute-done((bf16[64,256]{1,0:T(8,128)(2,1)S(1)}, bf16[64,256]{1,0:T(8,128)(2,1)S(1)}, u32[]{:S(2)}, u32[]{:S(2)}) %collective-permute-start.14) | collective-permute-done | bytes 32800 | tf_op jit(solution)/shard_map/ppermute | solution.py:29
  34.4 0.0 collective-permute-done.13
  34.4 0.7 %convert_add_fusion = f32[64,256]{1,0:T(8,128)} fusion(bf16[64,256]{1,0:T(8,128)(2,1)S(1)} %collective-permute-done.15, bf16[64,256]{1,0:T(8,128)(2,1)S(1)} %collective-permute-done.14, bf16[64,256]{1,0:T(8,128)(2,1)S(1)} %collective-permute-done.13, f32[64,256]{1,0:T(8,128)S(1)} %get-tuple-element.33, bf16[64,256]{1,0:T(8,128)(2,1)S(1)} %collective-permute-done.12), kind=kLoop, calls=%fused_computation.5 | loop fusion | flops 131072 | bytes 262144 | tf_op jit(solution)/shard_map/add | solution.py:181
  35.1 3.7 %collective-permute-done.7.r2 = bf16[256,256]{1,0:T(8,128)(2,1)S(1)} collective-permute-done((bf16[256,256]{1,0:T(8,128)(2,1)S(1)}, bf16[256,256]{1,0:T(8,128)(2,1)S(1)}, u32[]{:S(2)}, u32[]{:S(2)}) %collective-permute-start.7) | collective-permute-done | bytes 131104 | tf_op jit(solution)/shard_map/ppermute | solution.py:29
  38.8 0.0 collective-permute-done.8.r3
  38.8 0.0 collective-permute-done.6.r1
  38.8 0.9 %shard_map.96 = (f32[4,128,256]{2,1,0:T(8,128)}, bf16[4,128,256]{2,1,0:T(8,128)(2,1)}) custom-call(f32[128,256]{1,0:T(8,128)S(1)} %get-tuple-element.19.w0, bf16[128,256]{1,0:T(8,128)(2,1)S(1)} %get-tuple-element.23.v0, bf16[256,256]{1,0:T(8,128)(2,1)S(1)} %collective-permute-done.6.r1, bf16[256,256]{1,0:T(8,128)(2,1)S(1)} %collective-permute-done.7.r2, ...), custom_call_target="tpu_custom_call" | custom-call | flops 1000 | bytes 1000 | tf_op jit(solution)/shard_map/pallas_call | solution.py:183
  (4 shorter events, 0.1 us)
Async XLA Ops:
  1.9 11.8 %copy-start.2 = (bf16[512,64]{0,1:T(8,128)(2,1)S(1)}, bf16[512,64]{0,1:T(8,128)(2,1)}, u32[]{:S(2)}) copy-start(bf16[512,64]{0,1:T(8,128)(2,1)} %param.11) | copy-start | bytes 196612
  1.9 9.9 %collective-permute-start.1 = (bf16[256,256]{1,0:T(8,128)(2,1)S(1)}, bf16[256,256]{1,0:T(8,128)(2,1)S(1)}, u32[]{:S(2)}, u32[]{:S(2)}) collective-permute-start(bf16[256,256]{1,0:T(8,128)(2,1)S(1)} %bitcast.28), channel_id=1, source_target_pairs={{0,16},{8,24},{16,0},{24,8},{1,17},{9,25},{17,1},{25,9},{2,18},{10... | collective-permute-start | bytes 393224 | tf_op jit(solution)/shard_map/ppermute | solution.py:29
  5.0 8.5 %collective-permute-start.2 = (bf16[256,256]{1,0:T(8,128)(2,1)S(1)}, bf16[256,256]{1,0:T(8,128)(2,1)S(1)}, u32[]{:S(2)}, u32[]{:S(2)}) collective-permute-start(bf16[256,256]{1,0:T(8,128)(2,1)S(1)} %bitcast.27), channel_id=1, source_target_pairs={{0,24},{8,16},{16,8},{24,0},{1,25},{9,17},{17,9},{25,1},{2,26},{10... | collective-permute-start | bytes 393224 | tf_op jit(solution)/shard_map/ppermute | solution.py:29
  6.4 7.3 %collective-permute-start = (bf16[256,256]{1,0:T(8,128)(2,1)S(1)}, bf16[256,256]{1,0:T(8,128)(2,1)S(1)}, u32[]{:S(2)}, u32[]{:S(2)}) collective-permute-start(bf16[256,256]{1,0:T(8,128)(2,1)S(1)} %bitcast.26), channel_id=1, source_target_pairs={{0,8},{8,0},{16,24},{24,16},{1,9},{9,1},{17,25},{25,17},{2,10},{10... | collective-permute-start | bytes 393224 | tf_op jit(solution)/shard_map/ppermute | solution.py:29
  6.5 7.2 %copy-start = (bf16[512,256]{1,0:T(8,128)(2,1)S(1)}, bf16[512,256]{1,0:T(8,128)(2,1)}, u32[]{:S(2)}) copy-start(bf16[512,256]{1,0:T(8,128)(2,1)} %constant.28.clone.back) | copy-start | bytes 786436
  6.5 7.2 %copy-start.1 = (bf16[256,512]{1,0:T(8,128)(2,1)S(1)}, bf16[256,512]{1,0:T(8,128)(2,1)}, u32[]{:S(2)}) copy-start(bf16[256,512]{1,0:T(8,128)(2,1)} %constant.27.clone.table) | copy-start | bytes 786436
  6.5 13.3 %collective-permute-start.5 = (bf16[128,256]{1,0:T(8,128)(2,1)S(1)}, bf16[128,256]{1,0:T(8,128)(2,1)S(1)}, u32[]{:S(2)}, u32[]{:S(2)}) collective-permute-start(bf16[128,256]{1,0:T(8,128)(2,1)S(1)} %get-tuple-element.35), channel_id=1, source_target_pairs={{0,24},{8,16},{16,8},{24,0},{1,25},{9,17},{17,9},{25,1},{2,26},{10... | collective-permute-start | bytes 196616 | tf_op jit(solution)/shard_map/ppermute | solution.py:29
  9.5 10.6 %collective-permute-start.4 = (bf16[128,256]{1,0:T(8,128)(2,1)S(1)}, bf16[128,256]{1,0:T(8,128)(2,1)S(1)}, u32[]{:S(2)}, u32[]{:S(2)}) collective-permute-start(bf16[128,256]{1,0:T(8,128)(2,1)S(1)} %get-tuple-element.36), channel_id=1, source_target_pairs={{0,16},{8,24},{16,0},{24,8},{1,17},{9,25},{17,1},{25,9},{2,18},{10... | collective-permute-start | bytes 196616 | tf_op jit(solution)/shard_map/ppermute | solution.py:29
  11.9 8.2 %collective-permute-start.3 = (bf16[128,256]{1,0:T(8,128)(2,1)S(1)}, bf16[128,256]{1,0:T(8,128)(2,1)S(1)}, u32[]{:S(2)}, u32[]{:S(2)}) collective-permute-start(bf16[128,256]{1,0:T(8,128)(2,1)S(1)} %get-tuple-element.37), channel_id=1, source_target_pairs={{0,8},{8,0},{16,24},{24,16},{1,9},{9,1},{17,25},{25,17},{2,10},{10... | collective-permute-start | bytes 196616 | tf_op jit(solution)/shard_map/ppermute | solution.py:29
  13.7 0.7 %copy-start.3 = (f32[512]{0:T(512)S(1)}, f32[512]{0:T(512)}, u32[]{:S(2)}) copy-start(f32[512]{0:T(512)} %param.10) | copy-start | bytes 6148
  16.3 5.0 %collective-permute-start.9 = (bf16[64,256]{1,0:T(8,128)(2,1)S(1)}, bf16[64,256]{1,0:T(8,128)(2,1)S(1)}, u32[]{:S(2)}, u32[]{:S(2)}) collective-permute-start(bf16[64,256]{1,0:T(8,128)(2,1)S(1)} %get-tuple-element.30), channel_id=1, source_target_pairs={{0,8},{8,0},{16,24},{24,16},{1,9},{9,1},{17,25},{25,17},{2,10},{10... | collective-permute-start | bytes 98312 | tf_op jit(solution)/shard_map/ppermute | solution.py:29
  18.3 3.9 %collective-permute-start.10 = (bf16[64,256]{1,0:T(8,128)(2,1)S(1)}, bf16[64,256]{1,0:T(8,128)(2,1)S(1)}, u32[]{:S(2)}, u32[]{:S(2)}) collective-permute-start(bf16[64,256]{1,0:T(8,128)(2,1)S(1)} %get-tuple-element.31), channel_id=1, source_target_pairs={{0,16},{8,24},{16,0},{24,8},{1,17},{9,25},{17,1},{25,9},{2,18},{10... | collective-permute-start | bytes 98312 | tf_op jit(solution)/shard_map/ppermute | solution.py:29
  19.8 4.8 %collective-permute-start.11 = (bf16[64,256]{1,0:T(8,128)(2,1)S(1)}, bf16[64,256]{1,0:T(8,128)(2,1)S(1)}, u32[]{:S(2)}, u32[]{:S(2)}) collective-permute-start(bf16[64,256]{1,0:T(8,128)(2,1)S(1)} %get-tuple-element.32), channel_id=1, source_target_pairs={{0,24},{8,16},{16,8},{24,0},{1,25},{9,17},{17,9},{25,1},{2,26},{10... | collective-permute-start | bytes 98312 | tf_op jit(solution)/shard_map/ppermute | solution.py:29
  24.7 1.3 %collective-permute-start.12 = (bf16[64,256]{1,0:T(8,128)(2,1)S(1)}, bf16[64,256]{1,0:T(8,128)(2,1)S(1)}, u32[]{:S(2)}, u32[]{:S(2)}) collective-permute-start(bf16[64,256]{1,0:T(8,128)(2,1)S(1)} %get-tuple-element.34), channel_id=1, source_target_pairs={{0,1},{1,0},{2,3},{3,2},{4,5},{5,4},{6,7},{7,6},{8,9},{9,8},{10,11... | collective-permute-start | bytes 98312 | tf_op jit(solution)/shard_map/ppermute | solution.py:29
  26.0 5.8 %collective-permute-start.15 = (bf16[64,256]{1,0:T(8,128)(2,1)S(1)}, bf16[64,256]{1,0:T(8,128)(2,1)S(1)}, u32[]{:S(2)}, u32[]{:S(2)}) collective-permute-start(bf16[64,256]{1,0:T(8,128)(2,1)S(1)} %fusion), channel_id=1, source_target_pairs={{0,6},{1,7},{2,4},{3,5},{4,2},{5,3},{6,0},{7,1},{8,14},{9,15},{10,... | collective-permute-start | bytes 98312 | tf_op jit(solution)/shard_map/ppermute | solution.py:29
  29.6 4.8 %collective-permute-start.14 = (bf16[64,256]{1,0:T(8,128)(2,1)S(1)}, bf16[64,256]{1,0:T(8,128)(2,1)S(1)}, u32[]{:S(2)}, u32[]{:S(2)}) collective-permute-start(bf16[64,256]{1,0:T(8,128)(2,1)S(1)} %fusion), channel_id=1, source_target_pairs={{0,4},{1,5},{2,6},{3,7},{4,0},{5,1},{6,2},{7,3},{8,12},{9,13},{10,... | collective-permute-start | bytes 98312 | tf_op jit(solution)/shard_map/ppermute | solution.py:29
  29.6 4.8 %collective-permute-start.13 = (bf16[64,256]{1,0:T(8,128)(2,1)S(1)}, bf16[64,256]{1,0:T(8,128)(2,1)S(1)}, u32[]{:S(2)}, u32[]{:S(2)}) collective-permute-start(bf16[64,256]{1,0:T(8,128)(2,1)S(1)} %fusion), channel_id=1, source_target_pairs={{0,2},{1,3},{2,0},{3,1},{4,6},{5,7},{6,4},{7,5},{8,10},{9,11},{10,... | collective-permute-start | bytes 98312 | tf_op jit(solution)/shard_map/ppermute | solution.py:29
  30.4 8.4 %collective-permute-start.6 = (bf16[256,256]{1,0:T(8,128)(2,1)S(1)}, bf16[256,256]{1,0:T(8,128)(2,1)S(1)}, u32[]{:S(2)}, u32[]{:S(2)}) collective-permute-start(bf16[256,256]{1,0:T(8,128)(2,1)S(1)} %get-tuple-element.24.after), channel_id=1, source_target_pairs={{0,8},{8,0},{16,24},{24,16},{1,9},{9,1},{17,25},{25,17},{2,10},{10... | collective-permute-start | bytes 393224 | tf_op jit(solution)/shard_map/ppermute | solution.py:29
  31.2 7.6 %collective-permute-start.7 = (bf16[256,256]{1,0:T(8,128)(2,1)S(1)}, bf16[256,256]{1,0:T(8,128)(2,1)S(1)}, u32[]{:S(2)}, u32[]{:S(2)}) collective-permute-start(bf16[256,256]{1,0:T(8,128)(2,1)S(1)} %get-tuple-element.25), channel_id=1, source_target_pairs={{0,16},{8,24},{16,0},{24,8},{1,17},{9,25},{17,1},{25,9},{2,18},{10... | collective-permute-start | bytes 393224 | tf_op jit(solution)/shard_map/ppermute | solution.py:29
  31.7 7.0 %collective-permute-start.8 = (bf16[256,256]{1,0:T(8,128)(2,1)S(1)}, bf16[256,256]{1,0:T(8,128)(2,1)S(1)}, u32[]{:S(2)}, u32[]{:S(2)}) collective-permute-start(bf16[256,256]{1,0:T(8,128)(2,1)S(1)} %get-tuple-element.26), channel_id=1, source_target_pairs={{0,24},{8,16},{16,8},{24,0},{1,25},{9,17},{17,9},{25,1},{2,26},{10... | collective-permute-start | bytes 393224 | tf_op jit(solution)/shard_map/ppermute | solution.py:29

commit v2 on v1

--- a/solution.py
+++ b/solution.py
@@ -64,55 +64,63 @@
     lax.fori_loop(0, rows // step, chunk, 0)
 
 
-def filter_kernel(rows, block, total, s0, s1, s2, s3, table, back, rates_ref, mix_ref, *refs):
-    filt_out, hidden_out, (spec_g, spec_z, prod) = refs[:4], refs[4:8], refs[8:]
+def window_kernel(rows, block, total, rates_ref, f_ref, decay, f_out):
+    del f_ref, f_out
+    lags = lax.broadcasted_iota(jnp.int32, (rows, block), 1) + lax.axis_index("seq") * block
+    for n in range(4):
+        rates = jnp.broadcast_to(rates_ref[:, n * rows : (n + 1) * rows], (block, rows)).T
+        decay[n] = jnp.exp(-rates * lags.astype(F32) / total)
+
+
+def filter_kernel(rows, s0, s1, s2, s3, table, back, *refs):
+    outs, (spec_g, spec_z, prod) = refs[:4], refs[4:]
     me = lax.axis_index("seq")
     for k, slot in enumerate((s0, s1, s2, s3)):
         spec = dot(slot[...], table[...])
         spec_g[me ^ k] = spec[:rows]
         spec_z[me ^ k] = spec[rows:]
-    correlate(rows, block, spec_g, spec_z, prod)
-    mine = pl.ds(pl.multiple_of(me * rows, rows), rows)
-    rates = jnp.broadcast_to(rates_ref[:, mine], (block, rows)).T
-    mix = mix_ref[:, mine]
-    for k in range(4):
-        values = dot(prod[me ^ k], back[...])
-        lags = lax.broadcasted_iota(jnp.int32, (rows, block), 1) + (me ^ k) * block
-        windowed = values * jnp.exp(-rates * lags.astype(F32) / total)
-        high = windowed.astype(BF16)
-        low = (windowed - high.astype(F32)).astype(BF16)
-        hidden = dot(mix, high) + dot(mix, low)
-        filt_out[k][...] = values.astype(filt_out[k].dtype)
-        hidden_out[k][...] = hidden.astype(hidden_out[k].dtype)
-
-
-def input_kernel(rows, block, s0, s1, s2, s3, f0, f1, f2, f3, w1, w2, w3, table, back, *refs):
+    correlate(rows, table.shape[0], spec_g, spec_z, prod)
+    for k, out in enumerate(outs):
+        out[...] = dot(prod[me ^ k], back[...]).astype(out.dtype)
+
+
+def input_kernel(rows, s0, s1, s2, s3, f0, f1, f2, f3, table, back, *refs):
     outs, (spec_g, spec_z, prod) = refs[:4], refs[4:]
     me = lax.axis_index("seq")
     for k, (slot, f) in enumerate(((s0, f0), (s1, f1), (s2, f2), (s3, f3))):
         spec_g[me ^ k] = dot(slot[:rows], table[...])
         spec_z[me ^ k] = dot(f[...], table[...])
-    correlate(rows, block, spec_g, spec_z, prod)
+    correlate(rows, table.shape[0], spec_g, spec_z, prod)
     for k, out in enumerate(outs):
-        out[:rows] = dot(prod[me ^ k], back[...]).astype(BF16)
-    for out, w in zip(outs[1:], (w1, w2, w3)):
-        out[rows:] = w[...]
-
-
-def sum_kernel(h0, h1, h2, h3, after, out, sent):
+        out[...] = dot(prod[me ^ k], back[...]).astype(BF16)
+
+
+def hidden_kernel(rows, w0, w1, w2, w3, decay, mix, after, filt_out, hidden, sent):
     del after
-    total = (h0[...] + h1[...].astype(F32)) + (h2[...].astype(F32) + h3[...].astype(F32))
-    out[...] = total
+    me = lax.axis_index("seq")
+    total = None
+    for k, w in enumerate((w0, w1, w2, w3)):
+        values = w[...].astype(F32)
+        filt_out[me ^ k] = values
+        windowed = values * decay[me ^ k]
+        high = windowed.astype(BF16)
+        low = (windowed - high.astype(F32)).astype(BF16)
+        weight = mix[:, pl.ds(pl.multiple_of((me ^ k) * rows, rows), rows)]
+        term = dot(weight, high) + dot(weight, low)
+        total = term if total is None else total + term
+    hidden[...] = total
     sent[...] = total.astype(BF16)
 
 
-def unpack_kernel(rows, w0, v0, r1, r2, r3, filt_out, in_out):
-    me = lax.axis_index("seq")
-    filt_out[me] = w0[...]
-    in_out[me] = v0[...]
-    for k, r in enumerate((r1, r2, r3), 1):
-        in_out[me ^ k] = r[:rows]
-        filt_out[me ^ k] = r[rows:].astype(F32)
+def final_kernel(v0, v1, v2, v3, pair, *refs):
+    others, (in_out, hidden_out) = refs[:-2], refs[-2:]
+    me = lax.axis_index("seq")
+    for k, v in enumerate((v0, v1, v2, v3)):
+        in_out[me ^ k] = v[...]
+    hidden = pair[...]
+    for other in others:
+        hidden = hidden + other[...].astype(F32)
+    hidden_out[...] = hidden
 
 
 def body_four(channel_axis, inputs, grad_out, filt, rates, mix_weight):
@@ -124,7 +132,7 @@
     shape = jax.ShapeDtypeStruct
     vmem = pl.BlockSpec(memory_space=pltpu.VMEM)
     params = pltpu.CompilerParams(vmem_limit_bytes=8 * 1024 * 1024)
-    small = pltpu.CompilerParams(vmem_limit_bytes=2 * 1024 * 1024)
+    small = pltpu.CompilerParams(vmem_limit_bytes=4 * 1024 * 1024)
     cost = pl.CostEstimate(flops=1000, bytes_accessed=1000, transcendentals=0)
     scratch = [
         pltpu.VMEM((4, rows, 2 * block), F32),
@@ -137,57 +145,61 @@
     parts = [lax.dynamic_index_in_dim(arrays, me ^ k, 0, keepdims=False) for k in range(4)]
     slots = [p[:2].reshape(2 * rows, block) for p in parts]
     slots_f = [p[2] for p in parts]
+    space = pl.BlockSpec(memory_space=pl.ANY)
+    decay, slots_f[1] = pl.pallas_call(
+        functools.partial(window_kernel, rows, block, total),
+        out_shape=[shape((4, rows, block), F32), shape((rows, block), BF16)],
+        in_specs=[vmem, space],
+        out_specs=[vmem, space],
+        input_output_aliases={1: 1},
+        compiler_params=small,
+        cost_estimate=cost,
+    )(rates.reshape(1, channels), slots_f[1])
     slots = slots[:1] + [xor_permute(slots[k], "seq", 4, k) for k in (1, 2, 3)]
     slots_f = slots_f[:1] + [xor_permute(slots_f[k], "seq", 4, k) for k in (1, 2, 3)]
 
     made = pl.pallas_call(
-        functools.partial(filter_kernel, rows, block, total),
-        out_shape=[shape((rows, block), F32)]
-        + [shape((rows, block), BF16)] * 3
-        + [shape((hidden, block), F32)]
-        + [shape((hidden, block), BF16)] * 3,
-        in_specs=[vmem] * 8,
-        out_specs=[vmem] * 8,
-        scratch_shapes=scratch,
-        compiler_params=params,
-        cost_estimate=cost,
-    )(*slots, forward, back, rates.reshape(1, channels), mix_weight.T)
-
-    got_hidden = [xor_permute(made[4 + k], "seq", 4, k) for k in (1, 2, 3)]
-
-    made_in = pl.pallas_call(
-        functools.partial(input_kernel, rows, block),
-        out_shape=[shape((rows, block), BF16)] + [shape((2 * rows, block), BF16)] * 3,
-        in_specs=[vmem] * 13,
+        functools.partial(filter_kernel, rows),
+        out_shape=[shape((rows, block), F32)] + [shape((rows, block), BF16)] * 3,
+        in_specs=[vmem] * 6,
         out_specs=[vmem] * 4,
         scratch_shapes=scratch,
         compiler_params=params,
         cost_estimate=cost,
-    )(*slots, *slots_f, *made[1:4], forward, back)
-    got = [xor_permute(made_in[k], "seq", 4, k) for k in (1, 2, 3)]
-
-    partial, partial_sent = pl.pallas_call(
-        sum_kernel,
-        out_shape=[shape((hidden, block), F32), shape((hidden, block), BF16)],
-        in_specs=[vmem] * 4 + [pl.BlockSpec(memory_space=pl.ANY)],
+    )(*slots, forward, back)
+    got = [xor_permute(made[k], "seq", 4, k) for k in (1, 2, 3)]
+
+    made_in = pl.pallas_call(
+        functools.partial(input_kernel, rows),
+        out_shape=[shape((rows, block), BF16)] * 4,
+        in_specs=[vmem] * 10,
+        out_specs=[vmem] * 4,
+        scratch_shapes=scratch,
+        compiler_params=params,
+        cost_estimate=cost,
+    )(*slots, *slots_f, forward, back)
+    got_in = [xor_permute(made_in[k], "seq", 4, k) for k in (1, 2, 3)]
+
+    grad_filt, partial, partial_sent = pl.pallas_call(
+        functools.partial(hidden_kernel, rows),
+        out_shape=[shape((4, rows, block), F32), shape((hidden, block), F32), shape((hidden, block), BF16)],
+        in_specs=[vmem] * 6 + [space],
+        out_specs=[vmem] * 3,
+        compiler_params=small,
+        cost_estimate=cost,
+    )(made[0], *got, decay, mix_weight.T, made_in[1])
+    pair = partial + xor_permute(partial_sent, "chan", channel_axis, 1).astype(F32)
+    pair_sent = pair.astype(BF16)
+    others = [xor_permute(pair_sent, "chan", channel_axis, k) for k in range(2, channel_axis, 2)]
+
+    grad_in, grad_hidden = pl.pallas_call(
+        final_kernel,
+        out_shape=[shape((4, rows, block), BF16), shape((hidden, block), F32)],
+        in_specs=[vmem] * (5 + len(others)),
         out_specs=[vmem] * 2,
         compiler_params=small,
         cost_estimate=cost,
-    )(made[4], *got_hidden, made_in[1])
-    pair = partial + xor_permute(partial_sent, "chan", channel_axis, 1).astype(F32)
-    pair_sent = pair.astype(BF16)
-    grad_hidden = pair
-    for k in range(2, channel_axis, 2):
-        grad_hidden = grad_hidden + xor_permute(pair_sent, "chan", channel_axis, k).astype(F32)
-
-    grad_filt, grad_in = pl.pallas_call(
-        functools.partial(unpack_kernel, rows),
-        out_shape=[shape((4, rows, block), F32), shape((4, rows, block), BF16)],
-        in_specs=[vmem] * 5,
-        out_specs=[vmem] * 2,
-        compiler_params=small,
-        cost_estimate=cost,
-    )(made[0], made_in[0], *got)
+    )(made_in[0], *got_in, pair, *others)
     return grad_in.reshape(channels, block), grad_filt.reshape(channels, block), grad_hidden
 
 

time: 39.9 us -> 37.4 us (0.937)
  waiting for transfers between devices: 11.3 us -> 8.97 us
  other arithmetic: 1.86 us -> 1.21 us
  starting transfers between devices: 21 us -> 21.4 us
    ppermute x16, waiting for transfers between devices: 11.3 us -> 8.97 us  [xor_permute(): return lax.ppermute(value, axis, [(j, j ^ k) for j in range(size)])]
    add x1 -> x0, other arithmetic: 0.65 us -> none  [body_four(): grad_hidden + xor_permute(pair_sent, 'chan', channel_axis, k).astype(F32)]
    pallas_call x4 -> x5, Pallas kernels: 4.08 us -> 4.16 us  [the longest x1 1.17 us: body_four(): pl.pallas_call(functools.partial(input_kernel, rows), out_shape=[shape((r...]
  transfers between devices with their start and end apart: 16 -> 16, of which waited for: 8 -> 6; matrix products, arithmetic and copies ran while one was open for 2% -> 0% of each run, Pallas kernels for 8% -> 7%
where the time goes in v2:
time: 37.4 us; the launch traced here: 37.2 us
  starting transfers between devices  21.4 us (57%)
  waiting for transfers between devices  8.97 us (24%)
  Pallas kernels  4.16 us (11%)
  other arithmetic  1.21 us (3%)
  local copies, waits for them, and re-layouts  0.81 us (2%)
  between operations  0.73 us (2%)
    ppermute x16, starting transfers between devices, xor_permute(): return lax.ppermute(value, axis, [(j, j ^ k) for j in range(size)])  21.4 us
    ppermute x16, waiting for transfers between devices, xor_permute(): return lax.ppermute(value, axis, [(j, j ^ k) for j in range(size)])  8.97 us
    another operation x1, other arithmetic, body_four(): jnp.stack([value.reshape(4, rows, block) for value in (grad_out, inputs,...  1.2 us
    pallas_call x1, Pallas kernels, body_four(): pl.pallas_call(functools.partial(input_kernel, rows), out_shape=[shape((r...  1.17 us
    pallas_call x1, Pallas kernels, body_four(): pl.pallas_call(functools.partial(filter_kernel, rows), out_shape=[shape((...  1.17 us
    pallas_call x1, Pallas kernels, body_four(): pl.pallas_call(functools.partial(hidden_kernel, rows), out_shape=[shape((...  0.93 us
  transfers between devices with their start and end apart: 16, of which 6 were waited for; matrix products, arithmetic and copies ran while one was open for 0% of the time, Pallas kernels for 7%

profile of v2, /device:TPU:0, one launch (start us, length us, event | category | flops | bytes accessed | tf_op | source)
XLA Modules:
  0.0 37.2 jit_solution(2587526106980839182)
XLA Ops:
  0.7 1.2 %pad_maximum_fusion = bf16[4,3,128,256]{3,2,1,0:T(8,128)(2,1)S(1)} fusion(bf16[4,1,128,256]{3,2,1,0:T(8,128)(2,1)} %bitcast.23, bf16[4,1,128,256]{3,2,1,0:T(8,128)(2,1)} %bitcast.24, bf16[4,1,128,256]{3,2,1,0:T(8,128)(2,1)} %bitcast.25), kind=kLoop, calls=%fused_computation | loop fusion | flops 786432 | bytes 1572864 | tf_op jit(solution)/shard_map/stack | solution.py:144
  1.9 3.0 %collective-permute-start = (bf16[256,256]{1,0:T(8,128)(2,1)S(1)}, bf16[256,256]{1,0:T(8,128)(2,1)S(1)}, u32[]{:S(2)}, u32[]{:S(2)}) collective-permute-start(bf16[256,256]{1,0:T(8,128)(2,1)S(1)} %bitcast.28), channel_id=1, source_target_pairs={{0,8},{8,0},{16,24},{24,16},{1,9},{9,1},{17,25},{25,17},{2,10},{10... | collective-permute-start | bytes 393224 | tf_op jit(solution)/shard_map/ppermute | solution.py:29
  4.9 1.5 %collective-permute-start.1 = (bf16[256,256]{1,0:T(8,128)(2,1)S(1)}, bf16[256,256]{1,0:T(8,128)(2,1)S(1)}, u32[]{:S(2)}, u32[]{:S(2)}) collective-permute-start(bf16[256,256]{1,0:T(8,128)(2,1)S(1)} %bitcast.27), channel_id=1, source_target_pairs={{0,16},{8,24},{16,0},{24,8},{1,17},{9,25},{17,1},{25,9},{2,18},{10... | collective-permute-start | bytes 393224 | tf_op jit(solution)/shard_map/ppermute | solution.py:29
  6.4 0.0 collective-permute-start.2
  6.5 0.0 copy-start
  6.5 0.0 copy-start.1
  6.5 0.0 copy-start.3
  6.5 0.7 %copy-done.3 = f32[512]{0:T(512)S(1)} copy-done((f32[512]{0:T(512)S(1)}, f32[512]{0:T(512)}, u32[]{:S(2)}) %copy-start.3) | copy-done | bytes 2072
  7.2 0.1 shard_map.94
  7.4 2.0 %collective-permute-start.3 = (bf16[128,256]{1,0:T(8,128)(2,1)S(1)}, bf16[128,256]{1,0:T(8,128)(2,1)S(1)}, u32[]{:S(2)}, u32[]{:S(2)}) collective-permute-start(bf16[128,256]{1,0:T(8,128)(2,1)S(1)} %get-tuple-element.18), channel_id=1, source_target_pairs={{0,8},{8,0},{16,24},{24,16},{1,9},{9,1},{17,25},{25,17},{2,10},{10... | collective-permute-start | bytes 196616 | tf_op jit(solution)/shard_map/ppermute | solution.py:29
  9.4 1.5 %collective-permute-start.4 = (bf16[128,256]{1,0:T(8,128)(2,1)S(1)}, bf16[128,256]{1,0:T(8,128)(2,1)S(1)}, u32[]{:S(2)}, u32[]{:S(2)}) collective-permute-start(bf16[128,256]{1,0:T(8,128)(2,1)S(1)} %get-tuple-element.36), channel_id=1, source_target_pairs={{0,16},{8,24},{16,0},{24,8},{1,17},{9,25},{17,1},{25,9},{2,18},{10... | collective-permute-start | bytes 196616 | tf_op jit(solution)/shard_map/ppermute | solution.py:29
  10.9 0.0 collective-permute-done.s1
  10.9 1.3 %collective-permute-start.5 = (bf16[128,256]{1,0:T(8,128)(2,1)S(1)}, bf16[128,256]{1,0:T(8,128)(2,1)S(1)}, u32[]{:S(2)}, u32[]{:S(2)}) collective-permute-start(bf16[128,256]{1,0:T(8,128)(2,1)S(1)} %get-tuple-element.35), channel_id=1, source_target_pairs={{0,24},{8,16},{16,8},{24,0},{1,25},{9,17},{17,9},{25,1},{2,26},{10... | collective-permute-start | bytes 196616 | tf_op jit(solution)/shard_map/ppermute | solution.py:29
  12.3 0.9 %collective-permute-done.1.s2 = bf16[256,256]{1,0:T(8,128)(2,1)S(1)} collective-permute-done((bf16[256,256]{1,0:T(8,128)(2,1)S(1)}, bf16[256,256]{1,0:T(8,128)(2,1)S(1)}, u32[]{:S(2)}, u32[]{:S(2)}) %collective-permute-start.1) | collective-permute-done | bytes 131104 | tf_op jit(solution)/shard_map/ppermute | solution.py:29
  13.1 0.4 collective-permute-done.2.s3
  13.5 0.0 copy-done
  13.5 0.0 copy-done.1
  13.5 1.2 %shard_map.96 = (f32[128,256]{1,0:T(8,128)S(1)}, bf16[128,256]{1,0:T(8,128)(2,1)S(1)}, bf16[128,256]{1,0:T(8,128)(2,1)S(1)}, bf16[128,256]{1,0:T(8,128)(2,1)S(1)}) custom-call(bf16[256,256]{1,0:T(8,128)(2,1)S(1)} %bitcast.19, bf16[256,256]{1,0:T(8,128)(2,1)S(1)} %collective-permute-done.s1, bf16[256,256]{1,0:T(8,128)(2,1)S(1)} %collective-permute-done.1.s2, ...), custom_call_target="tpu_custom_call" | custom-call | flops 1000 | bytes 1000 | tf_op jit(solution)/shard_map/pallas_call | solution.py:161
  14.7 1.7 %collective-permute-start.9 = (bf16[128,256]{1,0:T(8,128)(2,1)S(1)}, bf16[128,256]{1,0:T(8,128)(2,1)S(1)}, u32[]{:S(2)}, u32[]{:S(2)}) collective-permute-start(bf16[128,256]{1,0:T(8,128)(2,1)S(1)} %get-tuple-element.24), channel_id=1, source_target_pairs={{0,8},{8,0},{16,24},{24,16},{1,9},{9,1},{17,25},{25,17},{2,10},{10... | collective-permute-start | bytes 196616 | tf_op jit(solution)/shard_map/ppermute | solution.py:29
  16.4 0.6 %collective-permute-start.10 = (bf16[128,256]{1,0:T(8,128)(2,1)S(1)}, bf16[128,256]{1,0:T(8,128)(2,1)S(1)}, u32[]{:S(2)}, u32[]{:S(2)}) collective-permute-start(bf16[128,256]{1,0:T(8,128)(2,1)S(1)} %get-tuple-element.25), channel_id=1, source_target_pairs={{0,16},{8,24},{16,0},{24,8},{1,17},{9,25},{17,1},{25,9},{2,18},{10... | collective-permute-start | bytes 196616 | tf_op jit(solution)/shard_map/ppermute | solution.py:29
  16.9 0.0 collective-permute-done.3.f1
  16.9 1.4 %collective-permute-start.11 = (bf16[128,256]{1,0:T(8,128)(2,1)S(1)}, bf16[128,256]{1,0:T(8,128)(2,1)S(1)}, u32[]{:S(2)}, u32[]{:S(2)}) collective-permute-start(bf16[128,256]{1,0:T(8,128)(2,1)S(1)} %get-tuple-element.26), channel_id=1, source_target_pairs={{0,24},{8,16},{16,8},{24,0},{1,25},{9,17},{17,9},{25,1},{2,26},{10... | collective-permute-start | bytes 196616 | tf_op jit(solution)/shard_map/ppermute | solution.py:29
  18.3 0.0 collective-permute-done.4.f2
  18.3 0.0 collective-permute-done.5.f3
  18.3 0.0 copy-start.2
  18.3 1.2 %shard_map.95 = (bf16[128,256]{1,0:T(8,128)(2,1)S(1)}, bf16[128,256]{1,0:T(8,128)(2,1)S(1)}, bf16[128,256]{1,0:T(8,128)(2,1)S(1)}, bf16[128,256]{1,0:T(8,128)(2,1)S(1)}) custom-call(bf16[256,256]{1,0:T(8,128)(2,1)S(1)} %bitcast.20, bf16[256,256]{1,0:T(8,128)(2,1)S(1)} %collective-permute-done.s1, bf16[256,256]{1,0:T(8,128)(2,1)S(1)} %collective-permute-done.1.s2, ...), custom_call_target="tpu_custom_call" | custom-call | flops 1000 | bytes 1000 | tf_op jit(solution)/shard_map/pallas_call | solution.py:172
  19.5 0.0 collective-permute-done.9.w1
  19.5 1.1 %collective-permute-done.10.w2 = bf16[128,256]{1,0:T(8,128)(2,1)S(1)} collective-permute-done((bf16[128,256]{1,0:T(8,128)(2,1)S(1)}, bf16[128,256]{1,0:T(8,128)(2,1)S(1)}, u32[]{:S(2)}, u32[]{:S(2)}) %collective-permute-start.10) | collective-permute-done | bytes 65568 | tf_op jit(solution)/shard_map/ppermute | solution.py:29
  20.6 1.5 %collective-permute-done.11.w3 = bf16[128,256]{1,0:T(8,128)(2,1)S(1)} collective-permute-done((bf16[128,256]{1,0:T(8,128)(2,1)S(1)}, bf16[128,256]{1,0:T(8,128)(2,1)S(1)}, u32[]{:S(2)}, u32[]{:S(2)}) %collective-permute-start.11) | collective-permute-done | bytes 65568 | tf_op jit(solution)/shard_map/ppermute | solution.py:29
  22.1 0.0 copy-done.2
  22.1 0.9 %shard_map.97 = (f32[4,128,256]{2,1,0:T(8,128)}, f32[64,256]{1,0:T(8,128)S(1)}, bf16[64,256]{1,0:T(8,128)(2,1)S(1)}) custom-call(f32[128,256]{1,0:T(8,128)S(1)} %get-tuple-element.23.w0, bf16[128,256]{1,0:T(8,128)(2,1)S(1)} %collective-permute-done.9.w1, bf16[128,256]{1,0:T(8,128)(2,1)S(1)} %collective-permute-done.10.w2, ...), custom_call_target="tpu_custom_call" | custom-call | flops 1000 | bytes 1000 | tf_op jit(solution)/shard_map/pallas_call | solution.py:183
  23.0 0.0 collective-permute-start.12
  23.0 1.9 %collective-permute-start.6 = (bf16[128,256]{1,0:T(8,128)(2,1)S(1)}, bf16[128,256]{1,0:T(8,128)(2,1)S(1)}, u32[]{:S(2)}, u32[]{:S(2)}) collective-permute-start(bf16[128,256]{1,0:T(8,128)(2,1)S(1)} %get-tuple-element.20.after), channel_id=1, source_target_pairs={{0,8},{8,0},{16,24},{24,16},{1,9},{9,1},{17,25},{25,17},{2,10},{10... | collective-permute-start | bytes 196616 | tf_op jit(solution)/shard_map/ppermute | solution.py:29
  25.0 0.0 collective-permute-start.7
  25.0 1.5 %collective-permute-start.8 = (bf16[128,256]{1,0:T(8,128)(2,1)S(1)}, bf16[128,256]{1,0:T(8,128)(2,1)S(1)}, u32[]{:S(2)}, u32[]{:S(2)}) collective-permute-start(bf16[128,256]{1,0:T(8,128)(2,1)S(1)} %get-tuple-element.22), channel_id=1, source_target_pairs={{0,24},{8,16},{16,8},{24,0},{1,25},{9,17},{17,9},{25,1},{2,26},{10... | collective-permute-start | bytes 196616 | tf_op jit(solution)/shard_map/ppermute | solution.py:29
  26.5 0.0 collective-permute-done.12
  26.6 1.6 %collective-permute-start.13 = (bf16[64,256]{1,0:T(8,128)(2,1)S(1)}, bf16[64,256]{1,0:T(8,128)(2,1)S(1)}, u32[]{:S(2)}, u32[]{:S(2)}) collective-permute-start(bf16[64,256]{1,0:T(8,128)(2,1)S(1)} %get-tuple-element.33), channel_id=1, source_target_pairs={{0,2},{1,3},{2,0},{3,1},{4,6},{5,7},{6,4},{7,5},{8,10},{9,11},{10,... | collective-permute-start | bytes 98312 | tf_op jit(solution)/shard_map/ppermute | solution.py:29
  28.2 2.6 %collective-permute-start.14 = (bf16[64,256]{1,0:T(8,128)(2,1)S(1)}, bf16[64,256]{1,0:T(8,128)(2,1)S(1)}, u32[]{:S(2)}, u32[]{:S(2)}) collective-permute-start(bf16[64,256]{1,0:T(8,128)(2,1)S(1)} %get-tuple-element.33), channel_id=1, source_target_pairs={{0,4},{1,5},{2,6},{3,7},{4,0},{5,1},{6,2},{7,3},{8,12},{9,13},{10,... | collective-permute-start | bytes 98312 | tf_op jit(solution)/shard_map/ppermute | solution.py:29
  30.8 0.0 collective-permute-done.6.v1
  30.8 0.6 %collective-permute-start.15 = (bf16[64,256]{1,0:T(8,128)(2,1)S(1)}, bf16[64,256]{1,0:T(8,128)(2,1)S(1)}, u32[]{:S(2)}, u32[]{:S(2)}) collective-permute-start(bf16[64,256]{1,0:T(8,128)(2,1)S(1)} %get-tuple-element.33), channel_id=1, source_target_pairs={{0,6},{1,7},{2,4},{3,5},{4,2},{5,3},{6,0},{7,1},{8,14},{9,15},{10,... | collective-permute-start | bytes 98312 | tf_op jit(solution)/shard_map/ppermute | solution.py:29
  31.4 0.0 collective-permute-done.7.v2
  31.4 0.0 collective-permute-done.8.v3
  31.4 0.0 collective-permute-done.13.refs_0_
  31.4 2.2 %collective-permute-done.14.refs_1_ = bf16[64,256]{1,0:T(8,128)(2,1)S(1)} collective-permute-done((bf16[64,256]{1,0:T(8,128)(2,1)S(1)}, bf16[64,256]{1,0:T(8,128)(2,1)S(1)}, u32[]{:S(2)}, u32[]{:S(2)}) %collective-permute-start.14) | collective-permute-done | bytes 32800 | tf_op jit(solution)/shard_map/ppermute | solution.py:29
  33.6 2.9 %collective-permute-done.15.refs_2_ = bf16[64,256]{1,0:T(8,128)(2,1)S(1)} collective-permute-done((bf16[64,256]{1,0:T(8,128)(2,1)S(1)}, bf16[64,256]{1,0:T(8,128)(2,1)S(1)}, u32[]{:S(2)}, u32[]{:S(2)}) %collective-permute-start.15) | collective-permute-done | bytes 32800 | tf_op jit(solution)/shard_map/ppermute | solution.py:29
  36.5 0.7 %shard_map.98 = (bf16[4,128,256]{2,1,0:T(8,128)(2,1)}, f32[64,256]{1,0:T(8,128)}) custom-call(bf16[128,256]{1,0:T(8,128)(2,1)S(1)} %get-tuple-element.19.v0, bf16[128,256]{1,0:T(8,128)(2,1)S(1)} %collective-permute-done.6.v1, bf16[128,256]{1,0:T(8,128)(2,1)S(1)} %collective-permute-done.7.v2, bf16[128,256]{1,0:T(8,128)(2,1)S(1)} %collective-permute-done.8.v3, ...), custom_call_target="tpu_custom_call" | custom-call | flops 1000 | bytes 1000 | tf_op jit(solution)/shard_map/pallas_call | solution.py:195
  (3 shorter events, 0.1 us)
Async XLA Ops:
  1.9 9.0 %collective-permute-start = (bf16[256,256]{1,0:T(8,128)(2,1)S(1)}, bf16[256,256]{1,0:T(8,128)(2,1)S(1)}, u32[]{:S(2)}, u32[]{:S(2)}) collective-permute-start(bf16[256,256]{1,0:T(8,128)(2,1)S(1)} %bitcast.28), channel_id=1, source_target_pairs={{0,8},{8,0},{16,24},{24,16},{1,9},{9,1},{17,25},{25,17},{2,10},{10... | collective-permute-start | bytes 393224 | tf_op jit(solution)/shard_map/ppermute | solution.py:29
  4.9 8.2 %collective-permute-start.1 = (bf16[256,256]{1,0:T(8,128)(2,1)S(1)}, bf16[256,256]{1,0:T(8,128)(2,1)S(1)}, u32[]{:S(2)}, u32[]{:S(2)}) collective-permute-start(bf16[256,256]{1,0:T(8,128)(2,1)S(1)} %bitcast.27), channel_id=1, source_target_pairs={{0,16},{8,24},{16,0},{24,8},{1,17},{9,25},{17,1},{25,9},{2,18},{10... | collective-permute-start | bytes 393224 | tf_op jit(solution)/shard_map/ppermute | solution.py:29
  6.4 7.1 %collective-permute-start.2 = (bf16[256,256]{1,0:T(8,128)(2,1)S(1)}, bf16[256,256]{1,0:T(8,128)(2,1)S(1)}, u32[]{:S(2)}, u32[]{:S(2)}) collective-permute-start(bf16[256,256]{1,0:T(8,128)(2,1)S(1)} %bitcast.26), channel_id=1, source_target_pairs={{0,24},{8,16},{16,8},{24,0},{1,25},{9,17},{17,9},{25,1},{2,26},{10... | collective-permute-start | bytes 393224 | tf_op jit(solution)/shard_map/ppermute | solution.py:29
  6.5 7.0 %copy-start = (bf16[256,512]{1,0:T(8,128)(2,1)S(1)}, bf16[256,512]{1,0:T(8,128)(2,1)}, u32[]{:S(2)}) copy-start(bf16[256,512]{1,0:T(8,128)(2,1)} %constant.27.clone.table) | copy-start | bytes 786436
  6.5 7.0 %copy-start.1 = (bf16[512,256]{1,0:T(8,128)(2,1)S(1)}, bf16[512,256]{1,0:T(8,128)(2,1)}, u32[]{:S(2)}) copy-start(bf16[512,256]{1,0:T(8,128)(2,1)} %constant.28.clone.back) | copy-start | bytes 786436
  6.5 0.7 %copy-start.3 = (f32[512]{0:T(512)S(1)}, f32[512]{0:T(512)}, u32[]{:S(2)}) copy-start(f32[512]{0:T(512)} %param.10) | copy-start | bytes 6148
  7.4 9.6 %collective-permute-start.3 = (bf16[128,256]{1,0:T(8,128)(2,1)S(1)}, bf16[128,256]{1,0:T(8,128)(2,1)S(1)}, u32[]{:S(2)}, u32[]{:S(2)}) collective-permute-start(bf16[128,256]{1,0:T(8,128)(2,1)S(1)} %get-tuple-element.18), channel_id=1, source_target_pairs={{0,8},{8,0},{16,24},{24,16},{1,9},{9,1},{17,25},{25,17},{2,10},{10... | collective-permute-start | bytes 196616 | tf_op jit(solution)/shard_map/ppermute | solution.py:29
  9.4 8.9 %collective-permute-start.4 = (bf16[128,256]{1,0:T(8,128)(2,1)S(1)}, bf16[128,256]{1,0:T(8,128)(2,1)S(1)}, u32[]{:S(2)}, u32[]{:S(2)}) collective-permute-start(bf16[128,256]{1,0:T(8,128)(2,1)S(1)} %get-tuple-element.36), channel_id=1, source_target_pairs={{0,16},{8,24},{16,0},{24,8},{1,17},{9,25},{17,1},{25,9},{2,18},{10... | collective-permute-start | bytes 196616 | tf_op jit(solution)/shard_map/ppermute | solution.py:29
  10.9 7.4 %collective-permute-start.5 = (bf16[128,256]{1,0:T(8,128)(2,1)S(1)}, bf16[128,256]{1,0:T(8,128)(2,1)S(1)}, u32[]{:S(2)}, u32[]{:S(2)}) collective-permute-start(bf16[128,256]{1,0:T(8,128)(2,1)S(1)} %get-tuple-element.35), channel_id=1, source_target_pairs={{0,24},{8,16},{16,8},{24,0},{1,25},{9,17},{17,9},{25,1},{2,26},{10... | collective-permute-start | bytes 196616 | tf_op jit(solution)/shard_map/ppermute | solution.py:29
  14.7 4.9 %collective-permute-start.9 = (bf16[128,256]{1,0:T(8,128)(2,1)S(1)}, bf16[128,256]{1,0:T(8,128)(2,1)S(1)}, u32[]{:S(2)}, u32[]{:S(2)}) collective-permute-start(bf16[128,256]{1,0:T(8,128)(2,1)S(1)} %get-tuple-element.24), channel_id=1, source_target_pairs={{0,8},{8,0},{16,24},{24,16},{1,9},{9,1},{17,25},{25,17},{2,10},{10... | collective-permute-start | bytes 196616 | tf_op jit(solution)/shard_map/ppermute | solution.py:29
  16.4 4.3 %collective-permute-start.10 = (bf16[128,256]{1,0:T(8,128)(2,1)S(1)}, bf16[128,256]{1,0:T(8,128)(2,1)S(1)}, u32[]{:S(2)}, u32[]{:S(2)}) collective-permute-start(bf16[128,256]{1,0:T(8,128)(2,1)S(1)} %get-tuple-element.25), channel_id=1, source_target_pairs={{0,16},{8,24},{16,0},{24,8},{1,17},{9,25},{17,1},{25,9},{2,18},{10... | collective-permute-start | bytes 196616 | tf_op jit(solution)/shard_map/ppermute | solution.py:29
  16.9 5.2 %collective-permute-start.11 = (bf16[128,256]{1,0:T(8,128)(2,1)S(1)}, bf16[128,256]{1,0:T(8,128)(2,1)S(1)}, u32[]{:S(2)}, u32[]{:S(2)}) collective-permute-start(bf16[128,256]{1,0:T(8,128)(2,1)S(1)} %get-tuple-element.26), channel_id=1, source_target_pairs={{0,24},{8,16},{16,8},{24,0},{1,25},{9,17},{17,9},{25,1},{2,26},{10... | collective-permute-start | bytes 196616 | tf_op jit(solution)/shard_map/ppermute | solution.py:29
  18.3 3.8 %copy-start.2 = (bf16[512,64]{0,1:T(8,128)(2,1)S(1)}, bf16[512,64]{0,1:T(8,128)(2,1)}, u32[]{:S(2)}) copy-start(bf16[512,64]{0,1:T(8,128)(2,1)} %param.11) | copy-start | bytes 196612
  23.0 3.5 %collective-permute-start.12 = (bf16[64,256]{1,0:T(8,128)(2,1)S(1)}, bf16[64,256]{1,0:T(8,128)(2,1)S(1)}, u32[]{:S(2)}, u32[]{:S(2)}) collective-permute-start(bf16[64,256]{1,0:T(8,128)(2,1)S(1)} %get-tuple-element.29), channel_id=1, source_target_pairs={{0,1},{1,0},{2,3},{3,2},{4,5},{5,4},{6,7},{7,6},{8,9},{9,8},{10,11... | collective-permute-start | bytes 98312 | tf_op jit(solution)/shard_map/ppermute | solution.py:29
  23.0 7.7 %collective-permute-start.6 = (bf16[128,256]{1,0:T(8,128)(2,1)S(1)}, bf16[128,256]{1,0:T(8,128)(2,1)S(1)}, u32[]{:S(2)}, u32[]{:S(2)}) collective-permute-start(bf16[128,256]{1,0:T(8,128)(2,1)S(1)} %get-tuple-element.20.after), channel_id=1, source_target_pairs={{0,8},{8,0},{16,24},{24,16},{1,9},{9,1},{17,25},{25,17},{2,10},{10... | collective-permute-start | bytes 196616 | tf_op jit(solution)/shard_map/ppermute | solution.py:29
  25.0 6.4 %collective-permute-start.7 = (bf16[128,256]{1,0:T(8,128)(2,1)S(1)}, bf16[128,256]{1,0:T(8,128)(2,1)S(1)}, u32[]{:S(2)}, u32[]{:S(2)}) collective-permute-start(bf16[128,256]{1,0:T(8,128)(2,1)S(1)} %get-tuple-element.21), channel_id=1, source_target_pairs={{0,16},{8,24},{16,0},{24,8},{1,17},{9,25},{17,1},{25,9},{2,18},{10... | collective-permute-start | bytes 196616 | tf_op jit(solution)/shard_map/ppermute | solution.py:29
  25.0 6.4 %collective-permute-start.8 = (bf16[128,256]{1,0:T(8,128)(2,1)S(1)}, bf16[128,256]{1,0:T(8,128)(2,1)S(1)}, u32[]{:S(2)}, u32[]{:S(2)}) collective-permute-start(bf16[128,256]{1,0:T(8,128)(2,1)S(1)} %get-tuple-element.22), channel_id=1, source_target_pairs={{0,24},{8,16},{16,8},{24,0},{1,25},{9,17},{17,9},{25,1},{2,26},{10... | collective-permute-start | bytes 196616 | tf_op jit(solution)/shard_map/ppermute | solution.py:29
  26.6 4.8 %collective-permute-start.13 = (bf16[64,256]{1,0:T(8,128)(2,1)S(1)}, bf16[64,256]{1,0:T(8,128)(2,1)S(1)}, u32[]{:S(2)}, u32[]{:S(2)}) collective-permute-start(bf16[64,256]{1,0:T(8,128)(2,1)S(1)} %get-tuple-element.33), channel_id=1, source_target_pairs={{0,2},{1,3},{2,0},{3,1},{4,6},{5,7},{6,4},{7,5},{8,10},{9,11},{10,... | collective-permute-start | bytes 98312 | tf_op jit(solution)/shard_map/ppermute | solution.py:29
  28.2 5.4 %collective-permute-start.14 = (bf16[64,256]{1,0:T(8,128)(2,1)S(1)}, bf16[64,256]{1,0:T(8,128)(2,1)S(1)}, u32[]{:S(2)}, u32[]{:S(2)}) collective-permute-start(bf16[64,256]{1,0:T(8,128)(2,1)S(1)} %get-tuple-element.33), channel_id=1, source_target_pairs={{0,4},{1,5},{2,6},{3,7},{4,0},{5,1},{6,2},{7,3},{8,12},{9,13},{10,... | collective-permute-start | bytes 98312 | tf_op jit(solution)/shard_map/ppermute | solution.py:29
  30.8 5.7 %collective-permute-start.15 = (bf16[64,256]{1,0:T(8,128)(2,1)S(1)}, bf16[64,256]{1,0:T(8,128)(2,1)S(1)}, u32[]{:S(2)}, u32[]{:S(2)}) collective-permute-start(bf16[64,256]{1,0:T(8,128)(2,1)S(1)} %get-tuple-element.33), channel_id=1, source_target_pairs={{0,6},{1,7},{2,4},{3,5},{4,2},{5,3},{6,0},{7,1},{8,14},{9,15},{10,... | collective-permute-start | bytes 98312 | tf_op jit(solution)/shard_map/ppermute | solution.py:29

commit v3 on v2

--- a/solution.py
+++ b/solution.py
@@ -92,17 +92,15 @@
         spec_z[me ^ k] = dot(f[...], table[...])
     correlate(rows, table.shape[0], spec_g, spec_z, prod)
     for k, out in enumerate(outs):
-        out[...] = dot(prod[me ^ k], back[...]).astype(BF16)
-
-
-def hidden_kernel(rows, w0, w1, w2, w3, decay, mix, after, filt_out, hidden, sent):
+        out[...] = dot(prod[me ^ k], back[...])
+
+
+def hidden_kernel(rows, w0, w1, w2, w3, decay, mix, after, hidden, sent):
     del after
     me = lax.axis_index("seq")
     total = None
     for k, w in enumerate((w0, w1, w2, w3)):
-        values = w[...].astype(F32)
-        filt_out[me ^ k] = values
-        windowed = values * decay[me ^ k]
+        windowed = w[...].astype(F32) * decay[me ^ k]
         high = windowed.astype(BF16)
         low = (windowed - high.astype(F32)).astype(BF16)
         weight = mix[:, pl.ds(pl.multiple_of((me ^ k) * rows, rows), rows)]
@@ -112,15 +110,32 @@
     sent[...] = total.astype(BF16)
 
 
-def final_kernel(v0, v1, v2, v3, pair, *refs):
-    others, (in_out, hidden_out) = refs[:-2], refs[-2:]
+def unpack_kernel(w0, w1, w2, w3, filt_out, token):
+    me = lax.axis_index("seq")
+    for k, w in enumerate((w0, w1, w2, w3)):
+        filt_out[me ^ k] = w[...].astype(F32)
+    token[...] = jnp.zeros_like(token)
+
+
+def pair_kernel(own, other, out, sent):
+    total = own[...] + other[...].astype(F32)
+    out[...] = total
+    sent[...] = total.astype(BF16)
+
+
+def sum_kernel(pair, first, second, token, out, sent):
+    del token
+    lead = lax.axis_index("chan") % 2 == 1
+    total = first[...].astype(F32) + jnp.where(lead, second[...].astype(F32), pair[...])
+    out[...] = total
+    sent[...] = total.astype(BF16)
+
+
+def final_kernel(v0, v1, v2, v3, own, other, in_out, hidden_out):
     me = lax.axis_index("seq")
     for k, v in enumerate((v0, v1, v2, v3)):
-        in_out[me ^ k] = v[...]
-    hidden = pair[...]
-    for other in others:
-        hidden = hidden + other[...].astype(F32)
-    hidden_out[...] = hidden
+        in_out[me ^ k] = v[...].astype(BF16)
+    hidden_out[...] = own[...] + other[...].astype(F32)
 
 
 def body_four(channel_axis, inputs, grad_out, filt, rates, mix_weight):
@@ -141,10 +156,9 @@
     ]
 
     me = lax.axis_index("seq")
-    arrays = jnp.stack([value.reshape(4, rows, block) for value in (grad_out, inputs, filt)], 1)
-    parts = [lax.dynamic_index_in_dim(arrays, me ^ k, 0, keepdims=False) for k in range(4)]
-    slots = [p[:2].reshape(2 * rows, block) for p in parts]
-    slots_f = [p[2] for p in parts]
+    arrays = jnp.stack([value.reshape(4, rows, block) for value in (grad_out, inputs)], 1)
+    slots = [lax.dynamic_index_in_dim(arrays, me ^ k, 0, keepdims=False).reshape(2 * rows, block) for k in range(4)]
+    slots_f = [lax.dynamic_index_in_dim(filt.reshape(4, rows, block), me ^ k, 0, keepdims=False) for k in range(4)]
     space = pl.BlockSpec(memory_space=pl.ANY)
     decay, slots_f[1] = pl.pallas_call(
         functools.partial(window_kernel, rows, block, total),
@@ -171,7 +185,7 @@
 
     made_in = pl.pallas_call(
         functools.partial(input_kernel, rows),
-        out_shape=[shape((rows, block), BF16)] * 4,
+        out_shape=[shape((rows, block), F32)] * 4,
         in_specs=[vmem] * 10,
         out_specs=[vmem] * 4,
         scratch_shapes=scratch,
@@ -180,26 +194,50 @@
     )(*slots, *slots_f, forward, back)
     got_in = [xor_permute(made_in[k], "seq", 4, k) for k in (1, 2, 3)]
 
-    grad_filt, partial, partial_sent = pl.pallas_call(
+    partial, partial_sent = pl.pallas_call(
         functools.partial(hidden_kernel, rows),
-        out_shape=[shape((4, rows, block), F32), shape((hidden, block), F32), shape((hidden, block), BF16)],
+        out_shape=[shape((hidden, block), F32), shape((hidden, block), BF16)],
         in_specs=[vmem] * 6 + [space],
-        out_specs=[vmem] * 3,
+        out_specs=[vmem] * 2,
         compiler_params=small,
         cost_estimate=cost,
     )(made[0], *got, decay, mix_weight.T, made_in[1])
-    pair = partial + xor_permute(partial_sent, "chan", channel_axis, 1).astype(F32)
-    pair_sent = pair.astype(BF16)
-    others = [xor_permute(pair_sent, "chan", channel_axis, k) for k in range(2, channel_axis, 2)]
+    grad_filt, token = pl.pallas_call(
+        unpack_kernel,
+        out_shape=[shape((4, rows, block), F32), shape((8, 128), F32)],
+        in_specs=[vmem] * 4,
+        out_specs=[vmem] * 2,
+        compiler_params=small,
+        cost_estimate=cost,
+    )(made[0], *got)
+    pair, pair_sent = pl.pallas_call(
+        pair_kernel,
+        out_shape=[shape((hidden, block), F32), shape((hidden, block), BF16)],
+        in_specs=[vmem] * 2,
+        out_specs=[vmem] * 2,
+        compiler_params=small,
+        cost_estimate=cost,
+    )(partial, xor_permute(partial_sent, "chan", channel_axis, 1))
+    first = lax.ppermute(pair_sent, "chan", [(c, c ^ (4 if c % 2 else 6)) for c in range(channel_axis)])
+    second = lax.ppermute(pair_sent, "chan", [(c, c ^ (2 if c % 2 else 0)) for c in range(channel_axis)])
+    half_sum, half_sent = pl.pallas_call(
+        sum_kernel,
+        out_shape=[shape((hidden, block), F32), shape((hidden, block), BF16)],
+        in_specs=[vmem] * 3 + [space],
+        out_specs=[vmem] * 2,
+        compiler_params=small,
+        cost_estimate=cost,
+    )(pair, first, second, token)
+    other_half = xor_permute(half_sent, "chan", channel_axis, 1)
 
     grad_in, grad_hidden = pl.pallas_call(
         final_kernel,
         out_shape=[shape((4, rows, block), BF16), shape((hidden, block), F32)],
-        in_specs=[vmem] * (5 + len(others)),
-        out_specs=[vmem] * 2,
-        compiler_params=small,
-        cost_estimate=cost,
-    )(made_in[0], *got_in, pair, *others)
+        in_specs=[vmem] * 6,
+        out_specs=[vmem] * 2,
+        compiler_params=small,
+        cost_estimate=cost,
+    )(made_in[0], *got_in, half_sum, other_half)
     return grad_in.reshape(channels, block), grad_filt.reshape(channels, block), grad_hidden
 
 

time: 37.4 us -> 33.6 us (0.90)
  waiting for transfers between devices: 8.97 us -> 3.92 us
  starting transfers between devices: 21.4 us -> 22.5 us
    ppermute x16 -> x14, waiting for transfers between devices: 8.97 us -> 3.29 us  [xor_permute(): return lax.ppermute(value, axis, [(j, j ^ k) for j in range(size)])]
    ppermute x0 -> x2, starting transfers between devices: none -> 4.31 us  [the longest x1 3.66 us: body_four(): lax.ppermute(pair_sent, 'chan', [(c, c ^ (4 if c % 2 else 6)) for c in ra...]
    ppermute x16 -> x14, starting transfers between devices: 21.4 us -> 18.2 us  [xor_permute(): return lax.ppermute(value, axis, [(j, j ^ k) for j in range(size)])]
    pallas_call x0 -> x3, Pallas kernels: none -> 0.87 us  [the longest x1 0.84 us: body_four(): pl.pallas_call(unpack_kernel, out_shape=[shape((4, rows, block), F32), sh...]
    pallas_call x1, Pallas kernels: 0.93 us -> 0.27 us  [body_four(): pl.pallas_call(functools.partial(hidden_kernel, rows), out_shape=[shape((...]
    ppermute x0 -> x2, waiting for transfers between devices: none -> 0.62 us  [the longest x1 0.62 us: body_four(): lax.ppermute(pair_sent, 'chan', [(c, c ^ (4 if c % 2 else 6)) for c in ra...]
  transfers between devices with their start and end apart: 16 -> 16, of which waited for: 6 -> 5; matrix products, arithmetic and copies ran while one was open for 0% -> 0% of each run, Pallas kernels for 7% -> 11%
where the time goes in v3:
time: 33.6 us; the launch traced here: 33.5 us
  starting transfers between devices  22.5 us (67%)
  Pallas kernels  4.39 us (13%)
  waiting for transfers between devices  3.92 us (12%)
  other arithmetic  1.16 us (3%)
  local copies, waits for them, and re-layouts  0.76 us (2%)
  between operations  0.76 us (2%)
    ppermute x14, starting transfers between devices, xor_permute(): return lax.ppermute(value, axis, [(j, j ^ k) for j in range(size)])  18.2 us
    ppermute x1, starting transfers between devices, body_four(): lax.ppermute(pair_sent, 'chan', [(c, c ^ (4 if c % 2 else 6)) for c in ra...  3.66 us
    ppermute x14, waiting for transfers between devices, xor_permute(): return lax.ppermute(value, axis, [(j, j ^ k) for j in range(size)])  3.29 us
    pallas_call x1, Pallas kernels, body_four(): pl.pallas_call(functools.partial(input_kernel, rows), out_shape=[shape((r...  1.18 us
    pallas_call x1, Pallas kernels, body_four(): pl.pallas_call(functools.partial(filter_kernel, rows), out_shape=[shape((...  1.17 us
    another operation x1, other arithmetic, body_four(): jnp.stack([value.reshape(4, rows, block) for value in (grad_out, inputs)]...  1.16 us
    pallas_call x1, Pallas kernels, body_four(): pl.pallas_call(unpack_kernel, out_shape=[shape((4, rows, block), F32), sh...  0.84 us
    pallas_call x1, Pallas kernels, body_four(): pl.pallas_call(final_kernel, out_shape=[shape((4, rows, block), BF16), sh...  0.75 us
  transfers between devices with their start and end apart: 16, of which 5 were waited for; matrix products, arithmetic and copies ran while one was open for 0% of the time, Pallas kernels for 11%

profile of v3, /device:TPU:0, one launch (start us, length us, event | category | flops | bytes accessed | tf_op | source)
XLA Modules:
  0.0 33.5 jit_solution(565815027408361186)
XLA Ops:
  0.7 0.0 copy-start.4
  0.7 1.2 %fusion = (bf16[1,2,128,256]{3,2,1,0:T(8,128)(2,1)S(1)}, bf16[1,2,128,256]{3,2,1,0:T(8,128)(2,1)S(1)}, bf16[1,2,128,256]{3,2,1,0:T(8,128)(2,1)S(1)}, bf16[1,2,128,256]{3,2,1,0:T(8,128)(2,1)S(1)}) fusion(s32[]{:T(128)S(6)} %select_n.21, bf16[4,1,128,256]{3,2,1,0:T(8,128)(2,1)} %bitcast.28, bf16[4,1,128,256]{3,2,1,0:T(8,128)(2,1)} %bitcast.29, ...), kind=kLoop, calls=%fused_computation.8 | loop fusion | flops 262144 | bytes 1048592 | tf_op jit(solution)/shard_map/stack | solution.py:159
  1.8 3.0 %collective-permute-start = (bf16[256,256]{1,0:T(8,128)(2,1)S(1)}, bf16[256,256]{1,0:T(8,128)(2,1)S(1)}, u32[]{:S(2)}, u32[]{:S(2)}) collective-permute-start(bf16[256,256]{1,0:T(8,128)(2,1)S(1)} %bitcast.32), channel_id=1, source_target_pairs={{0,8},{8,0},{16,24},{24,16},{1,9},{9,1},{17,25},{25,17},{2,10},{10... | collective-permute-start | bytes 393224 | tf_op jit(solution)/shard_map/ppermute | solution.py:29
  4.8 1.5 %collective-permute-start.1 = (bf16[256,256]{1,0:T(8,128)(2,1)S(1)}, bf16[256,256]{1,0:T(8,128)(2,1)S(1)}, u32[]{:S(2)}, u32[]{:S(2)}) collective-permute-start(bf16[256,256]{1,0:T(8,128)(2,1)S(1)} %bitcast.31), channel_id=1, source_target_pairs={{0,16},{8,24},{16,0},{24,8},{1,17},{9,25},{17,1},{25,9},{2,18},{10... | collective-permute-start | bytes 393224 | tf_op jit(solution)/shard_map/ppermute | solution.py:29
  6.3 0.0 collective-permute-start.2
  6.4 0.0 copy-done.4
  6.4 0.0 copy-start
  6.4 0.0 copy-start.1
  6.4 0.0 copy-start.3
  6.4 0.7 %copy-done.3 = f32[512]{0:T(512)S(1)} copy-done((f32[512]{0:T(512)S(1)}, f32[512]{0:T(512)}, u32[]{:S(2)}) %copy-start.3) | copy-done | bytes 2072
  7.1 0.1 shard_map.94
  7.3 2.0 %collective-permute-start.3 = (bf16[128,256]{1,0:T(8,128)(2,1)S(1)}, bf16[128,256]{1,0:T(8,128)(2,1)S(1)}, u32[]{:S(2)}, u32[]{:S(2)}) collective-permute-start(bf16[128,256]{1,0:T(8,128)(2,1)S(1)} %get-tuple-element.23), channel_id=1, source_target_pairs={{0,8},{8,0},{16,24},{24,16},{1,9},{9,1},{17,25},{25,17},{2,10},{10... | collective-permute-start | bytes 196616 | tf_op jit(solution)/shard_map/ppermute | solution.py:29
  9.3 1.5 %collective-permute-start.4 = (bf16[128,256]{1,0:T(8,128)(2,1)S(1)}, bf16[128,256]{1,0:T(8,128)(2,1)S(1)}, u32[]{:S(2)}, u32[]{:S(2)}) collective-permute-start(bf16[128,256]{1,0:T(8,128)(2,1)S(1)} %get-tuple-element.48), channel_id=1, source_target_pairs={{0,16},{8,24},{16,0},{24,8},{1,17},{9,25},{17,1},{25,9},{2,18},{10... | collective-permute-start | bytes 196616 | tf_op jit(solution)/shard_map/ppermute | solution.py:29
  10.8 0.0 collective-permute-done.s1
  10.8 1.3 %collective-permute-start.5 = (bf16[128,256]{1,0:T(8,128)(2,1)S(1)}, bf16[128,256]{1,0:T(8,128)(2,1)S(1)}, u32[]{:S(2)}, u32[]{:S(2)}) collective-permute-start(bf16[128,256]{1,0:T(8,128)(2,1)S(1)} %get-tuple-element.47), channel_id=1, source_target_pairs={{0,24},{8,16},{16,8},{24,0},{1,25},{9,17},{17,9},{25,1},{2,26},{10... | collective-permute-start | bytes 196616 | tf_op jit(solution)/shard_map/ppermute | solution.py:29
  12.2 0.9 %collective-permute-done.1.s2 = bf16[256,256]{1,0:T(8,128)(2,1)S(1)} collective-permute-done((bf16[256,256]{1,0:T(8,128)(2,1)S(1)}, bf16[256,256]{1,0:T(8,128)(2,1)S(1)}, u32[]{:S(2)}, u32[]{:S(2)}) %collective-permute-start.1) | collective-permute-done | bytes 131104 | tf_op jit(solution)/shard_map/ppermute | solution.py:29
  13.0 0.4 %collective-permute-done.2.s3 = bf16[256,256]{1,0:T(8,128)(2,1)S(1)} collective-permute-done((bf16[256,256]{1,0:T(8,128)(2,1)S(1)}, bf16[256,256]{1,0:T(8,128)(2,1)S(1)}, u32[]{:S(2)}, u32[]{:S(2)}) %collective-permute-start.2) | collective-permute-done | bytes 131104 | tf_op jit(solution)/shard_map/ppermute | solution.py:29
  13.4 0.0 copy-done
  13.4 0.0 copy-done.1
  13.4 1.2 %shard_map.96 = (f32[128,256]{1,0:T(8,128)S(1)}, bf16[128,256]{1,0:T(8,128)(2,1)S(1)}, bf16[128,256]{1,0:T(8,128)(2,1)S(1)}, bf16[128,256]{1,0:T(8,128)(2,1)S(1)}) custom-call(bf16[256,256]{1,0:T(8,128)(2,1)S(1)} %bitcast.23, bf16[256,256]{1,0:T(8,128)(2,1)S(1)} %collective-permute-done.s1, bf16[256,256]{1,0:T(8,128)(2,1)S(1)} %collective-permute-done.1.s2, ...), custom_call_target="tpu_custom_call" | custom-call | flops 1000 | bytes 1000 | tf_op jit(solution)/shard_map/pallas_call | solution.py:175
  14.6 1.7 %collective-permute-start.9 = (bf16[128,256]{1,0:T(8,128)(2,1)S(1)}, bf16[128,256]{1,0:T(8,128)(2,1)S(1)}, u32[]{:S(2)}, u32[]{:S(2)}) collective-permute-start(bf16[128,256]{1,0:T(8,128)(2,1)S(1)} %get-tuple-element.29), channel_id=1, source_target_pairs={{0,8},{8,0},{16,24},{24,16},{1,9},{9,1},{17,25},{25,17},{2,10},{10... | collective-permute-start | bytes 196616 | tf_op jit(solution)/shard_map/ppermute | solution.py:29
  16.3 0.6 %collective-permute-start.10 = (bf16[128,256]{1,0:T(8,128)(2,1)S(1)}, bf16[128,256]{1,0:T(8,128)(2,1)S(1)}, u32[]{:S(2)}, u32[]{:S(2)}) collective-permute-start(bf16[128,256]{1,0:T(8,128)(2,1)S(1)} %get-tuple-element.30), channel_id=1, source_target_pairs={{0,16},{8,24},{16,0},{24,8},{1,17},{9,25},{17,1},{25,9},{2,18},{10... | collective-permute-start | bytes 196616 | tf_op jit(solution)/shard_map/ppermute | solution.py:29
  16.9 0.0 collective-permute-done.3.f1
  16.9 1.4 %collective-permute-start.11 = (bf16[128,256]{1,0:T(8,128)(2,1)S(1)}, bf16[128,256]{1,0:T(8,128)(2,1)S(1)}, u32[]{:S(2)}, u32[]{:S(2)}) collective-permute-start(bf16[128,256]{1,0:T(8,128)(2,1)S(1)} %get-tuple-element.31), channel_id=1, source_target_pairs={{0,24},{8,16},{16,8},{24,0},{1,25},{9,17},{17,9},{25,1},{2,26},{10... | collective-permute-start | bytes 196616 | tf_op jit(solution)/shard_map/ppermute | solution.py:29
  18.2 0.0 collective-permute-done.4.f2
  18.2 0.0 collective-permute-done.5.f3
  18.3 1.2 %shard_map.95 = (f32[128,256]{1,0:T(8,128)S(1)}, f32[128,256]{1,0:T(8,128)S(1)}, f32[128,256]{1,0:T(8,128)S(1)}, f32[128,256]{1,0:T(8,128)S(1)}) custom-call(bf16[256,256]{1,0:T(8,128)(2,1)S(1)} %bitcast.24, bf16[256,256]{1,0:T(8,128)(2,1)S(1)} %collective-permute-done.s1, bf16[256,256]{1,0:T(8,128)(2,1)S(1)} %collective-permute-done.1.s2, ...), custom_call_target="tpu_custom_call" | custom-call | flops 1000 | bytes 1000 | tf_op jit(solution)/shard_map/pallas_call | solution.py:186
  19.4 1.6 %collective-permute-start.6 = (f32[128,256]{1,0:T(8,128)S(1)}, f32[128,256]{1,0:T(8,128)S(1)}, u32[]{:S(2)}, u32[]{:S(2)}) collective-permute-start(f32[128,256]{1,0:T(8,128)S(1)} %get-tuple-element.25.after), channel_id=1, source_target_pairs={{0,8},{8,0},{16,24},{24,16},{1,9},{9,1},{17,25},{25,17},{2,10},{10... | collective-permute-start | bytes 393224 | tf_op jit(solution)/shard_map/ppermute | solution.py:29
  21.0 0.6 %collective-permute-start.7 = (f32[128,256]{1,0:T(8,128)S(1)}, f32[128,256]{1,0:T(8,128)S(1)}, u32[]{:S(2)}, u32[]{:S(2)}) collective-permute-start(f32[128,256]{1,0:T(8,128)S(1)} %get-tuple-element.26), channel_id=1, source_target_pairs={{0,16},{8,24},{16,0},{24,8},{1,17},{9,25},{17,1},{25,9},{2,18},{10... | collective-permute-start | bytes 393224 | tf_op jit(solution)/shard_map/ppermute | solution.py:29
  21.6 0.0 collective-permute-done.9.w1
  21.6 1.4 %collective-permute-start.8 = (f32[128,256]{1,0:T(8,128)S(1)}, f32[128,256]{1,0:T(8,128)S(1)}, u32[]{:S(2)}, u32[]{:S(2)}) collective-permute-start(f32[128,256]{1,0:T(8,128)S(1)} %get-tuple-element.27), channel_id=1, source_target_pairs={{0,24},{8,16},{16,8},{24,0},{1,25},{9,17},{17,9},{25,1},{2,26},{10... | collective-permute-start | bytes 393224 | tf_op jit(solution)/shard_map/ppermute | solution.py:29
  23.0 0.0 collective-permute-done.10.w2
  23.0 0.0 collective-permute-done.11.w3
  23.0 0.0 copy-done.2
  23.0 0.3 shard_map.97
  23.3 0.1 collective-permute-start.12
  23.4 1.2 %collective-permute-done.12.other = bf16[64,256]{1,0:T(8,128)(2,1)S(1)} collective-permute-done((bf16[64,256]{1,0:T(8,128)(2,1)S(1)}, bf16[64,256]{1,0:T(8,128)(2,1)S(1)}, u32[]{:S(2)}, u32[]{:S(2)}) %collective-permute-start.12) | collective-permute-done | bytes 32800 | tf_op jit(solution)/shard_map/ppermute | solution.py:29
  24.6 3.7 %collective-permute-start.13 = (bf16[64,256]{1,0:T(8,128)(2,1)S(1)}, bf16[64,256]{1,0:T(8,128)(2,1)S(1)}, u32[]{:S(2)}, u32[]{:S(2)}) collective-permute-start(bf16[64,256]{1,0:T(8,128)(2,1)S(1)} %get-tuple-element.36), channel_id=1, source_target_pairs={{0,6},{1,5},{2,4},{3,7},{4,2},{5,1},{6,0},{7,3},{8,14},{9,13},{10,... | collective-permute-start | bytes 98312 | tf_op jit(solution)/shard_map/ppermute | solution.py:221
  28.2 0.7 %collective-permute-start.14 = (bf16[64,256]{1,0:T(8,128)(2,1)S(1)}, bf16[64,256]{1,0:T(8,128)(2,1)S(1)}, u32[]{:S(2)}, u32[]{:S(2)}) collective-permute-start(bf16[64,256]{1,0:T(8,128)(2,1)S(1)} %get-tuple-element.36), channel_id=1, source_target_pairs={{0,0},{1,3},{2,2},{3,1},{4,4},{5,7},{6,6},{7,5},{8,8},{9,11},{10,1... | collective-permute-start | bytes 98312 | tf_op jit(solution)/shard_map/ppermute | solution.py:222
  28.9 0.8 %shard_map.99 = (f32[4,128,256]{2,1,0:T(8,128)}, f32[8,128]{1,0:T(8,128)S(1)}) custom-call(f32[128,256]{1,0:T(8,128)S(1)} %get-tuple-element.28.w0, bf16[128,256]{1,0:T(8,128)(2,1)S(1)} %collective-permute-done.9.w1, bf16[128,256]{1,0:T(8,128)(2,1)S(1)} %collective-permute-done.10.w2, bf16[128,256]{1,0:T(8,128)(2,1)S(1)} %collective-permute-done.11.w3), custom_call_target="tpu_custom_call" | custom-call | flops 1000 | bytes 1000 | tf_op jit(solution)/shard_map/pallas_call | solution.py:205
  29.7 0.6 %collective-permute-done.13.first = bf16[64,256]{1,0:T(8,128)(2,1)S(1)} collective-permute-done((bf16[64,256]{1,0:T(8,128)(2,1)S(1)}, bf16[64,256]{1,0:T(8,128)(2,1)S(1)}, u32[]{:S(2)}, u32[]{:S(2)}) %collective-permute-start.13) | collective-permute-done | bytes 32800 | tf_op jit(solution)/shard_map/ppermute | solution.py:221
  30.4 0.0 collective-permute-done.14.second
  30.4 1.5 %collective-permute-start.15 = (bf16[64,256]{1,0:T(8,128)(2,1)S(1)}, bf16[64,256]{1,0:T(8,128)(2,1)S(1)}, u32[]{:S(2)}, u32[]{:S(2)}) collective-permute-start(bf16[64,256]{1,0:T(8,128)(2,1)S(1)} %get-tuple-element.39), channel_id=1, source_target_pairs={{0,1},{1,0},{2,3},{3,2},{4,5},{5,4},{6,7},{7,6},{8,9},{9,8},{10,11... | collective-permute-start | bytes 98312 | tf_op jit(solution)/shard_map/ppermute | solution.py:29
  31.8 0.0 collective-permute-done.6.v1
  31.8 0.0 collective-permute-done.7.v2
  31.9 0.0 collective-permute-done.8.v3
  31.9 0.8 %collective-permute-done.15.other = bf16[64,256]{1,0:T(8,128)(2,1)S(1)} collective-permute-done((bf16[64,256]{1,0:T(8,128)(2,1)S(1)}, bf16[64,256]{1,0:T(8,128)(2,1)S(1)}, u32[]{:S(2)}, u32[]{:S(2)}) %collective-permute-start.15) | collective-permute-done | bytes 32800 | tf_op jit(solution)/shard_map/ppermute | solution.py:29
  32.7 0.8 %shard_map.101 = (bf16[4,128,256]{2,1,0:T(8,128)(2,1)}, f32[64,256]{1,0:T(8,128)}) custom-call(f32[128,256]{1,0:T(8,128)S(1)} %get-tuple-element.24.v0, f32[128,256]{1,0:T(8,128)S(1)} %collective-permute-done.6.v1, f32[128,256]{1,0:T(8,128)S(1)} %collective-permute-done.7.v2, f32[128,256]{1,0:T(8,128)S(1)} %collective-permute-done.8.v3, ...), custom_call_target="tpu_custom_call" | custom-call | flops 1000 | bytes 1000 | tf_op jit(solution)/shard_map/pallas_call | solution.py:233
  (4 shorter events, 0.0 us)
Async XLA Ops:
  0.7 5.7 %copy-start.4 = (bf16[512,256]{1,0:T(8,128)(2,1)S(1)}, bf16[512,256]{1,0:T(8,128)(2,1)}, u32[]{:S(2)}) copy-start(bf16[512,256]{1,0:T(8,128)(2,1)} %param.9) | copy-start | bytes 786436
  1.8 9.0 %collective-permute-start = (bf16[256,256]{1,0:T(8,128)(2,1)S(1)}, bf16[256,256]{1,0:T(8,128)(2,1)S(1)}, u32[]{:S(2)}, u32[]{:S(2)}) collective-permute-start(bf16[256,256]{1,0:T(8,128)(2,1)S(1)} %bitcast.32), channel_id=1, source_target_pairs={{0,8},{8,0},{16,24},{24,16},{1,9},{9,1},{17,25},{25,17},{2,10},{10... | collective-permute-start | bytes 393224 | tf_op jit(solution)/shard_map/ppermute | solution.py:29
  4.8 8.2 %collective-permute-start.1 = (bf16[256,256]{1,0:T(8,128)(2,1)S(1)}, bf16[256,256]{1,0:T(8,128)(2,1)S(1)}, u32[]{:S(2)}, u32[]{:S(2)}) collective-permute-start(bf16[256,256]{1,0:T(8,128)(2,1)S(1)} %bitcast.31), channel_id=1, source_target_pairs={{0,16},{8,24},{16,0},{24,8},{1,17},{9,25},{17,1},{25,9},{2,18},{10... | collective-permute-start | bytes 393224 | tf_op jit(solution)/shard_map/ppermute | solution.py:29
  6.3 7.0 %collective-permute-start.2 = (bf16[256,256]{1,0:T(8,128)(2,1)S(1)}, bf16[256,256]{1,0:T(8,128)(2,1)S(1)}, u32[]{:S(2)}, u32[]{:S(2)}) collective-permute-start(bf16[256,256]{1,0:T(8,128)(2,1)S(1)} %bitcast.30), channel_id=1, source_target_pairs={{0,24},{8,16},{16,8},{24,0},{1,25},{9,17},{17,9},{25,1},{2,26},{10... | collective-permute-start | bytes 393224 | tf_op jit(solution)/shard_map/ppermute | solution.py:29
  6.4 7.0 %copy-start = (bf16[256,512]{1,0:T(8,128)(2,1)S(1)}, bf16[256,512]{1,0:T(8,128)(2,1)}, u32[]{:S(2)}) copy-start(bf16[256,512]{1,0:T(8,128)(2,1)} %constant.37.clone.table) | copy-start | bytes 786436
  6.4 7.0 %copy-start.1 = (bf16[512,256]{1,0:T(8,128)(2,1)S(1)}, bf16[512,256]{1,0:T(8,128)(2,1)}, u32[]{:S(2)}) copy-start(bf16[512,256]{1,0:T(8,128)(2,1)} %constant.38.clone.back) | copy-start | bytes 786436
  6.4 0.7 %copy-start.3 = (f32[512]{0:T(512)S(1)}, f32[512]{0:T(512)}, u32[]{:S(2)}) copy-start(f32[512]{0:T(512)} %param.10) | copy-start | bytes 6148
  7.3 9.6 %collective-permute-start.3 = (bf16[128,256]{1,0:T(8,128)(2,1)S(1)}, bf16[128,256]{1,0:T(8,128)(2,1)S(1)}, u32[]{:S(2)}, u32[]{:S(2)}) collective-permute-start(bf16[128,256]{1,0:T(8,128)(2,1)S(1)} %get-tuple-element.23), channel_id=1, source_target_pairs={{0,8},{8,0},{16,24},{24,16},{1,9},{9,1},{17,25},{25,17},{2,10},{10... | collective-permute-start | bytes 196616 | tf_op jit(solution)/shard_map/ppermute | solution.py:29
  9.3 8.9 %collective-permute-start.4 = (bf16[128,256]{1,0:T(8,128)(2,1)S(1)}, bf16[128,256]{1,0:T(8,128)(2,1)S(1)}, u32[]{:S(2)}, u32[]{:S(2)}) collective-permute-start(bf16[128,256]{1,0:T(8,128)(2,1)S(1)} %get-tuple-element.48), channel_id=1, source_target_pairs={{0,16},{8,24},{16,0},{24,8},{1,17},{9,25},{17,1},{25,9},{2,18},{10... | collective-permute-start | bytes 196616 | tf_op jit(solution)/shard_map/ppermute | solution.py:29
  10.8 7.4 %collective-permute-start.5 = (bf16[128,256]{1,0:T(8,128)(2,1)S(1)}, bf16[128,256]{1,0:T(8,128)(2,1)S(1)}, u32[]{:S(2)}, u32[]{:S(2)}) collective-permute-start(bf16[128,256]{1,0:T(8,128)(2,1)S(1)} %get-tuple-element.47), channel_id=1, source_target_pairs={{0,24},{8,16},{16,8},{24,0},{1,25},{9,17},{17,9},{25,1},{2,26},{10... | collective-permute-start | bytes 196616 | tf_op jit(solution)/shard_map/ppermute | solution.py:29
  14.6 7.0 %collective-permute-start.9 = (bf16[128,256]{1,0:T(8,128)(2,1)S(1)}, bf16[128,256]{1,0:T(8,128)(2,1)S(1)}, u32[]{:S(2)}, u32[]{:S(2)}) collective-permute-start(bf16[128,256]{1,0:T(8,128)(2,1)S(1)} %get-tuple-element.29), channel_id=1, source_target_pairs={{0,8},{8,0},{16,24},{24,16},{1,9},{9,1},{17,25},{25,17},{2,10},{10... | collective-permute-start | bytes 196616 | tf_op jit(solution)/shard_map/ppermute | solution.py:29
  16.3 6.7 %collective-permute-start.10 = (bf16[128,256]{1,0:T(8,128)(2,1)S(1)}, bf16[128,256]{1,0:T(8,128)(2,1)S(1)}, u32[]{:S(2)}, u32[]{:S(2)}) collective-permute-start(bf16[128,256]{1,0:T(8,128)(2,1)S(1)} %get-tuple-element.30), channel_id=1, source_target_pairs={{0,16},{8,24},{16,0},{24,8},{1,17},{9,25},{17,1},{25,9},{2,18},{10... | collective-permute-start | bytes 196616 | tf_op jit(solution)/shard_map/ppermute | solution.py:29
  16.9 6.2 %collective-permute-start.11 = (bf16[128,256]{1,0:T(8,128)(2,1)S(1)}, bf16[128,256]{1,0:T(8,128)(2,1)S(1)}, u32[]{:S(2)}, u32[]{:S(2)}) collective-permute-start(bf16[128,256]{1,0:T(8,128)(2,1)S(1)} %get-tuple-element.31), channel_id=1, source_target_pairs={{0,24},{8,16},{16,8},{24,0},{1,25},{9,17},{17,9},{25,1},{2,26},{10... | collective-permute-start | bytes 196616 | tf_op jit(solution)/shard_map/ppermute | solution.py:29
  18.2 4.8 %copy-start.2 = (bf16[512,64]{0,1:T(8,128)(2,1)S(1)}, bf16[512,64]{0,1:T(8,128)(2,1)}, u32[]{:S(2)}) copy-start(bf16[512,64]{0,1:T(8,128)(2,1)} %param.11) | copy-start | bytes 196612
  19.4 12.4 %collective-permute-start.6 = (f32[128,256]{1,0:T(8,128)S(1)}, f32[128,256]{1,0:T(8,128)S(1)}, u32[]{:S(2)}, u32[]{:S(2)}) collective-permute-start(f32[128,256]{1,0:T(8,128)S(1)} %get-tuple-element.25.after), channel_id=1, source_target_pairs={{0,8},{8,0},{16,24},{24,16},{1,9},{9,1},{17,25},{25,17},{2,10},{10... | collective-permute-start | bytes 393224 | tf_op jit(solution)/shard_map/ppermute | solution.py:29
  21.0 10.8 %collective-permute-start.7 = (f32[128,256]{1,0:T(8,128)S(1)}, f32[128,256]{1,0:T(8,128)S(1)}, u32[]{:S(2)}, u32[]{:S(2)}) collective-permute-start(f32[128,256]{1,0:T(8,128)S(1)} %get-tuple-element.26), channel_id=1, source_target_pairs={{0,16},{8,24},{16,0},{24,8},{1,17},{9,25},{17,1},{25,9},{2,18},{10... | collective-permute-start | bytes 393224 | tf_op jit(solution)/shard_map/ppermute | solution.py:29
  21.6 10.2 %collective-permute-start.8 = (f32[128,256]{1,0:T(8,128)S(1)}, f32[128,256]{1,0:T(8,128)S(1)}, u32[]{:S(2)}, u32[]{:S(2)}) collective-permute-start(f32[128,256]{1,0:T(8,128)S(1)} %get-tuple-element.27), channel_id=1, source_target_pairs={{0,24},{8,16},{16,8},{24,0},{1,25},{9,17},{17,9},{25,1},{2,26},{10... | collective-permute-start | bytes 393224 | tf_op jit(solution)/shard_map/ppermute | solution.py:29
  23.3 1.3 %collective-permute-start.12 = (bf16[64,256]{1,0:T(8,128)(2,1)S(1)}, bf16[64,256]{1,0:T(8,128)(2,1)S(1)}, u32[]{:S(2)}, u32[]{:S(2)}) collective-permute-start(bf16[64,256]{1,0:T(8,128)(2,1)S(1)} %get-tuple-element.34), channel_id=1, source_target_pairs={{0,1},{1,0},{2,3},{3,2},{4,5},{5,4},{6,7},{7,6},{8,9},{9,8},{10,11... | collective-permute-start | bytes 98312 | tf_op jit(solution)/shard_map/ppermute | solution.py:29
  24.6 5.8 %collective-permute-start.13 = (bf16[64,256]{1,0:T(8,128)(2,1)S(1)}, bf16[64,256]{1,0:T(8,128)(2,1)S(1)}, u32[]{:S(2)}, u32[]{:S(2)}) collective-permute-start(bf16[64,256]{1,0:T(8,128)(2,1)S(1)} %get-tuple-element.36), channel_id=1, source_target_pairs={{0,6},{1,5},{2,4},{3,7},{4,2},{5,1},{6,0},{7,3},{8,14},{9,13},{10,... | collective-permute-start | bytes 98312 | tf_op jit(solution)/shard_map/ppermute | solution.py:221
  28.2 2.1 %collective-permute-start.14 = (bf16[64,256]{1,0:T(8,128)(2,1)S(1)}, bf16[64,256]{1,0:T(8,128)(2,1)S(1)}, u32[]{:S(2)}, u32[]{:S(2)}) collective-permute-start(bf16[64,256]{1,0:T(8,128)(2,1)S(1)} %get-tuple-element.36), channel_id=1, source_target_pairs={{0,0},{1,3},{2,2},{3,1},{4,4},{5,7},{6,6},{7,5},{8,8},{9,11},{10,1... | collective-permute-start | bytes 98312 | tf_op jit(solution)/shard_map/ppermute | solution.py:222
  30.4 2.3 %collective-permute-start.15 = (bf16[64,256]{1,0:T(8,128)(2,1)S(1)}, bf16[64,256]{1,0:T(8,128)(2,1)S(1)}, u32[]{:S(2)}, u32[]{:S(2)}) collective-permute-start(bf16[64,256]{1,0:T(8,128)(2,1)S(1)} %get-tuple-element.39), channel_id=1, source_target_pairs={{0,1},{1,0},{2,3},{3,2},{4,5},{5,4},{6,7},{7,6},{8,9},{9,8},{10,11... | collective-permute-start | bytes 98312 | tf_op jit(solution)/shard_map/ppermute | solution.py:29

commit v4 on v3

--- a/solution.py
+++ b/solution.py
@@ -166,7 +166,7 @@
         in_specs=[vmem, space],
         out_specs=[vmem, space],
         input_output_aliases={1: 1},
-        compiler_params=small,
+        compiler_params=pltpu.CompilerParams(vmem_limit_bytes=60 * 1024 * 1024),
         cost_estimate=cost,
     )(rates.reshape(1, channels), slots_f[1])
     slots = slots[:1] + [xor_permute(slots[k], "seq", 4, k) for k in (1, 2, 3)]

time: 33.6 us -> 33 us (0.982)
  starting transfers between devices: 22.5 us -> 20.5 us
  Pallas kernels: 4.39 us -> 5.84 us
    pallas_call x1, Pallas kernels: 0.15 us -> 1.63 us  [body_four(): pl.pallas_call(functools.partial(window_kernel, rows, block, total), out_...]
    ppermute x14, starting transfers between devices: 18.2 us -> 16.7 us  [xor_permute(): return lax.ppermute(value, axis, [(j, j ^ k) for j in range(size)])]
    unnamed x10, local copies, waits for them, and re-layouts: 0.74 us -> 0.02 us
    squeeze x1, local copies, waits for them, and re-layouts: 0.02 us -> 0.65 us  [body_four(): lax.dynamic_index_in_dim(filt.reshape(4, rows, block), me ^ k, 0, keepdim...]
    ppermute x1, starting transfers between devices: 3.66 us -> 3.16 us  [body_four(): lax.ppermute(pair_sent, 'chan', [(c, c ^ (4 if c % 2 else 6)) for c in ra...]
    ppermute x1, waiting for transfers between devices: 0.62 us -> 1.12 us  [body_four(): lax.ppermute(pair_sent, 'chan', [(c, c ^ (4 if c % 2 else 6)) for c in ra...]
    ppermute x14, waiting for transfers between devices: 3.29 us -> 2.8 us  [xor_permute(): return lax.ppermute(value, axis, [(j, j ^ k) for j in range(size)])]
  transfers between devices with their start and end apart: 16 -> 16, of which waited for: 5 -> 5; matrix products, arithmetic and copies ran while one was open for 0% -> 2% of each run, Pallas kernels for 11% -> 15%
where the time goes in v4:
time: 33 us; the launch traced here: 32.9 us
  starting transfers between devices  20.5 us (62%)
  Pallas kernels  5.84 us (18%)
  waiting for transfers between devices  3.92 us (12%)
  other arithmetic  1.16 us (4%)
  between operations  0.76 us (2%)
  local copies, waits for them, and re-layouts  0.67 us (2%)
    ppermute x14, starting transfers between devices, xor_permute(): return lax.ppermute(value, axis, [(j, j ^ k) for j in range(size)])  16.7 us
    ppermute x1, starting transfers between devices, body_four(): lax.ppermute(pair_sent, 'chan', [(c, c ^ (4 if c % 2 else 6)) for c in ra...  3.16 us
    ppermute x14, waiting for transfers between devices, xor_permute(): return lax.ppermute(value, axis, [(j, j ^ k) for j in range(size)])  2.8 us
    pallas_call x1, Pallas kernels, body_four(): pl.pallas_call(functools.partial(window_kernel, rows, block, total), out_...  1.63 us
    pallas_call x1, Pallas kernels, body_four(): pl.pallas_call(functools.partial(input_kernel, rows), out_shape=[shape((r...  1.17 us
    pallas_call x1, Pallas kernels, body_four(): pl.pallas_call(functools.partial(filter_kernel, rows), out_shape=[shape((...  1.16 us
    another operation x1, other arithmetic, body_four(): jnp.stack([value.reshape(4, rows, block) for value in (grad_out, inputs)]...  1.16 us
    ppermute x1, waiting for transfers between devices, body_four(): lax.ppermute(pair_sent, 'chan', [(c, c ^ (4 if c % 2 else 6)) for c in ra...  1.12 us
  transfers between devices with their start and end apart: 16, of which 5 were waited for; matrix products, arithmetic and copies ran while one was open for 2% of the time, Pallas kernels for 15%

profile of v4, /device:TPU:0, one launch (start us, length us, event | category | flops | bytes accessed | tf_op | source)
XLA Modules:
  0.0 32.9 jit_solution(9438061556125230784)
XLA Ops:
  0.7 0.0 copy-start.4
  0.7 1.2 %fusion = (bf16[1,2,128,256]{3,2,1,0:T(8,128)(2,1)S(1)}, bf16[1,2,128,256]{3,2,1,0:T(8,128)(2,1)S(1)}, bf16[1,2,128,256]{3,2,1,0:T(8,128)(2,1)S(1)}, bf16[1,2,128,256]{3,2,1,0:T(8,128)(2,1)S(1)}) fusion(s32[]{:T(128)S(6)} %select_n.21, bf16[4,1,128,256]{3,2,1,0:T(8,128)(2,1)} %bitcast.27, bf16[4,1,128,256]{3,2,1,0:T(8,128)(2,1)} %bitcast.28, ...), kind=kLoop, calls=%fused_computation.8 | loop fusion | flops 262144 | bytes 1048592 | tf_op jit(solution)/shard_map/stack | solution.py:159
  1.8 3.0 %collective-permute-start = (bf16[256,256]{1,0:T(8,128)(2,1)S(1)}, bf16[256,256]{1,0:T(8,128)(2,1)S(1)}, u32[]{:S(2)}, u32[]{:S(2)}) collective-permute-start(bf16[256,256]{1,0:T(8,128)(2,1)S(1)} %bitcast.31), channel_id=1, source_target_pairs={{0,8},{8,0},{16,24},{24,16},{1,9},{9,1},{17,25},{25,17},{2,10},{10... | collective-permute-start | bytes 393224 | tf_op jit(solution)/shard_map/ppermute | solution.py:29
  4.8 1.5 %collective-permute-start.1 = (bf16[256,256]{1,0:T(8,128)(2,1)S(1)}, bf16[256,256]{1,0:T(8,128)(2,1)S(1)}, u32[]{:S(2)}, u32[]{:S(2)}) collective-permute-start(bf16[256,256]{1,0:T(8,128)(2,1)S(1)} %bitcast.30), channel_id=1, source_target_pairs={{0,16},{8,24},{16,0},{24,8},{1,17},{9,25},{17,1},{25,9},{2,18},{10... | collective-permute-start | bytes 393224 | tf_op jit(solution)/shard_map/ppermute | solution.py:29
  6.3 0.0 collective-permute-start.2
  6.4 0.0 copy-done.4
  6.4 0.0 copy-start
  6.4 0.6 %dynamic-slice_bitcast_fusion = (bf16[128,256]{1,0:T(8,128)(2,1)S(1)}, bf16[128,256]{1,0:T(8,128)(2,1)S(1)}, bf16[128,256]{1,0:T(8,128)(2,1)}, bf16[128,256]{1,0:T(8,128)(2,1)S(1)}) fusion(bf16[4,128,256]{2,1,0:T(8,128)(2,1)S(1)} %bitcast.26, s32[]{:T(128)S(6)} %select_n.21, s32[]{:T(128)S(6)} %select_n.20, s32[]{:T(128)S(6)} %select_n.19, s32[]{:T(128)S(6)} %select_n.18), kind=kLoop, calls=%fused_computation.12 | loop fusion | bytes 524304 | tf_op jit(solution)/shard_map/jit(dynamic_index_in_dim)/squeeze | solution.py:161
  7.0 1.6 %shard_map.94 = (f32[4,128,256]{2,1,0:T(8,128)}, bf16[128,256]{1,0:T(8,128)(2,1)}) custom-call(f32[1,512]{1,0:T(1,128)} %bitcast.32, bf16[128,256]{1,0:T(8,128)(2,1)} %get-tuple-element.49.f_ref), custom_call_target="tpu_custom_call", output_to_operand_aliasing={{1}: (1, {})} | custom-call | flops 1000 | bytes 1000 | tf_op jit(solution)/shard_map/pallas_call | solution.py:163
  8.7 1.9 %collective-permute-start.3 = (bf16[128,256]{1,0:T(8,128)(2,1)}, bf16[128,256]{1,0:T(8,128)(2,1)S(1)}, u32[]{:S(2)}, u32[]{:S(2)}) collective-permute-start(bf16[128,256]{1,0:T(8,128)(2,1)} %get-tuple-element.23), channel_id=1, source_target_pairs={{0,8},{8,0},{16,24},{24,16},{1,9},{9,1},{17,25},{25,17},{2,10},{10... | collective-permute-start | bytes 196616 | tf_op jit(solution)/shard_map/ppermute | solution.py:29
  10.6 1.5 %collective-permute-start.4 = (bf16[128,256]{1,0:T(8,128)(2,1)S(1)}, bf16[128,256]{1,0:T(8,128)(2,1)S(1)}, u32[]{:S(2)}, u32[]{:S(2)}) collective-permute-start(bf16[128,256]{1,0:T(8,128)(2,1)S(1)} %get-tuple-element.48), channel_id=1, source_target_pairs={{0,16},{8,24},{16,0},{24,8},{1,17},{9,25},{17,1},{25,9},{2,18},{10... | collective-permute-start | bytes 196616 | tf_op jit(solution)/shard_map/ppermute | solution.py:29
  12.1 0.0 collective-permute-done.s1
  12.1 0.0 collective-permute-start.5
  12.2 0.3 %collective-permute-done.1.s2 = bf16[256,256]{1,0:T(8,128)(2,1)S(1)} collective-permute-done((bf16[256,256]{1,0:T(8,128)(2,1)S(1)}, bf16[256,256]{1,0:T(8,128)(2,1)S(1)}, u32[]{:S(2)}, u32[]{:S(2)}) %collective-permute-start.1) | collective-permute-done | bytes 131104 | tf_op jit(solution)/shard_map/ppermute | solution.py:29
  12.5 0.4 %collective-permute-done.2.s3 = bf16[256,256]{1,0:T(8,128)(2,1)S(1)} collective-permute-done((bf16[256,256]{1,0:T(8,128)(2,1)S(1)}, bf16[256,256]{1,0:T(8,128)(2,1)S(1)}, u32[]{:S(2)}, u32[]{:S(2)}) %collective-permute-start.2) | collective-permute-done | bytes 131104 | tf_op jit(solution)/shard_map/ppermute | solution.py:29
  12.9 0.0 copy-done
  12.9 0.0 copy-done.1
  12.9 1.2 %shard_map.96 = (f32[128,256]{1,0:T(8,128)S(1)}, bf16[128,256]{1,0:T(8,128)(2,1)S(1)}, bf16[128,256]{1,0:T(8,128)(2,1)S(1)}, bf16[128,256]{1,0:T(8,128)(2,1)S(1)}) custom-call(bf16[256,256]{1,0:T(8,128)(2,1)S(1)} %bitcast.23, bf16[256,256]{1,0:T(8,128)(2,1)S(1)} %collective-permute-done.s1, bf16[256,256]{1,0:T(8,128)(2,1)S(1)} %collective-permute-done.1.s2, ...), custom_call_target="tpu_custom_call" | custom-call | flops 1000 | bytes 1000 | tf_op jit(solution)/shard_map/pallas_call | solution.py:175
  14.1 1.4 %collective-permute-start.9 = (bf16[128,256]{1,0:T(8,128)(2,1)S(1)}, bf16[128,256]{1,0:T(8,128)(2,1)S(1)}, u32[]{:S(2)}, u32[]{:S(2)}) collective-permute-start(bf16[128,256]{1,0:T(8,128)(2,1)S(1)} %get-tuple-element.29), channel_id=1, source_target_pairs={{0,8},{8,0},{16,24},{24,16},{1,9},{9,1},{17,25},{25,17},{2,10},{10... | collective-permute-start | bytes 196616 | tf_op jit(solution)/shard_map/ppermute | solution.py:29
  15.5 1.4 %collective-permute-start.10 = (bf16[128,256]{1,0:T(8,128)(2,1)S(1)}, bf16[128,256]{1,0:T(8,128)(2,1)S(1)}, u32[]{:S(2)}, u32[]{:S(2)}) collective-permute-start(bf16[128,256]{1,0:T(8,128)(2,1)S(1)} %get-tuple-element.30), channel_id=1, source_target_pairs={{0,16},{8,24},{16,0},{24,8},{1,17},{9,25},{17,1},{25,9},{2,18},{10... | collective-permute-start | bytes 196616 | tf_op jit(solution)/shard_map/ppermute | solution.py:29
  16.9 0.0 collective-permute-done.3.f1
  16.9 1.3 %collective-permute-start.11 = (bf16[128,256]{1,0:T(8,128)(2,1)S(1)}, bf16[128,256]{1,0:T(8,128)(2,1)S(1)}, u32[]{:S(2)}, u32[]{:S(2)}) collective-permute-start(bf16[128,256]{1,0:T(8,128)(2,1)S(1)} %get-tuple-element.31), channel_id=1, source_target_pairs={{0,24},{8,16},{16,8},{24,0},{1,25},{9,17},{17,9},{25,1},{2,26},{10... | collective-permute-start | bytes 196616 | tf_op jit(solution)/shard_map/ppermute | solution.py:29
  18.1 0.0 collective-permute-done.4.f2
  18.2 0.0 collective-permute-done.5.f3
  18.2 0.0 copy-start.3
  18.2 1.2 %shard_map.95 = (f32[128,256]{1,0:T(8,128)S(1)}, f32[128,256]{1,0:T(8,128)S(1)}, f32[128,256]{1,0:T(8,128)S(1)}, f32[128,256]{1,0:T(8,128)S(1)}) custom-call(bf16[256,256]{1,0:T(8,128)(2,1)S(1)} %bitcast.24, bf16[256,256]{1,0:T(8,128)(2,1)S(1)} %collective-permute-done.s1, bf16[256,256]{1,0:T(8,128)(2,1)S(1)} %collective-permute-done.1.s2, ...), custom_call_target="tpu_custom_call" | custom-call | flops 1000 | bytes 1000 | tf_op jit(solution)/shard_map/pallas_call | solution.py:186
  19.3 0.9 %collective-permute-start.6 = (f32[128,256]{1,0:T(8,128)S(1)}, f32[128,256]{1,0:T(8,128)S(1)}, u32[]{:S(2)}, u32[]{:S(2)}) collective-permute-start(f32[128,256]{1,0:T(8,128)S(1)} %get-tuple-element.25.after), channel_id=1, source_target_pairs={{0,8},{8,0},{16,24},{24,16},{1,9},{9,1},{17,25},{25,17},{2,10},{10... | collective-permute-start | bytes 393224 | tf_op jit(solution)/shard_map/ppermute | solution.py:29
  20.3 1.4 %collective-permute-start.7 = (f32[128,256]{1,0:T(8,128)S(1)}, f32[128,256]{1,0:T(8,128)S(1)}, u32[]{:S(2)}, u32[]{:S(2)}) collective-permute-start(f32[128,256]{1,0:T(8,128)S(1)} %get-tuple-element.26), channel_id=1, source_target_pairs={{0,16},{8,24},{16,0},{24,8},{1,17},{9,25},{17,1},{25,9},{2,18},{10... | collective-permute-start | bytes 393224 | tf_op jit(solution)/shard_map/ppermute | solution.py:29
  21.6 0.0 collective-permute-done.9.w1
  21.6 1.3 %collective-permute-start.8 = (f32[128,256]{1,0:T(8,128)S(1)}, f32[128,256]{1,0:T(8,128)S(1)}, u32[]{:S(2)}, u32[]{:S(2)}) collective-permute-start(f32[128,256]{1,0:T(8,128)S(1)} %get-tuple-element.27), channel_id=1, source_target_pairs={{0,24},{8,16},{16,8},{24,0},{1,25},{9,17},{17,9},{25,1},{2,26},{10... | collective-permute-start | bytes 393224 | tf_op jit(solution)/shard_map/ppermute | solution.py:29
  22.9 0.0 collective-permute-done.10.w2
  22.9 0.0 collective-permute-done.11.w3
  22.9 0.0 copy-done.2
  22.9 0.0 copy-done.3
  22.9 0.3 shard_map.97
  23.2 0.1 collective-permute-start.12
  23.3 1.2 %collective-permute-done.12.other = bf16[64,256]{1,0:T(8,128)(2,1)S(1)} collective-permute-done((bf16[64,256]{1,0:T(8,128)(2,1)S(1)}, bf16[64,256]{1,0:T(8,128)(2,1)S(1)}, u32[]{:S(2)}, u32[]{:S(2)}) %collective-permute-start.12) | collective-permute-done | bytes 32800 | tf_op jit(solution)/shard_map/ppermute | solution.py:29
  24.5 3.2 %collective-permute-start.13 = (bf16[64,256]{1,0:T(8,128)(2,1)S(1)}, bf16[64,256]{1,0:T(8,128)(2,1)S(1)}, u32[]{:S(2)}, u32[]{:S(2)}) collective-permute-start(bf16[64,256]{1,0:T(8,128)(2,1)S(1)} %get-tuple-element.36), channel_id=1, source_target_pairs={{0,6},{1,5},{2,4},{3,7},{4,2},{5,1},{6,0},{7,3},{8,14},{9,13},{10,... | collective-permute-start | bytes 98312 | tf_op jit(solution)/shard_map/ppermute | solution.py:221
  27.7 0.7 %collective-permute-start.14 = (bf16[64,256]{1,0:T(8,128)(2,1)S(1)}, bf16[64,256]{1,0:T(8,128)(2,1)S(1)}, u32[]{:S(2)}, u32[]{:S(2)}) collective-permute-start(bf16[64,256]{1,0:T(8,128)(2,1)S(1)} %get-tuple-element.36), channel_id=1, source_target_pairs={{0,0},{1,3},{2,2},{3,1},{4,4},{5,7},{6,6},{7,5},{8,8},{9,11},{10,1... | collective-permute-start | bytes 98312 | tf_op jit(solution)/shard_map/ppermute | solution.py:222
  28.3 0.8 %shard_map.99 = (f32[4,128,256]{2,1,0:T(8,128)}, f32[8,128]{1,0:T(8,128)S(1)}) custom-call(f32[128,256]{1,0:T(8,128)S(1)} %get-tuple-element.28.w0, bf16[128,256]{1,0:T(8,128)(2,1)S(1)} %collective-permute-done.9.w1, bf16[128,256]{1,0:T(8,128)(2,1)S(1)} %collective-permute-done.10.w2, bf16[128,256]{1,0:T(8,128)(2,1)S(1)} %collective-permute-done.11.w3), custom_call_target="tpu_custom_call" | custom-call | flops 1000 | bytes 1000 | tf_op jit(solution)/shard_map/pallas_call | solution.py:205
  29.2 1.1 %collective-permute-done.13.first = bf16[64,256]{1,0:T(8,128)(2,1)S(1)} collective-permute-done((bf16[64,256]{1,0:T(8,128)(2,1)S(1)}, bf16[64,256]{1,0:T(8,128)(2,1)S(1)}, u32[]{:S(2)}, u32[]{:S(2)}) %collective-permute-start.13) | collective-permute-done | bytes 32800 | tf_op jit(solution)/shard_map/ppermute | solution.py:221
  30.3 0.0 collective-permute-done.14.second
  30.3 0.9 %collective-permute-start.15 = (bf16[64,256]{1,0:T(8,128)(2,1)S(1)}, bf16[64,256]{1,0:T(8,128)(2,1)S(1)}, u32[]{:S(2)}, u32[]{:S(2)}) collective-permute-start(bf16[64,256]{1,0:T(8,128)(2,1)S(1)} %get-tuple-element.39), channel_id=1, source_target_pairs={{0,1},{1,0},{2,3},{3,2},{4,5},{5,4},{6,7},{7,6},{8,9},{9,8},{10,11... | collective-permute-start | bytes 98312 | tf_op jit(solution)/shard_map/ppermute | solution.py:29
  31.2 0.0 collective-permute-done.6.v1
  31.3 0.0 collective-permute-done.7.v2
  31.3 0.0 collective-permute-done.8.v3
  31.3 0.8 %collective-permute-done.15.other = bf16[64,256]{1,0:T(8,128)(2,1)S(1)} collective-permute-done((bf16[64,256]{1,0:T(8,128)(2,1)S(1)}, bf16[64,256]{1,0:T(8,128)(2,1)S(1)}, u32[]{:S(2)}, u32[]{:S(2)}) %collective-permute-start.15) | collective-permute-done | bytes 32800 | tf_op jit(solution)/shard_map/ppermute | solution.py:29
  32.1 0.8 %shard_map.101 = (bf16[4,128,256]{2,1,0:T(8,128)(2,1)}, f32[64,256]{1,0:T(8,128)}) custom-call(f32[128,256]{1,0:T(8,128)S(1)} %get-tuple-element.24.v0, f32[128,256]{1,0:T(8,128)S(1)} %collective-permute-done.6.v1, f32[128,256]{1,0:T(8,128)S(1)} %collective-permute-done.7.v2, f32[128,256]{1,0:T(8,128)S(1)} %collective-permute-done.8.v3, ...), custom_call_target="tpu_custom_call" | custom-call | flops 1000 | bytes 1000 | tf_op jit(solution)/shard_map/pallas_call | solution.py:233
  (4 shorter events, 0.0 us)
Async XLA Ops:
  0.7 5.7 %copy-start.4 = (bf16[512,256]{1,0:T(8,128)(2,1)S(1)}, bf16[512,256]{1,0:T(8,128)(2,1)}, u32[]{:S(2)}) copy-start(bf16[512,256]{1,0:T(8,128)(2,1)} %param.9) | copy-start | bytes 786436
  1.8 10.3 %collective-permute-start = (bf16[256,256]{1,0:T(8,128)(2,1)S(1)}, bf16[256,256]{1,0:T(8,128)(2,1)S(1)}, u32[]{:S(2)}, u32[]{:S(2)}) collective-permute-start(bf16[256,256]{1,0:T(8,128)(2,1)S(1)} %bitcast.31), channel_id=1, source_target_pairs={{0,8},{8,0},{16,24},{24,16},{1,9},{9,1},{17,25},{25,17},{2,10},{10... | collective-permute-start | bytes 393224 | tf_op jit(solution)/shard_map/ppermute | solution.py:29
  4.8 7.7 %collective-permute-start.1 = (bf16[256,256]{1,0:T(8,128)(2,1)S(1)}, bf16[256,256]{1,0:T(8,128)(2,1)S(1)}, u32[]{:S(2)}, u32[]{:S(2)}) collective-permute-start(bf16[256,256]{1,0:T(8,128)(2,1)S(1)} %bitcast.30), channel_id=1, source_target_pairs={{0,16},{8,24},{16,0},{24,8},{1,17},{9,25},{17,1},{25,9},{2,18},{10... | collective-permute-start | bytes 393224 | tf_op jit(solution)/shard_map/ppermute | solution.py:29
  6.3 6.6 %collective-permute-start.2 = (bf16[256,256]{1,0:T(8,128)(2,1)S(1)}, bf16[256,256]{1,0:T(8,128)(2,1)S(1)}, u32[]{:S(2)}, u32[]{:S(2)}) collective-permute-start(bf16[256,256]{1,0:T(8,128)(2,1)S(1)} %bitcast.29), channel_id=1, source_target_pairs={{0,24},{8,16},{16,8},{24,0},{1,25},{9,17},{17,9},{25,1},{2,26},{10... | collective-permute-start | bytes 393224 | tf_op jit(solution)/shard_map/ppermute | solution.py:29
  6.4 6.5 %copy-start = (bf16[256,512]{1,0:T(8,128)(2,1)S(1)}, bf16[256,512]{1,0:T(8,128)(2,1)}, u32[]{:S(2)}) copy-start(bf16[256,512]{1,0:T(8,128)(2,1)} %constant.37.clone.table) | copy-start | bytes 786436
  6.4 6.5 %copy-start.1 = (bf16[512,256]{1,0:T(8,128)(2,1)S(1)}, bf16[512,256]{1,0:T(8,128)(2,1)}, u32[]{:S(2)}) copy-start(bf16[512,256]{1,0:T(8,128)(2,1)} %constant.38.clone.back) | copy-start | bytes 786436
  8.7 8.2 %collective-permute-start.3 = (bf16[128,256]{1,0:T(8,128)(2,1)}, bf16[128,256]{1,0:T(8,128)(2,1)S(1)}, u32[]{:S(2)}, u32[]{:S(2)}) collective-permute-start(bf16[128,256]{1,0:T(8,128)(2,1)} %get-tuple-element.23), channel_id=1, source_target_pairs={{0,8},{8,0},{16,24},{24,16},{1,9},{9,1},{17,25},{25,17},{2,10},{10... | collective-permute-start | bytes 196616 | tf_op jit(solution)/shard_map/ppermute | solution.py:29
  10.6 7.6 %collective-permute-start.4 = (bf16[128,256]{1,0:T(8,128)(2,1)S(1)}, bf16[128,256]{1,0:T(8,128)(2,1)S(1)}, u32[]{:S(2)}, u32[]{:S(2)}) collective-permute-start(bf16[128,256]{1,0:T(8,128)(2,1)S(1)} %get-tuple-element.48), channel_id=1, source_target_pairs={{0,16},{8,24},{16,0},{24,8},{1,17},{9,25},{17,1},{25,9},{2,18},{10... | collective-permute-start | bytes 196616 | tf_op jit(solution)/shard_map/ppermute | solution.py:29
  12.1 6.0 %collective-permute-start.5 = (bf16[128,256]{1,0:T(8,128)(2,1)S(1)}, bf16[128,256]{1,0:T(8,128)(2,1)S(1)}, u32[]{:S(2)}, u32[]{:S(2)}) collective-permute-start(bf16[128,256]{1,0:T(8,128)(2,1)S(1)} %get-tuple-element.47), channel_id=1, source_target_pairs={{0,24},{8,16},{16,8},{24,0},{1,25},{9,17},{17,9},{25,1},{2,26},{10... | collective-permute-start | bytes 196616 | tf_op jit(solution)/shard_map/ppermute | solution.py:29
  14.1 7.6 %collective-permute-start.9 = (bf16[128,256]{1,0:T(8,128)(2,1)S(1)}, bf16[128,256]{1,0:T(8,128)(2,1)S(1)}, u32[]{:S(2)}, u32[]{:S(2)}) collective-permute-start(bf16[128,256]{1,0:T(8,128)(2,1)S(1)} %get-tuple-element.29), channel_id=1, source_target_pairs={{0,8},{8,0},{16,24},{24,16},{1,9},{9,1},{17,25},{25,17},{2,10},{10... | collective-permute-start | bytes 196616 | tf_op jit(solution)/shard_map/ppermute | solution.py:29
  15.5 7.4 %collective-permute-start.10 = (bf16[128,256]{1,0:T(8,128)(2,1)S(1)}, bf16[128,256]{1,0:T(8,128)(2,1)S(1)}, u32[]{:S(2)}, u32[]{:S(2)}) collective-permute-start(bf16[128,256]{1,0:T(8,128)(2,1)S(1)} %get-tuple-element.30), channel_id=1, source_target_pairs={{0,16},{8,24},{16,0},{24,8},{1,17},{9,25},{17,1},{25,9},{2,18},{10... | collective-permute-start | bytes 196616 | tf_op jit(solution)/shard_map/ppermute | solution.py:29
  16.9 6.0 %collective-permute-start.11 = (bf16[128,256]{1,0:T(8,128)(2,1)S(1)}, bf16[128,256]{1,0:T(8,128)(2,1)S(1)}, u32[]{:S(2)}, u32[]{:S(2)}) collective-permute-start(bf16[128,256]{1,0:T(8,128)(2,1)S(1)} %get-tuple-element.31), channel_id=1, source_target_pairs={{0,24},{8,16},{16,8},{24,0},{1,25},{9,17},{17,9},{25,1},{2,26},{10... | collective-permute-start | bytes 196616 | tf_op jit(solution)/shard_map/ppermute | solution.py:29
  18.2 4.8 %copy-start.2 = (f32[4,128,256]{2,1,0:T(8,128)S(1)}, f32[4,128,256]{2,1,0:T(8,128)}, u32[]{:S(2)}) copy-start(f32[4,128,256]{2,1,0:T(8,128)} %get-tuple-element.32.decay) | copy-start | bytes 1572868
  18.2 4.8 %copy-start.3 = (bf16[512,64]{0,1:T(8,128)(2,1)S(1)}, bf16[512,64]{0,1:T(8,128)(2,1)}, u32[]{:S(2)}) copy-start(bf16[512,64]{0,1:T(8,128)(2,1)} %param.11) | copy-start | bytes 196612
  19.3 11.9 %collective-permute-start.6 = (f32[128,256]{1,0:T(8,128)S(1)}, f32[128,256]{1,0:T(8,128)S(1)}, u32[]{:S(2)}, u32[]{:S(2)}) collective-permute-start(f32[128,256]{1,0:T(8,128)S(1)} %get-tuple-element.25.after), channel_id=1, source_target_pairs={{0,8},{8,0},{16,24},{24,16},{1,9},{9,1},{17,25},{25,17},{2,10},{10... | collective-permute-start | bytes 393224 | tf_op jit(solution)/shard_map/ppermute | solution.py:29
  20.3 11.0 %collective-permute-start.7 = (f32[128,256]{1,0:T(8,128)S(1)}, f32[128,256]{1,0:T(8,128)S(1)}, u32[]{:S(2)}, u32[]{:S(2)}) collective-permute-start(f32[128,256]{1,0:T(8,128)S(1)} %get-tuple-element.26), channel_id=1, source_target_pairs={{0,16},{8,24},{16,0},{24,8},{1,17},{9,25},{17,1},{25,9},{2,18},{10... | collective-permute-start | bytes 393224 | tf_op jit(solution)/shard_map/ppermute | solution.py:29
  21.6 9.6 %collective-permute-start.8 = (f32[128,256]{1,0:T(8,128)S(1)}, f32[128,256]{1,0:T(8,128)S(1)}, u32[]{:S(2)}, u32[]{:S(2)}) collective-permute-start(f32[128,256]{1,0:T(8,128)S(1)} %get-tuple-element.27), channel_id=1, source_target_pairs={{0,24},{8,16},{16,8},{24,0},{1,25},{9,17},{17,9},{25,1},{2,26},{10... | collective-permute-start | bytes 393224 | tf_op jit(solution)/shard_map/ppermute | solution.py:29
  23.2 1.3 %collective-permute-start.12 = (bf16[64,256]{1,0:T(8,128)(2,1)S(1)}, bf16[64,256]{1,0:T(8,128)(2,1)S(1)}, u32[]{:S(2)}, u32[]{:S(2)}) collective-permute-start(bf16[64,256]{1,0:T(8,128)(2,1)S(1)} %get-tuple-element.34), channel_id=1, source_target_pairs={{0,1},{1,0},{2,3},{3,2},{4,5},{5,4},{6,7},{7,6},{8,9},{9,8},{10,11... | collective-permute-start | bytes 98312 | tf_op jit(solution)/shard_map/ppermute | solution.py:29
  24.5 5.8 %collective-permute-start.13 = (bf16[64,256]{1,0:T(8,128)(2,1)S(1)}, bf16[64,256]{1,0:T(8,128)(2,1)S(1)}, u32[]{:S(2)}, u32[]{:S(2)}) collective-permute-start(bf16[64,256]{1,0:T(8,128)(2,1)S(1)} %get-tuple-element.36), channel_id=1, source_target_pairs={{0,6},{1,5},{2,4},{3,7},{4,2},{5,1},{6,0},{7,3},{8,14},{9,13},{10,... | collective-permute-start | bytes 98312 | tf_op jit(solution)/shard_map/ppermute | solution.py:221
  27.7 2.6 %collective-permute-start.14 = (bf16[64,256]{1,0:T(8,128)(2,1)S(1)}, bf16[64,256]{1,0:T(8,128)(2,1)S(1)}, u32[]{:S(2)}, u32[]{:S(2)}) collective-permute-start(bf16[64,256]{1,0:T(8,128)(2,1)S(1)} %get-tuple-element.36), channel_id=1, source_target_pairs={{0,0},{1,3},{2,2},{3,1},{4,4},{5,7},{6,6},{7,5},{8,8},{9,11},{10,1... | collective-permute-start | bytes 98312 | tf_op jit(solution)/shard_map/ppermute | solution.py:222
  30.3 1.8 %collective-permute-start.15 = (bf16[64,256]{1,0:T(8,128)(2,1)S(1)}, bf16[64,256]{1,0:T(8,128)(2,1)S(1)}, u32[]{:S(2)}, u32[]{:S(2)}) collective-permute-start(bf16[64,256]{1,0:T(8,128)(2,1)S(1)} %get-tuple-element.39), channel_id=1, source_target_pairs={{0,1},{1,0},{2,3},{3,2},{4,5},{5,4},{6,7},{7,6},{8,9},{9,8},{10,11... | collective-permute-start | bytes 98312 | tf_op jit(solution)/shard_map/ppermute | solution.py:29

commit v5 on v4

--- a/solution.py
+++ b/solution.py
@@ -61,7 +61,7 @@
                 later = (sum_re, sum_im)
         return carry
 
-    lax.fori_loop(0, rows // step, chunk, 0)
+    lax.fori_loop(0, rows // step, chunk, 0, unroll=True)
 
 
 def window_kernel(rows, block, total, rates_ref, f_ref, decay, f_out):
@@ -218,8 +218,8 @@
         compiler_params=small,
         cost_estimate=cost,
     )(partial, xor_permute(partial_sent, "chan", channel_axis, 1))
-    first = lax.ppermute(pair_sent, "chan", [(c, c ^ (4 if c % 2 else 6)) for c in range(channel_axis)])
-    second = lax.ppermute(pair_sent, "chan", [(c, c ^ (2 if c % 2 else 0)) for c in range(channel_axis)])
+    first = lax.ppermute(pair_sent, "chan", [(c, c ^ (2 if c % 2 else 6)) for c in range(channel_axis)])
+    second = lax.ppermute(pair_sent, "chan", [(c, c ^ (4 if c % 2 else 0)) for c in range(channel_axis)])
     half_sum, half_sent = pl.pallas_call(
         sum_kernel,
         out_shape=[shape((hidden, block), F32), shape((hidden, block), BF16)],

time: 33 us -> 32.9 us (level)
  no operation moved by 1% of the time
where the time goes in v5:
time: 32.9 us; the launch traced here: 32.7 us
  starting transfers between devices  20.6 us (63%)
  Pallas kernels  5.7 us (17%)
  waiting for transfers between devices  3.82 us (12%)
  other arithmetic  1.16 us (4%)
  between operations  0.75 us (2%)
  local copies, waits for them, and re-layouts  0.67 us (2%)
    ppermute x14, starting transfers between devices, xor_permute(): return lax.ppermute(value, axis, [(j, j ^ k) for j in range(size)])  16.7 us
    ppermute x1, starting transfers between devices, body_four(): lax.ppermute(pair_sent, 'chan', [(c, c ^ (2 if c % 2 else 6)) for c in ra...  3.26 us
    ppermute x14, waiting for transfers between devices, xor_permute(): return lax.ppermute(value, axis, [(j, j ^ k) for j in range(size)])  2.8 us
    pallas_call x1, Pallas kernels, body_four(): pl.pallas_call(functools.partial(window_kernel, rows, block, total), out_...  1.63 us
    another operation x1, other arithmetic, body_four(): jnp.stack([value.reshape(4, rows, block) for value in (grad_out, inputs)]...  1.16 us
    pallas_call x1, Pallas kernels, body_four(): pl.pallas_call(functools.partial(input_kernel, rows), out_shape=[shape((r...  1.1 us
    pallas_call x1, Pallas kernels, body_four(): pl.pallas_call(functools.partial(filter_kernel, rows), out_shape=[shape((...  1.09 us
    ppermute x1, waiting for transfers between devices, body_four(): lax.ppermute(pair_sent, 'chan', [(c, c ^ (2 if c % 2 else 6)) for c in ra...  1.02 us
  transfers between devices with their start and end apart: 16, of which 5 were waited for; matrix products, arithmetic and copies ran while one was open for 2% of the time, Pallas kernels for 15%

profile of v5, /device:TPU:0, one launch (start us, length us, event | category | flops | bytes accessed | tf_op | source)
XLA Modules:
  0.0 32.7 jit_solution(13836160395941761040)
XLA Ops:
  0.7 0.0 copy-start.4
  0.7 1.2 %fusion = (bf16[1,2,128,256]{3,2,1,0:T(8,128)(2,1)S(1)}, bf16[1,2,128,256]{3,2,1,0:T(8,128)(2,1)S(1)}, bf16[1,2,128,256]{3,2,1,0:T(8,128)(2,1)S(1)}, bf16[1,2,128,256]{3,2,1,0:T(8,128)(2,1)S(1)}) fusion(s32[]{:T(128)S(6)} %select_n.21, bf16[4,1,128,256]{3,2,1,0:T(8,128)(2,1)} %bitcast.27, bf16[4,1,128,256]{3,2,1,0:T(8,128)(2,1)} %bitcast.28, ...), kind=kLoop, calls=%fused_computation.8 | loop fusion | flops 262144 | bytes 1048592 | tf_op jit(solution)/shard_map/stack | solution.py:159
  1.8 3.0 %collective-permute-start = (bf16[256,256]{1,0:T(8,128)(2,1)S(1)}, bf16[256,256]{1,0:T(8,128)(2,1)S(1)}, u32[]{:S(2)}, u32[]{:S(2)}) collective-permute-start(bf16[256,256]{1,0:T(8,128)(2,1)S(1)} %bitcast.31), channel_id=1, source_target_pairs={{0,8},{8,0},{16,24},{24,16},{1,9},{9,1},{17,25},{25,17},{2,10},{10... | collective-permute-start | bytes 393224 | tf_op jit(solution)/shard_map/ppermute | solution.py:29
  4.8 1.5 %collective-permute-start.1 = (bf16[256,256]{1,0:T(8,128)(2,1)S(1)}, bf16[256,256]{1,0:T(8,128)(2,1)S(1)}, u32[]{:S(2)}, u32[]{:S(2)}) collective-permute-start(bf16[256,256]{1,0:T(8,128)(2,1)S(1)} %bitcast.30), channel_id=1, source_target_pairs={{0,16},{8,24},{16,0},{24,8},{1,17},{9,25},{17,1},{25,9},{2,18},{10... | collective-permute-start | bytes 393224 | tf_op jit(solution)/shard_map/ppermute | solution.py:29
  6.3 0.0 collective-permute-start.2
  6.4 0.0 copy-done.4
  6.4 0.0 copy-start
  6.4 0.6 %dynamic-slice_bitcast_fusion = (bf16[128,256]{1,0:T(8,128)(2,1)S(1)}, bf16[128,256]{1,0:T(8,128)(2,1)S(1)}, bf16[128,256]{1,0:T(8,128)(2,1)}, bf16[128,256]{1,0:T(8,128)(2,1)S(1)}) fusion(bf16[4,128,256]{2,1,0:T(8,128)(2,1)S(1)} %bitcast.26, s32[]{:T(128)S(6)} %select_n.21, s32[]{:T(128)S(6)} %select_n.20, s32[]{:T(128)S(6)} %select_n.19, s32[]{:T(128)S(6)} %select_n.18), kind=kLoop, calls=%fused_computation.12 | loop fusion | bytes 524304 | tf_op jit(solution)/shard_map/jit(dynamic_index_in_dim)/squeeze | solution.py:161
  7.0 1.6 %shard_map.94 = (f32[4,128,256]{2,1,0:T(8,128)}, bf16[128,256]{1,0:T(8,128)(2,1)}) custom-call(f32[1,512]{1,0:T(1,128)} %bitcast.32, bf16[128,256]{1,0:T(8,128)(2,1)} %get-tuple-element.49.f_ref), custom_call_target="tpu_custom_call", output_to_operand_aliasing={{1}: (1, {})} | custom-call | flops 1000 | bytes 1000 | tf_op jit(solution)/shard_map/pallas_call | solution.py:163
  8.7 1.9 %collective-permute-start.3 = (bf16[128,256]{1,0:T(8,128)(2,1)}, bf16[128,256]{1,0:T(8,128)(2,1)S(1)}, u32[]{:S(2)}, u32[]{:S(2)}) collective-permute-start(bf16[128,256]{1,0:T(8,128)(2,1)} %get-tuple-element.23), channel_id=1, source_target_pairs={{0,8},{8,0},{16,24},{24,16},{1,9},{9,1},{17,25},{25,17},{2,10},{10... | collective-permute-start | bytes 196616 | tf_op jit(solution)/shard_map/ppermute | solution.py:29
  10.6 1.5 %collective-permute-start.4 = (bf16[128,256]{1,0:T(8,128)(2,1)S(1)}, bf16[128,256]{1,0:T(8,128)(2,1)S(1)}, u32[]{:S(2)}, u32[]{:S(2)}) collective-permute-start(bf16[128,256]{1,0:T(8,128)(2,1)S(1)} %get-tuple-element.48), channel_id=1, source_target_pairs={{0,16},{8,24},{16,0},{24,8},{1,17},{9,25},{17,1},{25,9},{2,18},{10... | collective-permute-start | bytes 196616 | tf_op jit(solution)/shard_map/ppermute | solution.py:29
  12.1 0.0 collective-permute-done.s1
  12.1 0.0 collective-permute-start.5
  12.2 0.3 %collective-permute-done.1.s2 = bf16[256,256]{1,0:T(8,128)(2,1)S(1)} collective-permute-done((bf16[256,256]{1,0:T(8,128)(2,1)S(1)}, bf16[256,256]{1,0:T(8,128)(2,1)S(1)}, u32[]{:S(2)}, u32[]{:S(2)}) %collective-permute-start.1) | collective-permute-done | bytes 131104 | tf_op jit(solution)/shard_map/ppermute | solution.py:29
  12.5 0.4 %collective-permute-done.2.s3 = bf16[256,256]{1,0:T(8,128)(2,1)S(1)} collective-permute-done((bf16[256,256]{1,0:T(8,128)(2,1)S(1)}, bf16[256,256]{1,0:T(8,128)(2,1)S(1)}, u32[]{:S(2)}, u32[]{:S(2)}) %collective-permute-start.2) | collective-permute-done | bytes 131104 | tf_op jit(solution)/shard_map/ppermute | solution.py:29
  12.9 0.0 copy-done
  12.9 0.0 copy-done.1
  12.9 1.1 %shard_map.96 = (f32[128,256]{1,0:T(8,128)S(1)}, bf16[128,256]{1,0:T(8,128)(2,1)S(1)}, bf16[128,256]{1,0:T(8,128)(2,1)S(1)}, bf16[128,256]{1,0:T(8,128)(2,1)S(1)}) custom-call(bf16[256,256]{1,0:T(8,128)(2,1)S(1)} %bitcast.23, bf16[256,256]{1,0:T(8,128)(2,1)S(1)} %collective-permute-done.s1, bf16[256,256]{1,0:T(8,128)(2,1)S(1)} %collective-permute-done.1.s2, ...), custom_call_target="tpu_custom_call" | custom-call | flops 1000 | bytes 1000 | tf_op jit(solution)/shard_map/pallas_call | solution.py:175
  14.0 1.4 %collective-permute-start.9 = (bf16[128,256]{1,0:T(8,128)(2,1)S(1)}, bf16[128,256]{1,0:T(8,128)(2,1)S(1)}, u32[]{:S(2)}, u32[]{:S(2)}) collective-permute-start(bf16[128,256]{1,0:T(8,128)(2,1)S(1)} %get-tuple-element.29), channel_id=1, source_target_pairs={{0,8},{8,0},{16,24},{24,16},{1,9},{9,1},{17,25},{25,17},{2,10},{10... | collective-permute-start | bytes 196616 | tf_op jit(solution)/shard_map/ppermute | solution.py:29
  15.4 1.4 %collective-permute-start.10 = (bf16[128,256]{1,0:T(8,128)(2,1)S(1)}, bf16[128,256]{1,0:T(8,128)(2,1)S(1)}, u32[]{:S(2)}, u32[]{:S(2)}) collective-permute-start(bf16[128,256]{1,0:T(8,128)(2,1)S(1)} %get-tuple-element.30), channel_id=1, source_target_pairs={{0,16},{8,24},{16,0},{24,8},{1,17},{9,25},{17,1},{25,9},{2,18},{10... | collective-permute-start | bytes 196616 | tf_op jit(solution)/shard_map/ppermute | solution.py:29
  16.8 0.0 collective-permute-done.3.f1
  16.8 1.3 %collective-permute-start.11 = (bf16[128,256]{1,0:T(8,128)(2,1)S(1)}, bf16[128,256]{1,0:T(8,128)(2,1)S(1)}, u32[]{:S(2)}, u32[]{:S(2)}) collective-permute-start(bf16[128,256]{1,0:T(8,128)(2,1)S(1)} %get-tuple-element.31), channel_id=1, source_target_pairs={{0,24},{8,16},{16,8},{24,0},{1,25},{9,17},{17,9},{25,1},{2,26},{10... | collective-permute-start | bytes 196616 | tf_op jit(solution)/shard_map/ppermute | solution.py:29
  18.1 0.0 collective-permute-done.4.f2
  18.1 0.0 collective-permute-done.5.f3
  18.1 0.0 copy-start.3
  18.1 1.1 %shard_map.95 = (f32[128,256]{1,0:T(8,128)S(1)}, f32[128,256]{1,0:T(8,128)S(1)}, f32[128,256]{1,0:T(8,128)S(1)}, f32[128,256]{1,0:T(8,128)S(1)}) custom-call(bf16[256,256]{1,0:T(8,128)(2,1)S(1)} %bitcast.24, bf16[256,256]{1,0:T(8,128)(2,1)S(1)} %collective-permute-done.s1, bf16[256,256]{1,0:T(8,128)(2,1)S(1)} %collective-permute-done.1.s2, ...), custom_call_target="tpu_custom_call" | custom-call | flops 1000 | bytes 1000 | tf_op jit(solution)/shard_map/pallas_call | solution.py:186
  19.2 0.9 %collective-permute-start.6 = (f32[128,256]{1,0:T(8,128)S(1)}, f32[128,256]{1,0:T(8,128)S(1)}, u32[]{:S(2)}, u32[]{:S(2)}) collective-permute-start(f32[128,256]{1,0:T(8,128)S(1)} %get-tuple-element.25.after), channel_id=1, source_target_pairs={{0,8},{8,0},{16,24},{24,16},{1,9},{9,1},{17,25},{25,17},{2,10},{10... | collective-permute-start | bytes 393224 | tf_op jit(solution)/shard_map/ppermute | solution.py:29
  20.1 1.4 %collective-permute-start.7 = (f32[128,256]{1,0:T(8,128)S(1)}, f32[128,256]{1,0:T(8,128)S(1)}, u32[]{:S(2)}, u32[]{:S(2)}) collective-permute-start(f32[128,256]{1,0:T(8,128)S(1)} %get-tuple-element.26), channel_id=1, source_target_pairs={{0,16},{8,24},{16,0},{24,8},{1,17},{9,25},{17,1},{25,9},{2,18},{10... | collective-permute-start | bytes 393224 | tf_op jit(solution)/shard_map/ppermute | solution.py:29
  21.5 0.0 collective-permute-done.9.w1
  21.5 1.3 %collective-permute-start.8 = (f32[128,256]{1,0:T(8,128)S(1)}, f32[128,256]{1,0:T(8,128)S(1)}, u32[]{:S(2)}, u32[]{:S(2)}) collective-permute-start(f32[128,256]{1,0:T(8,128)S(1)} %get-tuple-element.27), channel_id=1, source_target_pairs={{0,24},{8,16},{16,8},{24,0},{1,25},{9,17},{17,9},{25,1},{2,26},{10... | collective-permute-start | bytes 393224 | tf_op jit(solution)/shard_map/ppermute | solution.py:29
  22.8 0.0 collective-permute-done.10.w2
  22.8 0.0 collective-permute-done.11.w3
  22.8 0.0 copy-done.2
  22.8 0.0 copy-done.3
  22.8 0.3 shard_map.97
  23.1 0.1 collective-permute-start.12
  23.1 1.2 %collective-permute-done.12.other = bf16[64,256]{1,0:T(8,128)(2,1)S(1)} collective-permute-done((bf16[64,256]{1,0:T(8,128)(2,1)S(1)}, bf16[64,256]{1,0:T(8,128)(2,1)S(1)}, u32[]{:S(2)}, u32[]{:S(2)}) %collective-permute-start.12) | collective-permute-done | bytes 32800 | tf_op jit(solution)/shard_map/ppermute | solution.py:29
  24.3 3.3 %collective-permute-start.13 = (bf16[64,256]{1,0:T(8,128)(2,1)S(1)}, bf16[64,256]{1,0:T(8,128)(2,1)S(1)}, u32[]{:S(2)}, u32[]{:S(2)}) collective-permute-start(bf16[64,256]{1,0:T(8,128)(2,1)S(1)} %get-tuple-element.36), channel_id=1, source_target_pairs={{0,6},{1,3},{2,4},{3,1},{4,2},{5,7},{6,0},{7,5},{8,14},{9,11},{10,... | collective-permute-start | bytes 98312 | tf_op jit(solution)/shard_map/ppermute | solution.py:221
  27.6 0.7 %collective-permute-start.14 = (bf16[64,256]{1,0:T(8,128)(2,1)S(1)}, bf16[64,256]{1,0:T(8,128)(2,1)S(1)}, u32[]{:S(2)}, u32[]{:S(2)}) collective-permute-start(bf16[64,256]{1,0:T(8,128)(2,1)S(1)} %get-tuple-element.36), channel_id=1, source_target_pairs={{0,0},{1,5},{2,2},{3,7},{4,4},{5,1},{6,6},{7,3},{8,8},{9,13},{10,1... | collective-permute-start | bytes 98312 | tf_op jit(solution)/shard_map/ppermute | solution.py:222
  28.3 0.8 %shard_map.99 = (f32[4,128,256]{2,1,0:T(8,128)}, f32[8,128]{1,0:T(8,128)S(1)}) custom-call(f32[128,256]{1,0:T(8,128)S(1)} %get-tuple-element.28.w0, bf16[128,256]{1,0:T(8,128)(2,1)S(1)} %collective-permute-done.9.w1, bf16[128,256]{1,0:T(8,128)(2,1)S(1)} %collective-permute-done.10.w2, bf16[128,256]{1,0:T(8,128)(2,1)S(1)} %collective-permute-done.11.w3), custom_call_target="tpu_custom_call" | custom-call | flops 1000 | bytes 1000 | tf_op jit(solution)/shard_map/pallas_call | solution.py:205
  29.1 1.0 %collective-permute-done.13.first = bf16[64,256]{1,0:T(8,128)(2,1)S(1)} collective-permute-done((bf16[64,256]{1,0:T(8,128)(2,1)S(1)}, bf16[64,256]{1,0:T(8,128)(2,1)S(1)}, u32[]{:S(2)}, u32[]{:S(2)}) %collective-permute-start.13) | collective-permute-done | bytes 32800 | tf_op jit(solution)/shard_map/ppermute | solution.py:221
  30.1 0.0 collective-permute-done.14.second
  30.2 1.0 %collective-permute-start.15 = (bf16[64,256]{1,0:T(8,128)(2,1)S(1)}, bf16[64,256]{1,0:T(8,128)(2,1)S(1)}, u32[]{:S(2)}, u32[]{:S(2)}) collective-permute-start(bf16[64,256]{1,0:T(8,128)(2,1)S(1)} %get-tuple-element.39), channel_id=1, source_target_pairs={{0,1},{1,0},{2,3},{3,2},{4,5},{5,4},{6,7},{7,6},{8,9},{9,8},{10,11... | collective-permute-start | bytes 98312 | tf_op jit(solution)/shard_map/ppermute | solution.py:29
  31.1 0.0 collective-permute-done.6.v1
  31.1 0.0 collective-permute-done.7.v2
  31.1 0.0 collective-permute-done.8.v3
  31.1 0.8 %collective-permute-done.15.other = bf16[64,256]{1,0:T(8,128)(2,1)S(1)} collective-permute-done((bf16[64,256]{1,0:T(8,128)(2,1)S(1)}, bf16[64,256]{1,0:T(8,128)(2,1)S(1)}, u32[]{:S(2)}, u32[]{:S(2)}) %collective-permute-start.15) | collective-permute-done | bytes 32800 | tf_op jit(solution)/shard_map/ppermute | solution.py:29
  32.0 0.8 %shard_map.101 = (bf16[4,128,256]{2,1,0:T(8,128)(2,1)}, f32[64,256]{1,0:T(8,128)}) custom-call(f32[128,256]{1,0:T(8,128)S(1)} %get-tuple-element.24.v0, f32[128,256]{1,0:T(8,128)S(1)} %collective-permute-done.6.v1, f32[128,256]{1,0:T(8,128)S(1)} %collective-permute-done.7.v2, f32[128,256]{1,0:T(8,128)S(1)} %collective-permute-done.8.v3, ...), custom_call_target="tpu_custom_call" | custom-call | flops 1000 | bytes 1000 | tf_op jit(solution)/shard_map/pallas_call | solution.py:233
  (4 shorter events, 0.0 us)
Async XLA Ops:
  0.7 5.7 %copy-start.4 = (bf16[512,256]{1,0:T(8,128)(2,1)S(1)}, bf16[512,256]{1,0:T(8,128)(2,1)}, u32[]{:S(2)}) copy-start(bf16[512,256]{1,0:T(8,128)(2,1)} %param.9) | copy-start | bytes 786436
  1.8 10.3 %collective-permute-start = (bf16[256,256]{1,0:T(8,128)(2,1)S(1)}, bf16[256,256]{1,0:T(8,128)(2,1)S(1)}, u32[]{:S(2)}, u32[]{:S(2)}) collective-permute-start(bf16[256,256]{1,0:T(8,128)(2,1)S(1)} %bitcast.31), channel_id=1, source_target_pairs={{0,8},{8,0},{16,24},{24,16},{1,9},{9,1},{17,25},{25,17},{2,10},{10... | collective-permute-start | bytes 393224 | tf_op jit(solution)/shard_map/ppermute | solution.py:29
  4.8 7.7 %collective-permute-start.1 = (bf16[256,256]{1,0:T(8,128)(2,1)S(1)}, bf16[256,256]{1,0:T(8,128)(2,1)S(1)}, u32[]{:S(2)}, u32[]{:S(2)}) collective-permute-start(bf16[256,256]{1,0:T(8,128)(2,1)S(1)} %bitcast.30), channel_id=1, source_target_pairs={{0,16},{8,24},{16,0},{24,8},{1,17},{9,25},{17,1},{25,9},{2,18},{10... | collective-permute-start | bytes 393224 | tf_op jit(solution)/shard_map/ppermute | solution.py:29
  6.3 6.6 %collective-permute-start.2 = (bf16[256,256]{1,0:T(8,128)(2,1)S(1)}, bf16[256,256]{1,0:T(8,128)(2,1)S(1)}, u32[]{:S(2)}, u32[]{:S(2)}) collective-permute-start(bf16[256,256]{1,0:T(8,128)(2,1)S(1)} %bitcast.29), channel_id=1, source_target_pairs={{0,24},{8,16},{16,8},{24,0},{1,25},{9,17},{17,9},{25,1},{2,26},{10... | collective-permute-start | bytes 393224 | tf_op jit(solution)/shard_map/ppermute | solution.py:29
  6.4 6.5 %copy-start = (bf16[256,512]{1,0:T(8,128)(2,1)S(1)}, bf16[256,512]{1,0:T(8,128)(2,1)}, u32[]{:S(2)}) copy-start(bf16[256,512]{1,0:T(8,128)(2,1)} %constant.37.clone.table) | copy-start | bytes 786436
  6.4 6.5 %copy-start.1 = (bf16[512,256]{1,0:T(8,128)(2,1)S(1)}, bf16[512,256]{1,0:T(8,128)(2,1)}, u32[]{:S(2)}) copy-start(bf16[512,256]{1,0:T(8,128)(2,1)} %constant.38.clone.back) | copy-start | bytes 786436
  8.7 8.1 %collective-permute-start.3 = (bf16[128,256]{1,0:T(8,128)(2,1)}, bf16[128,256]{1,0:T(8,128)(2,1)S(1)}, u32[]{:S(2)}, u32[]{:S(2)}) collective-permute-start(bf16[128,256]{1,0:T(8,128)(2,1)} %get-tuple-element.23), channel_id=1, source_target_pairs={{0,8},{8,0},{16,24},{24,16},{1,9},{9,1},{17,25},{25,17},{2,10},{10... | collective-permute-start | bytes 196616 | tf_op jit(solution)/shard_map/ppermute | solution.py:29
  10.6 7.5 %collective-permute-start.4 = (bf16[128,256]{1,0:T(8,128)(2,1)S(1)}, bf16[128,256]{1,0:T(8,128)(2,1)S(1)}, u32[]{:S(2)}, u32[]{:S(2)}) collective-permute-start(bf16[128,256]{1,0:T(8,128)(2,1)S(1)} %get-tuple-element.48), channel_id=1, source_target_pairs={{0,16},{8,24},{16,0},{24,8},{1,17},{9,25},{17,1},{25,9},{2,18},{10... | collective-permute-start | bytes 196616 | tf_op jit(solution)/shard_map/ppermute | solution.py:29
  12.1 6.0 %collective-permute-start.5 = (bf16[128,256]{1,0:T(8,128)(2,1)S(1)}, bf16[128,256]{1,0:T(8,128)(2,1)S(1)}, u32[]{:S(2)}, u32[]{:S(2)}) collective-permute-start(bf16[128,256]{1,0:T(8,128)(2,1)S(1)} %get-tuple-element.47), channel_id=1, source_target_pairs={{0,24},{8,16},{16,8},{24,0},{1,25},{9,17},{17,9},{25,1},{2,26},{10... | collective-permute-start | bytes 196616 | tf_op jit(solution)/shard_map/ppermute | solution.py:29
  14.0 7.5 %collective-permute-start.9 = (bf16[128,256]{1,0:T(8,128)(2,1)S(1)}, bf16[128,256]{1,0:T(8,128)(2,1)S(1)}, u32[]{:S(2)}, u32[]{:S(2)}) collective-permute-start(bf16[128,256]{1,0:T(8,128)(2,1)S(1)} %get-tuple-element.29), channel_id=1, source_target_pairs={{0,8},{8,0},{16,24},{24,16},{1,9},{9,1},{17,25},{25,17},{2,10},{10... | collective-permute-start | bytes 196616 | tf_op jit(solution)/shard_map/ppermute | solution.py:29
  15.4 7.4 %collective-permute-start.10 = (bf16[128,256]{1,0:T(8,128)(2,1)S(1)}, bf16[128,256]{1,0:T(8,128)(2,1)S(1)}, u32[]{:S(2)}, u32[]{:S(2)}) collective-permute-start(bf16[128,256]{1,0:T(8,128)(2,1)S(1)} %get-tuple-element.30), channel_id=1, source_target_pairs={{0,16},{8,24},{16,0},{24,8},{1,17},{9,25},{17,1},{25,9},{2,18},{10... | collective-permute-start | bytes 196616 | tf_op jit(solution)/shard_map/ppermute | solution.py:29
  16.8 6.0 %collective-permute-start.11 = (bf16[128,256]{1,0:T(8,128)(2,1)S(1)}, bf16[128,256]{1,0:T(8,128)(2,1)S(1)}, u32[]{:S(2)}, u32[]{:S(2)}) collective-permute-start(bf16[128,256]{1,0:T(8,128)(2,1)S(1)} %get-tuple-element.31), channel_id=1, source_target_pairs={{0,24},{8,16},{16,8},{24,0},{1,25},{9,17},{17,9},{25,1},{2,26},{10... | collective-permute-start | bytes 196616 | tf_op jit(solution)/shard_map/ppermute | solution.py:29
  18.1 4.7 %copy-start.2 = (f32[4,128,256]{2,1,0:T(8,128)S(1)}, f32[4,128,256]{2,1,0:T(8,128)}, u32[]{:S(2)}) copy-start(f32[4,128,256]{2,1,0:T(8,128)} %get-tuple-element.32.decay) | copy-start | bytes 1572868
  18.1 4.7 %copy-start.3 = (bf16[512,64]{0,1:T(8,128)(2,1)S(1)}, bf16[512,64]{0,1:T(8,128)(2,1)}, u32[]{:S(2)}) copy-start(bf16[512,64]{0,1:T(8,128)(2,1)} %param.11) | copy-start | bytes 196612
  19.2 11.9 %collective-permute-start.6 = (f32[128,256]{1,0:T(8,128)S(1)}, f32[128,256]{1,0:T(8,128)S(1)}, u32[]{:S(2)}, u32[]{:S(2)}) collective-permute-start(f32[128,256]{1,0:T(8,128)S(1)} %get-tuple-element.25.after), channel_id=1, source_target_pairs={{0,8},{8,0},{16,24},{24,16},{1,9},{9,1},{17,25},{25,17},{2,10},{10... | collective-permute-start | bytes 393224 | tf_op jit(solution)/shard_map/ppermute | solution.py:29
  20.1 11.0 %collective-permute-start.7 = (f32[128,256]{1,0:T(8,128)S(1)}, f32[128,256]{1,0:T(8,128)S(1)}, u32[]{:S(2)}, u32[]{:S(2)}) collective-permute-start(f32[128,256]{1,0:T(8,128)S(1)} %get-tuple-element.26), channel_id=1, source_target_pairs={{0,16},{8,24},{16,0},{24,8},{1,17},{9,25},{17,1},{25,9},{2,18},{10... | collective-permute-start | bytes 393224 | tf_op jit(solution)/shard_map/ppermute | solution.py:29
  21.5 9.6 %collective-permute-start.8 = (f32[128,256]{1,0:T(8,128)S(1)}, f32[128,256]{1,0:T(8,128)S(1)}, u32[]{:S(2)}, u32[]{:S(2)}) collective-permute-start(f32[128,256]{1,0:T(8,128)S(1)} %get-tuple-element.27), channel_id=1, source_target_pairs={{0,24},{8,16},{16,8},{24,0},{1,25},{9,17},{17,9},{25,1},{2,26},{10... | collective-permute-start | bytes 393224 | tf_op jit(solution)/shard_map/ppermute | solution.py:29
  23.1 1.3 %collective-permute-start.12 = (bf16[64,256]{1,0:T(8,128)(2,1)S(1)}, bf16[64,256]{1,0:T(8,128)(2,1)S(1)}, u32[]{:S(2)}, u32[]{:S(2)}) collective-permute-start(bf16[64,256]{1,0:T(8,128)(2,1)S(1)} %get-tuple-element.34), channel_id=1, source_target_pairs={{0,1},{1,0},{2,3},{3,2},{4,5},{5,4},{6,7},{7,6},{8,9},{9,8},{10,11... | collective-permute-start | bytes 98312 | tf_op jit(solution)/shard_map/ppermute | solution.py:29
  24.3 5.8 %collective-permute-start.13 = (bf16[64,256]{1,0:T(8,128)(2,1)S(1)}, bf16[64,256]{1,0:T(8,128)(2,1)S(1)}, u32[]{:S(2)}, u32[]{:S(2)}) collective-permute-start(bf16[64,256]{1,0:T(8,128)(2,1)S(1)} %get-tuple-element.36), channel_id=1, source_target_pairs={{0,6},{1,3},{2,4},{3,1},{4,2},{5,7},{6,0},{7,5},{8,14},{9,11},{10,... | collective-permute-start | bytes 98312 | tf_op jit(solution)/shard_map/ppermute | solution.py:221
  27.6 2.5 %collective-permute-start.14 = (bf16[64,256]{1,0:T(8,128)(2,1)S(1)}, bf16[64,256]{1,0:T(8,128)(2,1)S(1)}, u32[]{:S(2)}, u32[]{:S(2)}) collective-permute-start(bf16[64,256]{1,0:T(8,128)(2,1)S(1)} %get-tuple-element.36), channel_id=1, source_target_pairs={{0,0},{1,5},{2,2},{3,7},{4,4},{5,1},{6,6},{7,3},{8,8},{9,13},{10,1... | collective-permute-start | bytes 98312 | tf_op jit(solution)/shard_map/ppermute | solution.py:222
  30.2 1.8 %collective-permute-start.15 = (bf16[64,256]{1,0:T(8,128)(2,1)S(1)}, bf16[64,256]{1,0:T(8,128)(2,1)S(1)}, u32[]{:S(2)}, u32[]{:S(2)}) collective-permute-start(bf16[64,256]{1,0:T(8,128)(2,1)S(1)} %get-tuple-element.39), channel_id=1, source_target_pairs={{0,1},{1,0},{2,3},{3,2},{4,5},{5,4},{6,7},{7,6},{8,9},{9,8},{10,11... | collective-permute-start | bytes 98312 | tf_op jit(solution)/shard_map/ppermute | solution.py:29

commit v6 on v5

--- a/solution.py
+++ b/solution.py
@@ -92,7 +92,7 @@
         spec_z[me ^ k] = dot(f[...], table[...])
     correlate(rows, table.shape[0], spec_g, spec_z, prod)
     for k, out in enumerate(outs):
-        out[...] = dot(prod[me ^ k], back[...])
+        out[...] = dot(prod[me ^ k], back[...]).astype(out.dtype)
 
 
 def hidden_kernel(rows, w0, w1, w2, w3, decay, mix, after, hidden, sent):
@@ -185,7 +185,7 @@
 
     made_in = pl.pallas_call(
         functools.partial(input_kernel, rows),
-        out_shape=[shape((rows, block), F32)] * 4,
+        out_shape=[shape((rows, block), BF16)] + [shape((rows, block), F32)] * 3,
         in_specs=[vmem] * 10,
         out_specs=[vmem] * 4,
         scratch_shapes=scratch,

time: 32.9 us -> 32.9 us (level)
  no operation moved by 1% of the time
where the time goes in v6:
time: 32.9 us; the launch traced here: 32.7 us
  starting transfers between devices  20.6 us (63%)
  Pallas kernels  5.7 us (17%)
  waiting for transfers between devices  3.82 us (12%)
  other arithmetic  1.16 us (4%)
  between operations  0.75 us (2%)
  local copies, waits for them, and re-layouts  0.67 us (2%)
    ppermute x14, starting transfers between devices, xor_permute(): return lax.ppermute(value, axis, [(j, j ^ k) for j in range(size)])  16.7 us
    ppermute x1, starting transfers between devices, body_four(): lax.ppermute(pair_sent, 'chan', [(c, c ^ (2 if c % 2 else 6)) for c in ra...  3.26 us
    ppermute x14, waiting for transfers between devices, xor_permute(): return lax.ppermute(value, axis, [(j, j ^ k) for j in range(size)])  2.8 us
    pallas_call x1, Pallas kernels, body_four(): pl.pallas_call(functools.partial(window_kernel, rows, block, total), out_...  1.63 us
    another operation x1, other arithmetic, body_four(): jnp.stack([value.reshape(4, rows, block) for value in (grad_out, inputs)]...  1.16 us
    pallas_call x1, Pallas kernels, body_four(): pl.pallas_call(functools.partial(input_kernel, rows), out_shape=[shape((r...  1.1 us
    pallas_call x1, Pallas kernels, body_four(): pl.pallas_call(functools.partial(filter_kernel, rows), out_shape=[shape((...  1.09 us
    ppermute x1, waiting for transfers between devices, body_four(): lax.ppermute(pair_sent, 'chan', [(c, c ^ (2 if c % 2 else 6)) for c in ra...  1.02 us
  transfers between devices with their start and end apart: 16, of which 5 were waited for; matrix products, arithmetic and copies ran while one was open for 2% of the time, Pallas kernels for 15%

profile of v6, /device:TPU:0, one launch (start us, length us, event | category | flops | bytes accessed | tf_op | source)
XLA Modules:
  0.0 32.7 jit_solution(1639112995635390146)
XLA Ops:
  0.7 0.0 copy-start.4
  0.7 1.2 %fusion = (bf16[1,2,128,256]{3,2,1,0:T(8,128)(2,1)S(1)}, bf16[1,2,128,256]{3,2,1,0:T(8,128)(2,1)S(1)}, bf16[1,2,128,256]{3,2,1,0:T(8,128)(2,1)S(1)}, bf16[1,2,128,256]{3,2,1,0:T(8,128)(2,1)S(1)}) fusion(s32[]{:T(128)S(6)} %select_n.21, bf16[4,1,128,256]{3,2,1,0:T(8,128)(2,1)} %bitcast.27, bf16[4,1,128,256]{3,2,1,0:T(8,128)(2,1)} %bitcast.28, ...), kind=kLoop, calls=%fused_computation.8 | loop fusion | flops 262144 | bytes 1048592 | tf_op jit(solution)/shard_map/stack | solution.py:159
  1.8 3.0 %collective-permute-start = (bf16[256,256]{1,0:T(8,128)(2,1)S(1)}, bf16[256,256]{1,0:T(8,128)(2,1)S(1)}, u32[]{:S(2)}, u32[]{:S(2)}) collective-permute-start(bf16[256,256]{1,0:T(8,128)(2,1)S(1)} %bitcast.31), channel_id=1, source_target_pairs={{0,8},{8,0},{16,24},{24,16},{1,9},{9,1},{17,25},{25,17},{2,10},{10... | collective-permute-start | bytes 393224 | tf_op jit(solution)/shard_map/ppermute | solution.py:29
  4.8 1.5 %collective-permute-start.1 = (bf16[256,256]{1,0:T(8,128)(2,1)S(1)}, bf16[256,256]{1,0:T(8,128)(2,1)S(1)}, u32[]{:S(2)}, u32[]{:S(2)}) collective-permute-start(bf16[256,256]{1,0:T(8,128)(2,1)S(1)} %bitcast.30), channel_id=1, source_target_pairs={{0,16},{8,24},{16,0},{24,8},{1,17},{9,25},{17,1},{25,9},{2,18},{10... | collective-permute-start | bytes 393224 | tf_op jit(solution)/shard_map/ppermute | solution.py:29
  6.3 0.0 collective-permute-start.2
  6.4 0.0 copy-done.4
  6.4 0.0 copy-start
  6.4 0.6 %dynamic-slice_bitcast_fusion = (bf16[128,256]{1,0:T(8,128)(2,1)S(1)}, bf16[128,256]{1,0:T(8,128)(2,1)S(1)}, bf16[128,256]{1,0:T(8,128)(2,1)}, bf16[128,256]{1,0:T(8,128)(2,1)S(1)}) fusion(bf16[4,128,256]{2,1,0:T(8,128)(2,1)S(1)} %bitcast.26, s32[]{:T(128)S(6)} %select_n.21, s32[]{:T(128)S(6)} %select_n.20, s32[]{:T(128)S(6)} %select_n.19, s32[]{:T(128)S(6)} %select_n.18), kind=kLoop, calls=%fused_computation.12 | loop fusion | bytes 524304 | tf_op jit(solution)/shard_map/jit(dynamic_index_in_dim)/squeeze | solution.py:161
  7.0 1.6 %shard_map.94 = (f32[4,128,256]{2,1,0:T(8,128)}, bf16[128,256]{1,0:T(8,128)(2,1)}) custom-call(f32[1,512]{1,0:T(1,128)} %bitcast.32, bf16[128,256]{1,0:T(8,128)(2,1)} %get-tuple-element.49.f_ref), custom_call_target="tpu_custom_call", output_to_operand_aliasing={{1}: (1, {})} | custom-call | flops 1000 | bytes 1000 | tf_op jit(solution)/shard_map/pallas_call | solution.py:163
  8.7 1.9 %collective-permute-start.3 = (bf16[128,256]{1,0:T(8,128)(2,1)}, bf16[128,256]{1,0:T(8,128)(2,1)S(1)}, u32[]{:S(2)}, u32[]{:S(2)}) collective-permute-start(bf16[128,256]{1,0:T(8,128)(2,1)} %get-tuple-element.23), channel_id=1, source_target_pairs={{0,8},{8,0},{16,24},{24,16},{1,9},{9,1},{17,25},{25,17},{2,10},{10... | collective-permute-start | bytes 196616 | tf_op jit(solution)/shard_map/ppermute | solution.py:29
  10.6 1.5 %collective-permute-start.4 = (bf16[128,256]{1,0:T(8,128)(2,1)S(1)}, bf16[128,256]{1,0:T(8,128)(2,1)S(1)}, u32[]{:S(2)}, u32[]{:S(2)}) collective-permute-start(bf16[128,256]{1,0:T(8,128)(2,1)S(1)} %get-tuple-element.48), channel_id=1, source_target_pairs={{0,16},{8,24},{16,0},{24,8},{1,17},{9,25},{17,1},{25,9},{2,18},{10... | collective-permute-start | bytes 196616 | tf_op jit(solution)/shard_map/ppermute | solution.py:29
  12.1 0.0 collective-permute-done.s1
  12.1 0.0 collective-permute-start.5
  12.2 0.3 %collective-permute-done.1.s2 = bf16[256,256]{1,0:T(8,128)(2,1)S(1)} collective-permute-done((bf16[256,256]{1,0:T(8,128)(2,1)S(1)}, bf16[256,256]{1,0:T(8,128)(2,1)S(1)}, u32[]{:S(2)}, u32[]{:S(2)}) %collective-permute-start.1) | collective-permute-done | bytes 131104 | tf_op jit(solution)/shard_map/ppermute | solution.py:29
  12.5 0.4 %collective-permute-done.2.s3 = bf16[256,256]{1,0:T(8,128)(2,1)S(1)} collective-permute-done((bf16[256,256]{1,0:T(8,128)(2,1)S(1)}, bf16[256,256]{1,0:T(8,128)(2,1)S(1)}, u32[]{:S(2)}, u32[]{:S(2)}) %collective-permute-start.2) | collective-permute-done | bytes 131104 | tf_op jit(solution)/shard_map/ppermute | solution.py:29
  12.9 0.0 copy-done
  12.9 0.0 copy-done.1
  12.9 1.1 %shard_map.96 = (f32[128,256]{1,0:T(8,128)S(1)}, bf16[128,256]{1,0:T(8,128)(2,1)S(1)}, bf16[128,256]{1,0:T(8,128)(2,1)S(1)}, bf16[128,256]{1,0:T(8,128)(2,1)S(1)}) custom-call(bf16[256,256]{1,0:T(8,128)(2,1)S(1)} %bitcast.23, bf16[256,256]{1,0:T(8,128)(2,1)S(1)} %collective-permute-done.s1, bf16[256,256]{1,0:T(8,128)(2,1)S(1)} %collective-permute-done.1.s2, ...), custom_call_target="tpu_custom_call" | custom-call | flops 1000 | bytes 1000 | tf_op jit(solution)/shard_map/pallas_call | solution.py:175
  14.0 1.4 %collective-permute-start.9 = (bf16[128,256]{1,0:T(8,128)(2,1)S(1)}, bf16[128,256]{1,0:T(8,128)(2,1)S(1)}, u32[]{:S(2)}, u32[]{:S(2)}) collective-permute-start(bf16[128,256]{1,0:T(8,128)(2,1)S(1)} %get-tuple-element.29), channel_id=1, source_target_pairs={{0,8},{8,0},{16,24},{24,16},{1,9},{9,1},{17,25},{25,17},{2,10},{10... | collective-permute-start | bytes 196616 | tf_op jit(solution)/shard_map/ppermute | solution.py:29
  15.4 1.4 %collective-permute-start.10 = (bf16[128,256]{1,0:T(8,128)(2,1)S(1)}, bf16[128,256]{1,0:T(8,128)(2,1)S(1)}, u32[]{:S(2)}, u32[]{:S(2)}) collective-permute-start(bf16[128,256]{1,0:T(8,128)(2,1)S(1)} %get-tuple-element.30), channel_id=1, source_target_pairs={{0,16},{8,24},{16,0},{24,8},{1,17},{9,25},{17,1},{25,9},{2,18},{10... | collective-permute-start | bytes 196616 | tf_op jit(solution)/shard_map/ppermute | solution.py:29
  16.8 0.0 collective-permute-done.3.f1
  16.8 1.3 %collective-permute-start.11 = (bf16[128,256]{1,0:T(8,128)(2,1)S(1)}, bf16[128,256]{1,0:T(8,128)(2,1)S(1)}, u32[]{:S(2)}, u32[]{:S(2)}) collective-permute-start(bf16[128,256]{1,0:T(8,128)(2,1)S(1)} %get-tuple-element.31), channel_id=1, source_target_pairs={{0,24},{8,16},{16,8},{24,0},{1,25},{9,17},{17,9},{25,1},{2,26},{10... | collective-permute-start | bytes 196616 | tf_op jit(solution)/shard_map/ppermute | solution.py:29
  18.1 0.0 collective-permute-done.4.f2
  18.1 0.0 collective-permute-done.5.f3
  18.1 0.0 copy-start.3
  18.1 1.1 %shard_map.95 = (bf16[128,256]{1,0:T(8,128)(2,1)S(1)}, f32[128,256]{1,0:T(8,128)S(1)}, f32[128,256]{1,0:T(8,128)S(1)}, f32[128,256]{1,0:T(8,128)S(1)}) custom-call(bf16[256,256]{1,0:T(8,128)(2,1)S(1)} %bitcast.24, bf16[256,256]{1,0:T(8,128)(2,1)S(1)} %collective-permute-done.s1, bf16[256,256]{1,0:T(8,128)(2,1)S(1)} %collective-permute-done.1.s2, ...), custom_call_target="tpu_custom_call" | custom-call | flops 1000 | bytes 1000 | tf_op jit(solution)/shard_map/pallas_call | solution.py:186
  19.2 0.9 %collective-permute-start.6 = (f32[128,256]{1,0:T(8,128)S(1)}, f32[128,256]{1,0:T(8,128)S(1)}, u32[]{:S(2)}, u32[]{:S(2)}) collective-permute-start(f32[128,256]{1,0:T(8,128)S(1)} %get-tuple-element.25.after), channel_id=1, source_target_pairs={{0,8},{8,0},{16,24},{24,16},{1,9},{9,1},{17,25},{25,17},{2,10},{10... | collective-permute-start | bytes 393224 | tf_op jit(solution)/shard_map/ppermute | solution.py:29
  20.1 1.4 %collective-permute-start.7 = (f32[128,256]{1,0:T(8,128)S(1)}, f32[128,256]{1,0:T(8,128)S(1)}, u32[]{:S(2)}, u32[]{:S(2)}) collective-permute-start(f32[128,256]{1,0:T(8,128)S(1)} %get-tuple-element.26), channel_id=1, source_target_pairs={{0,16},{8,24},{16,0},{24,8},{1,17},{9,25},{17,1},{25,9},{2,18},{10... | collective-permute-start | bytes 393224 | tf_op jit(solution)/shard_map/ppermute | solution.py:29
  21.5 0.0 collective-permute-done.9.w1
  21.5 1.3 %collective-permute-start.8 = (f32[128,256]{1,0:T(8,128)S(1)}, f32[128,256]{1,0:T(8,128)S(1)}, u32[]{:S(2)}, u32[]{:S(2)}) collective-permute-start(f32[128,256]{1,0:T(8,128)S(1)} %get-tuple-element.27), channel_id=1, source_target_pairs={{0,24},{8,16},{16,8},{24,0},{1,25},{9,17},{17,9},{25,1},{2,26},{10... | collective-permute-start | bytes 393224 | tf_op jit(solution)/shard_map/ppermute | solution.py:29
  22.8 0.0 collective-permute-done.10.w2
  22.8 0.0 collective-permute-done.11.w3
  22.8 0.0 copy-done.2
  22.8 0.0 copy-done.3
  22.8 0.3 shard_map.97
  23.1 0.1 collective-permute-start.12
  23.1 1.2 %collective-permute-done.12.other = bf16[64,256]{1,0:T(8,128)(2,1)S(1)} collective-permute-done((bf16[64,256]{1,0:T(8,128)(2,1)S(1)}, bf16[64,256]{1,0:T(8,128)(2,1)S(1)}, u32[]{:S(2)}, u32[]{:S(2)}) %collective-permute-start.12) | collective-permute-done | bytes 32800 | tf_op jit(solution)/shard_map/ppermute | solution.py:29
  24.3 3.3 %collective-permute-start.13 = (bf16[64,256]{1,0:T(8,128)(2,1)S(1)}, bf16[64,256]{1,0:T(8,128)(2,1)S(1)}, u32[]{:S(2)}, u32[]{:S(2)}) collective-permute-start(bf16[64,256]{1,0:T(8,128)(2,1)S(1)} %get-tuple-element.36), channel_id=1, source_target_pairs={{0,6},{1,3},{2,4},{3,1},{4,2},{5,7},{6,0},{7,5},{8,14},{9,11},{10,... | collective-permute-start | bytes 98312 | tf_op jit(solution)/shard_map/ppermute | solution.py:221
  27.6 0.7 %collective-permute-start.14 = (bf16[64,256]{1,0:T(8,128)(2,1)S(1)}, bf16[64,256]{1,0:T(8,128)(2,1)S(1)}, u32[]{:S(2)}, u32[]{:S(2)}) collective-permute-start(bf16[64,256]{1,0:T(8,128)(2,1)S(1)} %get-tuple-element.36), channel_id=1, source_target_pairs={{0,0},{1,5},{2,2},{3,7},{4,4},{5,1},{6,6},{7,3},{8,8},{9,13},{10,1... | collective-permute-start | bytes 98312 | tf_op jit(solution)/shard_map/ppermute | solution.py:222
  28.3 0.8 %shard_map.99 = (f32[4,128,256]{2,1,0:T(8,128)}, f32[8,128]{1,0:T(8,128)S(1)}) custom-call(f32[128,256]{1,0:T(8,128)S(1)} %get-tuple-element.28.w0, bf16[128,256]{1,0:T(8,128)(2,1)S(1)} %collective-permute-done.9.w1, bf16[128,256]{1,0:T(8,128)(2,1)S(1)} %collective-permute-done.10.w2, bf16[128,256]{1,0:T(8,128)(2,1)S(1)} %collective-permute-done.11.w3), custom_call_target="tpu_custom_call" | custom-call | flops 1000 | bytes 1000 | tf_op jit(solution)/shard_map/pallas_call | solution.py:205
  29.1 1.0 %collective-permute-done.13.first = bf16[64,256]{1,0:T(8,128)(2,1)S(1)} collective-permute-done((bf16[64,256]{1,0:T(8,128)(2,1)S(1)}, bf16[64,256]{1,0:T(8,128)(2,1)S(1)}, u32[]{:S(2)}, u32[]{:S(2)}) %collective-permute-start.13) | collective-permute-done | bytes 32800 | tf_op jit(solution)/shard_map/ppermute | solution.py:221
  30.1 0.0 collective-permute-done.14.second
  30.2 1.0 %collective-permute-start.15 = (bf16[64,256]{1,0:T(8,128)(2,1)S(1)}, bf16[64,256]{1,0:T(8,128)(2,1)S(1)}, u32[]{:S(2)}, u32[]{:S(2)}) collective-permute-start(bf16[64,256]{1,0:T(8,128)(2,1)S(1)} %get-tuple-element.39), channel_id=1, source_target_pairs={{0,1},{1,0},{2,3},{3,2},{4,5},{5,4},{6,7},{7,6},{8,9},{9,8},{10,11... | collective-permute-start | bytes 98312 | tf_op jit(solution)/shard_map/ppermute | solution.py:29
  31.1 0.0 collective-permute-done.6.v1
  31.1 0.0 collective-permute-done.7.v2
  31.1 0.0 collective-permute-done.8.v3
  31.1 0.8 %collective-permute-done.15.other = bf16[64,256]{1,0:T(8,128)(2,1)S(1)} collective-permute-done((bf16[64,256]{1,0:T(8,128)(2,1)S(1)}, bf16[64,256]{1,0:T(8,128)(2,1)S(1)}, u32[]{:S(2)}, u32[]{:S(2)}) %collective-permute-start.15) | collective-permute-done | bytes 32800 | tf_op jit(solution)/shard_map/ppermute | solution.py:29
  32.0 0.7 %shard_map.101 = (bf16[4,128,256]{2,1,0:T(8,128)(2,1)}, f32[64,256]{1,0:T(8,128)}) custom-call(bf16[128,256]{1,0:T(8,128)(2,1)S(1)} %get-tuple-element.24.v0, f32[128,256]{1,0:T(8,128)S(1)} %collective-permute-done.6.v1, f32[128,256]{1,0:T(8,128)S(1)} %collective-permute-done.7.v2, f32[128,256]{1,0:T(8,128)S(1)} %collective-permute-done.8.v3, ...), custom_call_target="tpu_custom_call" | custom-call | flops 1000 | bytes 1000 | tf_op jit(solution)/shard_map/pallas_call | solution.py:233
  (4 shorter events, 0.0 us)
Async XLA Ops:
  0.7 5.7 %copy-start.4 = (bf16[512,256]{1,0:T(8,128)(2,1)S(1)}, bf16[512,256]{1,0:T(8,128)(2,1)}, u32[]{:S(2)}) copy-start(bf16[512,256]{1,0:T(8,128)(2,1)} %param.9) | copy-start | bytes 786436
  1.8 10.3 %collective-permute-start = (bf16[256,256]{1,0:T(8,128)(2,1)S(1)}, bf16[256,256]{1,0:T(8,128)(2,1)S(1)}, u32[]{:S(2)}, u32[]{:S(2)}) collective-permute-start(bf16[256,256]{1,0:T(8,128)(2,1)S(1)} %bitcast.31), channel_id=1, source_target_pairs={{0,8},{8,0},{16,24},{24,16},{1,9},{9,1},{17,25},{25,17},{2,10},{10... | collective-permute-start | bytes 393224 | tf_op jit(solution)/shard_map/ppermute | solution.py:29
  4.8 7.7 %collective-permute-start.1 = (bf16[256,256]{1,0:T(8,128)(2,1)S(1)}, bf16[256,256]{1,0:T(8,128)(2,1)S(1)}, u32[]{:S(2)}, u32[]{:S(2)}) collective-permute-start(bf16[256,256]{1,0:T(8,128)(2,1)S(1)} %bitcast.30), channel_id=1, source_target_pairs={{0,16},{8,24},{16,0},{24,8},{1,17},{9,25},{17,1},{25,9},{2,18},{10... | collective-permute-start | bytes 393224 | tf_op jit(solution)/shard_map/ppermute | solution.py:29
  6.3 6.6 %collective-permute-start.2 = (bf16[256,256]{1,0:T(8,128)(2,1)S(1)}, bf16[256,256]{1,0:T(8,128)(2,1)S(1)}, u32[]{:S(2)}, u32[]{:S(2)}) collective-permute-start(bf16[256,256]{1,0:T(8,128)(2,1)S(1)} %bitcast.29), channel_id=1, source_target_pairs={{0,24},{8,16},{16,8},{24,0},{1,25},{9,17},{17,9},{25,1},{2,26},{10... | collective-permute-start | bytes 393224 | tf_op jit(solution)/shard_map/ppermute | solution.py:29
  6.4 6.5 %copy-start = (bf16[256,512]{1,0:T(8,128)(2,1)S(1)}, bf16[256,512]{1,0:T(8,128)(2,1)}, u32[]{:S(2)}) copy-start(bf16[256,512]{1,0:T(8,128)(2,1)} %constant.37.clone.table) | copy-start | bytes 786436
  6.4 6.5 %copy-start.1 = (bf16[512,256]{1,0:T(8,128)(2,1)S(1)}, bf16[512,256]{1,0:T(8,128)(2,1)}, u32[]{:S(2)}) copy-start(bf16[512,256]{1,0:T(8,128)(2,1)} %constant.38.clone.back) | copy-start | bytes 786436
  8.7 8.1 %collective-permute-start.3 = (bf16[128,256]{1,0:T(8,128)(2,1)}, bf16[128,256]{1,0:T(8,128)(2,1)S(1)}, u32[]{:S(2)}, u32[]{:S(2)}) collective-permute-start(bf16[128,256]{1,0:T(8,128)(2,1)} %get-tuple-element.23), channel_id=1, source_target_pairs={{0,8},{8,0},{16,24},{24,16},{1,9},{9,1},{17,25},{25,17},{2,10},{10... | collective-permute-start | bytes 196616 | tf_op jit(solution)/shard_map/ppermute | solution.py:29
  10.6 7.5 %collective-permute-start.4 = (bf16[128,256]{1,0:T(8,128)(2,1)S(1)}, bf16[128,256]{1,0:T(8,128)(2,1)S(1)}, u32[]{:S(2)}, u32[]{:S(2)}) collective-permute-start(bf16[128,256]{1,0:T(8,128)(2,1)S(1)} %get-tuple-element.48), channel_id=1, source_target_pairs={{0,16},{8,24},{16,0},{24,8},{1,17},{9,25},{17,1},{25,9},{2,18},{10... | collective-permute-start | bytes 196616 | tf_op jit(solution)/shard_map/ppermute | solution.py:29
  12.1 6.0 %collective-permute-start.5 = (bf16[128,256]{1,0:T(8,128)(2,1)S(1)}, bf16[128,256]{1,0:T(8,128)(2,1)S(1)}, u32[]{:S(2)}, u32[]{:S(2)}) collective-permute-start(bf16[128,256]{1,0:T(8,128)(2,1)S(1)} %get-tuple-element.47), channel_id=1, source_target_pairs={{0,24},{8,16},{16,8},{24,0},{1,25},{9,17},{17,9},{25,1},{2,26},{10... | collective-permute-start | bytes 196616 | tf_op jit(solution)/shard_map/ppermute | solution.py:29
  14.0 7.5 %collective-permute-start.9 = (bf16[128,256]{1,0:T(8,128)(2,1)S(1)}, bf16[128,256]{1,0:T(8,128)(2,1)S(1)}, u32[]{:S(2)}, u32[]{:S(2)}) collective-permute-start(bf16[128,256]{1,0:T(8,128)(2,1)S(1)} %get-tuple-element.29), channel_id=1, source_target_pairs={{0,8},{8,0},{16,24},{24,16},{1,9},{9,1},{17,25},{25,17},{2,10},{10... | collective-permute-start | bytes 196616 | tf_op jit(solution)/shard_map/ppermute | solution.py:29
  15.4 7.4 %collective-permute-start.10 = (bf16[128,256]{1,0:T(8,128)(2,1)S(1)}, bf16[128,256]{1,0:T(8,128)(2,1)S(1)}, u32[]{:S(2)}, u32[]{:S(2)}) collective-permute-start(bf16[128,256]{1,0:T(8,128)(2,1)S(1)} %get-tuple-element.30), channel_id=1, source_target_pairs={{0,16},{8,24},{16,0},{24,8},{1,17},{9,25},{17,1},{25,9},{2,18},{10... | collective-permute-start | bytes 196616 | tf_op jit(solution)/shard_map/ppermute | solution.py:29
  16.8 6.0 %collective-permute-start.11 = (bf16[128,256]{1,0:T(8,128)(2,1)S(1)}, bf16[128,256]{1,0:T(8,128)(2,1)S(1)}, u32[]{:S(2)}, u32[]{:S(2)}) collective-permute-start(bf16[128,256]{1,0:T(8,128)(2,1)S(1)} %get-tuple-element.31), channel_id=1, source_target_pairs={{0,24},{8,16},{16,8},{24,0},{1,25},{9,17},{17,9},{25,1},{2,26},{10... | collective-permute-start | bytes 196616 | tf_op jit(solution)/shard_map/ppermute | solution.py:29
  18.1 4.7 %copy-start.2 = (f32[4,128,256]{2,1,0:T(8,128)S(1)}, f32[4,128,256]{2,1,0:T(8,128)}, u32[]{:S(2)}) copy-start(f32[4,128,256]{2,1,0:T(8,128)} %get-tuple-element.32.decay) | copy-start | bytes 1572868
  18.1 4.7 %copy-start.3 = (bf16[512,64]{0,1:T(8,128)(2,1)S(1)}, bf16[512,64]{0,1:T(8,128)(2,1)}, u32[]{:S(2)}) copy-start(bf16[512,64]{0,1:T(8,128)(2,1)} %param.11) | copy-start | bytes 196612
  19.2 11.9 %collective-permute-start.6 = (f32[128,256]{1,0:T(8,128)S(1)}, f32[128,256]{1,0:T(8,128)S(1)}, u32[]{:S(2)}, u32[]{:S(2)}) collective-permute-start(f32[128,256]{1,0:T(8,128)S(1)} %get-tuple-element.25.after), channel_id=1, source_target_pairs={{0,8},{8,0},{16,24},{24,16},{1,9},{9,1},{17,25},{25,17},{2,10},{10... | collective-permute-start | bytes 393224 | tf_op jit(solution)/shard_map/ppermute | solution.py:29
  20.1 11.0 %collective-permute-start.7 = (f32[128,256]{1,0:T(8,128)S(1)}, f32[128,256]{1,0:T(8,128)S(1)}, u32[]{:S(2)}, u32[]{:S(2)}) collective-permute-start(f32[128,256]{1,0:T(8,128)S(1)} %get-tuple-element.26), channel_id=1, source_target_pairs={{0,16},{8,24},{16,0},{24,8},{1,17},{9,25},{17,1},{25,9},{2,18},{10... | collective-permute-start | bytes 393224 | tf_op jit(solution)/shard_map/ppermute | solution.py:29
  21.5 9.6 %collective-permute-start.8 = (f32[128,256]{1,0:T(8,128)S(1)}, f32[128,256]{1,0:T(8,128)S(1)}, u32[]{:S(2)}, u32[]{:S(2)}) collective-permute-start(f32[128,256]{1,0:T(8,128)S(1)} %get-tuple-element.27), channel_id=1, source_target_pairs={{0,24},{8,16},{16,8},{24,0},{1,25},{9,17},{17,9},{25,1},{2,26},{10... | collective-permute-start | bytes 393224 | tf_op jit(solution)/shard_map/ppermute | solution.py:29
  23.1 1.3 %collective-permute-start.12 = (bf16[64,256]{1,0:T(8,128)(2,1)S(1)}, bf16[64,256]{1,0:T(8,128)(2,1)S(1)}, u32[]{:S(2)}, u32[]{:S(2)}) collective-permute-start(bf16[64,256]{1,0:T(8,128)(2,1)S(1)} %get-tuple-element.34), channel_id=1, source_target_pairs={{0,1},{1,0},{2,3},{3,2},{4,5},{5,4},{6,7},{7,6},{8,9},{9,8},{10,11... | collective-permute-start | bytes 98312 | tf_op jit(solution)/shard_map/ppermute | solution.py:29
  24.3 5.8 %collective-permute-start.13 = (bf16[64,256]{1,0:T(8,128)(2,1)S(1)}, bf16[64,256]{1,0:T(8,128)(2,1)S(1)}, u32[]{:S(2)}, u32[]{:S(2)}) collective-permute-start(bf16[64,256]{1,0:T(8,128)(2,1)S(1)} %get-tuple-element.36), channel_id=1, source_target_pairs={{0,6},{1,3},{2,4},{3,1},{4,2},{5,7},{6,0},{7,5},{8,14},{9,11},{10,... | collective-permute-start | bytes 98312 | tf_op jit(solution)/shard_map/ppermute | solution.py:221
  27.6 2.5 %collective-permute-start.14 = (bf16[64,256]{1,0:T(8,128)(2,1)S(1)}, bf16[64,256]{1,0:T(8,128)(2,1)S(1)}, u32[]{:S(2)}, u32[]{:S(2)}) collective-permute-start(bf16[64,256]{1,0:T(8,128)(2,1)S(1)} %get-tuple-element.36), channel_id=1, source_target_pairs={{0,0},{1,5},{2,2},{3,7},{4,4},{5,1},{6,6},{7,3},{8,8},{9,13},{10,1... | collective-permute-start | bytes 98312 | tf_op jit(solution)/shard_map/ppermute | solution.py:222
  30.2 1.8 %collective-permute-start.15 = (bf16[64,256]{1,0:T(8,128)(2,1)S(1)}, bf16[64,256]{1,0:T(8,128)(2,1)S(1)}, u32[]{:S(2)}, u32[]{:S(2)}) collective-permute-start(bf16[64,256]{1,0:T(8,128)(2,1)S(1)} %get-tuple-element.39), channel_id=1, source_target_pairs={{0,1},{1,0},{2,3},{3,2},{4,5},{5,4},{6,7},{7,6},{8,9},{9,8},{10,11... | collective-permute-start | bytes 98312 | tf_op jit(solution)/shard_map/ppermute | solution.py:29
